TPU v7x, 128 devices: a whole 4x4x4 slice. The times are simulated.
128 devices in a mesh: pair: 8 (over z_hi, y), blk: 16 (over z_lo, x, core).
Axes of the slice: x: 4, y: 4, z: 4 (z_hi: 2, z_lo: 2; z = z_hi * 2 + z_lo), core: 2. Of those that a mesh axis runs over, the one named last changes fastest.
Arguments:
- source: bfloat16 [32768, 1024], P(('pair', 'blk'))
- source_label: int32 [32768], P(('pair', 'blk')), may hold values from 0 to 7, as said below
- target: bfloat16 [32768, 1024], P(('pair', 'blk'))
- target_label: int32 [32768], P(('pair', 'blk')), may hold values from 0 to 7, as said below
Outputs:
- src_partner: float32 [32768, 1024], P(('pair', 'blk'))
- src_margin: float32 [32768], P(('pair', 'blk'))
- tgt_margin: float32 [32768], P(('pair', 'blk'))
Inputs may be any that keep to these rules, and one draw needn't show every extreme that they name: `source_label`: rows (i * 16 + k) * 256 to (i * 16 + k + 1) * 256 - 1 form block (i, k). For every k below 8, blocks (i, k) and (i, k + 8) together name every bucket exactly 64 times, so a block names one bucket at most 64 times, and in every draw some block names one bucket 64 times. `target_label`: rows (i * 16 + k) * 256 to (i * 16 + k + 1) * 256 - 1 form block (i, k). For every k below 8, blocks (i, k) and (i, k + 8) together name every bucket exactly 64 times, so a block names one bucket at most 64 times, and in every draw some block names one bucket 64 times.
All inputs are finite; a program needn't handle non-finite values.
Results may differ from a plain program's by a relative error of at most 0.0041.
Values may be sent and summed in bfloat16 or wider, within the bound.
No kernel may reach another device: no remote copies, remote signals or barrier semaphores. Data moves between devices by JAX's collectives and lax.ppermute only.
A program may use at most 128 MiB of HBM per device.

v0:
```python
import jax
import jax.numpy as jnp
from jax import lax
from jax.sharding import PartitionSpec as P

sharpness = 12.0


def normalize(row_block):
    values = row_block.astype(jnp.float32)
    square = jnp.mean(values * values, axis=-1, keepdims=True)
    return (values * lax.rsqrt(square + 1e-06)).astype(jnp.bfloat16)


def place_rows(labels, buckets, capacity):
    onehot = (labels[:, None] == jnp.arange(buckets, dtype=jnp.int32)[None, :]).astype(jnp.int32)
    before = jnp.cumsum(onehot, axis=0) - onehot
    slot_rank = jnp.sum(before * onehot, axis=1)
    return (labels * capacity + slot_rank, jnp.sum(onehot, axis=0))


def pack_rows(normed, slot_of, slot_total):
    return jnp.zeros((slot_total, normed.shape[1]), normed.dtype).at[slot_of].set(normed)


def safe_ratio(numer, denom):
    return numer / jnp.where(denom > 0.0, denom, 1.0)


def block_rows(length):
    best_size = 1
    for option in range(1, min(length, 512) + 1):
        if length % option == 0:
            best_size = option
    return best_size


def on_device(source, source_label, target, target_label):
    width = source.shape[1]
    own_rows = source.shape[0]
    buckets = lax.axis_size("pair")
    columns = lax.axis_size("blk")
    capacity = 2 * own_rows // buckets
    slot_total = buckets * capacity
    src_norm = normalize(source)
    tgt_norm = normalize(target)
    src_slot, src_count = place_rows(source_label, buckets, capacity)
    tgt_slot, tgt_count = place_rows(target_label, buckets, capacity)
    src_pack = pack_rows(src_norm, src_slot, slot_total).reshape(buckets, capacity, width)
    tgt_pack = pack_rows(tgt_norm, tgt_slot, slot_total).reshape(buckets, capacity, width)
    src_recv, tgt_recv, src_heard, tgt_heard = (
        lax.all_to_all(src_pack, "pair", split_axis=0, concat_axis=0, tiled=True),
        lax.all_to_all(tgt_pack, "pair", split_axis=0, concat_axis=0, tiled=True),
        lax.all_to_all(src_count, "pair", split_axis=0, concat_axis=0, tiled=True),
        lax.all_to_all(tgt_count, "pair", split_axis=0, concat_axis=0, tiled=True),
    )
    src_slots = src_recv.reshape(slot_total, width)
    tgt_slots = tgt_recv.reshape(slot_total, width)
    cap_spots = jnp.arange(capacity, dtype=jnp.int32)
    src_live = (cap_spots[None, :] < src_heard[:, None]).reshape(slot_total)
    tgt_live = (cap_spots[None, :] < tgt_heard[:, None]).reshape(slot_total)
    stay_live = src_live.astype(jnp.float32)
    move_live = tgt_live.astype(jnp.bfloat16)
    block_count = src_slots.shape[0]
    total_rows = columns * block_count

    def tile_weight(rows_block, live_block):
        similar = (
            lax.dot_general(
                src_slots, rows_block, (((1,), (1,)), ((), ())), preferred_element_type=jnp.float32
            )
            / width
        )
        weight = jnp.exp(sharpness * similar) * (
            stay_live[:, None] * live_block.astype(jnp.float32)[None, :]
        )
        return (similar, weight)

    zeros_rows = jnp.zeros((block_count,), jnp.float32)
    zeros_every = jnp.zeros((total_rows,), jnp.float32)
    held_init = jnp.zeros((1, 1), jnp.float32)
    first_init = (
        jnp.zeros((block_count, width), jnp.float32),
        zeros_rows,
        zeros_rows,
        zeros_every,
        zeros_every,
        held_init,
    )
    first_row = jnp.int32(0)
    part_rows = lax.all_gather(tgt_slots, "blk", axis=0, tiled=True)
    part_live = lax.all_gather(move_live, "blk", axis=0, tiled=True)
    length = part_rows.shape[0]
    step_rows = block_rows(length)

    def first_inner_step(block_index, state):
        partner_acc, fwd_total, fwd_sum, bwd_total, bwd_sum, held_tiles = state
        offset = block_index * step_rows
        rows_block = lax.dynamic_slice_in_dim(part_rows, offset, step_rows, 0)
        live_block = lax.dynamic_slice_in_dim(part_live, offset, step_rows, 0)
        similar, weight = tile_weight(rows_block, live_block)
        weighted = weight * similar
        partner_acc = partner_acc + jnp.dot(
            weight.astype(jnp.bfloat16), rows_block, preferred_element_type=jnp.float32
        )
        fwd_total = fwd_total + jnp.sum(weight, axis=1)
        fwd_sum = fwd_sum + jnp.sum(weighted, axis=1)
        bwd_total = lax.dynamic_update_slice_in_dim(
            bwd_total, jnp.sum(weight, axis=0), first_row + offset, 0
        )
        bwd_sum = lax.dynamic_update_slice_in_dim(
            bwd_sum, jnp.sum(weighted, axis=0), first_row + offset, 0
        )
        return (partner_acc, fwd_total, fwd_sum, bwd_total, bwd_sum, held_tiles)

    partner_acc, fwd_total, fwd_sum, part_total, part_sum, held_tiles = lax.fori_loop(
        0, length // step_rows, first_inner_step, first_init
    )
    summed_total, summed_weighted = lax.psum((part_total, part_sum), "blk")
    bwd_every = safe_ratio(summed_weighted, summed_total)
    own_index = lax.axis_index("blk")
    own_total = lax.dynamic_slice_in_dim(summed_total, own_index * block_count, block_count, 0)
    own_bwd = lax.dynamic_slice_in_dim(bwd_every, own_index * block_count, block_count, 0)
    fwd_stat = safe_ratio(fwd_sum, fwd_total)
    second_first_row = jnp.int32(0)
    second_part_rows = lax.all_gather(tgt_slots, "blk", axis=0, tiled=True)
    second_part_live = lax.all_gather(move_live, "blk", axis=0, tiled=True)
    length = second_part_rows.shape[0]
    second_step_rows = block_rows(length)

    def second_inner_step(block_index, state):
        back_acc, fore_part = state
        offset = block_index * second_step_rows
        rows_block = lax.dynamic_slice_in_dim(second_part_rows, offset, second_step_rows, 0)
        live_block = lax.dynamic_slice_in_dim(second_part_live, offset, second_step_rows, 0)
        similar, weight = tile_weight(rows_block, live_block)
        bwd_block = lax.dynamic_slice_in_dim(
            bwd_every, second_first_row + offset, second_step_rows, 0
        )
        back_acc = back_acc + jnp.dot(weight, bwd_block, precision=lax.Precision.HIGHEST)
        fore_block = jnp.dot(fwd_stat, weight, precision=lax.Precision.HIGHEST)
        fore_part = lax.dynamic_update_slice_in_dim(
            fore_part, fore_block, second_first_row + offset, 0
        )
        return (back_acc, fore_part)

    back_acc, fore_part = lax.fori_loop(
        0, length // second_step_rows, second_inner_step, (zeros_rows, zeros_every)
    )
    fore_own = lax.psum_scatter(
        fore_part.reshape(columns, block_count), "blk", scatter_dimension=0, tiled=True
    )[0]
    partner = safe_ratio(partner_acc, fwd_total[:, None])
    src_margin = fwd_stat - 0.5 * (fwd_stat + safe_ratio(back_acc, fwd_total))
    tgt_margin = own_bwd - 0.5 * (own_bwd + safe_ratio(fore_own, own_total))
    back_partner, back_src, back_tgt = (
        lax.all_to_all(
            partner.reshape(buckets, capacity, width),
            "pair",
            split_axis=0,
            concat_axis=0,
            tiled=True,
        ),
        lax.all_to_all(
            src_margin.reshape(buckets, capacity), "pair", split_axis=0, concat_axis=0, tiled=True
        ),
        lax.all_to_all(
            tgt_margin.reshape(buckets, capacity), "pair", split_axis=0, concat_axis=0, tiled=True
        ),
    )
    partner_out = back_partner.reshape(slot_total, width)[src_slot]
    src_out = back_src.reshape(slot_total)[src_slot]
    tgt_out = back_tgt.reshape(slot_total)[tgt_slot]
    return (partner_out, src_out, tgt_out)


def solution(mesh):
    return jax.shard_map(
        on_device,
        mesh=mesh,
        in_specs=(
            P(("pair", "blk"), None),
            P(("pair", "blk")),
            P(("pair", "blk"), None),
            P(("pair", "blk")),
        ),
        out_specs=(P(("pair", "blk"), None), P(("pair", "blk")), P(("pair", "blk"))),
        check_vma=False,
    )
```

profile of v0, /device:TPU:0, one launch (start us, length us, event | category | flops | bytes accessed | tf_op | source)
XLA Modules:
  0.0 527.3 jit_solution(6003493025504286049)
XLA Ops:
  14.1 25.0 %all_to_all.51 = bf16[8,64,1024]{2,1,0:T(8,128)(2,1)} all-to-all(bf16[8,64,1024]{2,1,0:T(8,128)(2,1)S(1)} %bitcast.88), channel_id=1, replica_groups=mesh['pair'=8,'blk'=16] {'pair'}, dimensions={0} | all-to-all | bytes 2097152 | tf_op jit(solution)/shard_map/all_to_all | solution.py:53
  39.7 3.3 all-to-all-start.3
  44.3 2.7 scatter_custom_fusion.1
  47.0 3.6 all-to-all-done.3
  50.6 11.0 %all_to_all.52 = s32[8,1,1]{2,1,0:T(1,128)S(1)} all-to-all(s32[8,1,1]{2,1,0:T(1,128)S(1)} %copy.10), channel_id=1, replica_groups=mesh['pair'=8,'blk'=16] {'pair'}, dimensions={0} | all-to-all | bytes 64 | tf_op jit(solution)/shard_map/all_to_all | solution.py:54
  61.6 4.2 all-to-all-start.1
  66.9 19.5 %all-gather = bf16[16,1,512]{2,1,0:T(2,128)(2,1)S(1)} all-gather(bf16[1,1,512]{2,1,0:T(2,128)(2,1)S(1)} %reshape.176), channel_id=1, replica_groups=mesh['pair'=8,'blk'=16] {'blk'}, dimensions={0}, use_global_device_ids=true | all-gather | bytes 17408 | tf_op jit(solution)/shard_map/all_gather | solution.py:92
  86.8 53.0 %all-gather.3.cloned.1.call-done = bf16[8192,1024]{1,0:T(8,128)(2,1)} async-done(((bf16[512,1024]{1,0:T(8,128)(2,1)}), bf16[8192,1024]{1,0:T(8,128)(2,1)}) %all-gather.3.cloned.1.call-update) | async-done | bytes 16777232 | tf_op jit(solution)/shard_map/all_gather | solution.py:91
  139.8 91.3 %while.42 = (s32[]{:T(128)}, f32[512,1024]{1,0:T(8,128)S(1)}, f32[512]{0:T(512)S(1)}, f32[512]{0:T(512)S(1)}, f32[8192]{0:T(1024)S(1)}, /*index=5*/f32[8192]{0:T...) while((s32[]{:T(128)}, f32[512,1024]{1,0:T(8,128)S(1)}, ...), condition=%wide.region_17.18_spmd.clone, body=%wide.region_12.17_spmd.clone.sunk | while | flops 1078199808 | bytes 9483506 | solution.py:116
  145.7 2.6 fusion.76
  151.4 2.6 fusion.76
  157.1 2.6 fusion.76
  162.9 2.6 fusion.76
  168.6 2.6 fusion.76
  174.3 2.6 fusion.76
  231.8 106.3 %all-reduce.4.cloned.1.call-done = (f32[8192]{0:T(1024)}, f32[8192]{0:T(1024)}) async-done(((f32[8192]{0:T(1024)}, f32[8192]{0:T(1024)}), (f32[8192]{0:T(1024)}, f32[8192]{0:T(1024)})) %all-reduce.4.cloned.1.call-update) | async-done | bytes 65552 | tf_op jit(solution)/shard_map/psum | solution.py:119
  338.9 71.8 %while.43 = (s32[]{:T(128)}, f32[512]{0:T(512)S(1)}, f32[8192]{0:T(1024)S(1)}, bf16[8192,1024]{1,0:T(8,128)(2,1)}, bf16[512,1024]{1,0:T(8,128)(2,1)}, /*index=5*...) while((s32[]{:T(128)}, f32[512]{0:T(512)S(1)}, ...), condition=%wide.region_21.22_spmd.clone, body=%wide.region_20.21_spmd.clone.sunk | while | flops 543951360 | bytes 5278949 | solution.py:147
  410.7 53.7 %all-reduce = f32[16,512]{1,0:T(8,128)S(1)} all-reduce(f32[16,512]{1,0:T(8,128)S(1)} %reshape.127), channel_id=2, replica_groups=mesh['pair'=8,'blk'=16] {'blk'}, use_global_device_ids=true, to_apply=%region_22.23.clone | all-reduce | flops 8192 | bytes 65536
  466.5 6.8 %all-to-all-start.6 = ((f32[8,1,64]{2,1,0:T(1,128)}), f32[8,1,64]{2,1,0:T(1,128)S(1)}, u32[]{:S(2)}, u32[]{:S(2)}) async-start(f32[8,1,64]{2,1,0:T(1,128)} %all_to_all.42), calls=%async_computation.6 | async-start | bytes 8192 | tf_op jit(solution)/shard_map/all_to_all | solution.py:167
  473.9 7.0 %all-to-all-done.6 = f32[8,1,64]{2,1,0:T(1,128)S(1)} async-done(((f32[8,1,64]{2,1,0:T(1,128)}), f32[8,1,64]{2,1,0:T(1,128)S(1)}, u32[]{:S(2)}, u32[]{:S(2)}) %all-to-all-start.6) | async-done | bytes 2080 | tf_op jit(solution)/shard_map/all_to_all | solution.py:167
  480.9 3.3 all-to-all-start.5
  485.8 5.9 %all-to-all-done.5 = f32[8,1,64]{2,1,0:T(1,128)S(1)} async-done(((f32[8,1,64]{2,1,0:T(1,128)}), f32[8,1,64]{2,1,0:T(1,128)S(1)}, u32[]{:S(2)}, u32[]{:S(2)}) %all-to-all-start.5) | async-done | bytes 2080 | tf_op jit(solution)/shard_map/all_to_all | solution.py:164
  491.7 3.6 all-to-all-start.4
  502.4 16.1 %all-to-all-done.4 = f32[8,64,1024]{2,1,0:T(8,128)S(1)} async-done(((f32[8,64,1024]{2,1,0:T(8,128)}), f32[8,64,1024]{2,1,0:T(8,128)S(1)}, u32[]{:S(2)}, u32[]{:S(2)}) %all-to-all-start.4) | async-done | bytes 2097184 | tf_op jit(solution)/shard_map/all_to_all | solution.py:157
  (335 shorter events, 171.4 us)
Async XLA Ops:
  7.2 132.6 %all-gather.3.cloned.1.call-start = ((), (), s32[]{:S(2)}) async-start(), calls=%async_computation.7 | async-start | bytes 17825792 | tf_op jit(solution)/shard_map/all_gather | solution.py:91
  11.5 31.5 %copy-start.3 = (s32[256]{0:T(256)S(1)}, s32[256]{0:T(256)}, u32[]{:S(2)}) copy-start(s32[256]{0:T(256)} %param.9) | copy-start | bytes 3076
  11.5 32.6 %copy-start = (bf16[256,1024]{1,0:T(8,128)(2,1)S(1)}, bf16[256,1024]{1,0:T(8,128)(2,1)}, u32[]{:S(2)}) copy-start(bf16[256,1024]{1,0:T(8,128)(2,1)} %param.8) | copy-start | bytes 1572868
  39.7 10.8 %all-to-all-start.3 = ((s32[8,1,1]{2,1,0:T(1,128)}), s32[8,1,1]{2,1,0:T(1,128)S(1)}, u32[]{:S(2)}, u32[]{:S(2)}) async-start(s32[8,1,1]{2,1,0:T(1,128)} %copy.9), calls=%async_computation.3 | async-start | bytes 8192 | tf_op jit(solution)/shard_map/all_to_all | solution.py:55
  44.1 21.8 %copy-start.4 = (u32[128]{0:T(128)S(1)}, u32[128]{0:T(128)}, u32[]{:S(2)}) copy-start(u32[128]{0:T(128)} %constant.168) | copy-start | bytes 1540
  61.6 25.2 %all-to-all-start.1 = ((bf16[8,64,1024]{2,1,0:T(8,128)(2,1)}), bf16[8,64,1024]{2,1,0:T(8,128)(2,1)}, u32[]{:S(2)}, u32[]{:S(2)}) async-start(bf16[8,64,1024]{2,1,0:T(8,128)(2,1)} %bitcast.8), calls=%async_computation.1 | async-start | bytes 2097152 | tf_op jit(solution)/shard_map/all_to_all | solution.py:52
  65.8 272.3 %all-reduce.4.cloned.1.call-start = ((), (), s32[]{:S(2)}) async-start(), calls=%async_computation.8 | async-start | bytes 131072 | tf_op jit(solution)/shard_map/psum | solution.py:119
  231.1 0.6 copy-start.1
  231.1 0.6 copy-start.2
  466.5 14.4 %all-to-all-start.6 = ((f32[8,1,64]{2,1,0:T(1,128)}), f32[8,1,64]{2,1,0:T(1,128)S(1)}, u32[]{:S(2)}, u32[]{:S(2)}) async-start(f32[8,1,64]{2,1,0:T(1,128)} %all_to_all.42), calls=%async_computation.6 | async-start | bytes 8192 | tf_op jit(solution)/shard_map/all_to_all | solution.py:167
  480.9 10.8 %all-to-all-start.5 = ((f32[8,1,64]{2,1,0:T(1,128)}), f32[8,1,64]{2,1,0:T(1,128)S(1)}, u32[]{:S(2)}, u32[]{:S(2)}) async-start(f32[8,1,64]{2,1,0:T(1,128)} %all_to_all.40), calls=%async_computation.5 | async-start | bytes 8192 | tf_op jit(solution)/shard_map/all_to_all | solution.py:164
  491.7 26.7 %all-to-all-start.4 = ((f32[8,64,1024]{2,1,0:T(8,128)}), f32[8,64,1024]{2,1,0:T(8,128)S(1)}, u32[]{:S(2)}, u32[]{:S(2)}) async-start(f32[8,64,1024]{2,1,0:T(8,128)} %bitcast.86), calls=%async_computation.4 | async-start | bytes 4194304 | tf_op jit(solution)/shard_map/all_to_all | solution.py:157
Sparse Core Ops, SparseCore 0:
  39.2 100.5 all-gather.2
  231.9 106.1 all-reduce.3
where the time goes:
time: 532 us; the launch traced here: 527 us
  waiting for transfers between devices  192 us (36%)
  matrix products  142 us (27%)
  blocking collectives  109 us (20%)
  local copies, waits for them, and re-layouts  27.3 us (5%)
  starting transfers between devices  21.2 us (4%)
  other arithmetic  20.6 us (4%)
  between operations  14.3 us (3%)
    psum x1, waiting for transfers between devices, on_device(): summed_total, summed_weighted = lax.psum((part_total, part_sum), 'blk')  106 us
    dot_general x32, matrix products, tile_weight(): lax.dot_general(src_slots, rows_block, (((1,), (1,)), ((), ())), preferre...  79 us
    unnamed x1, blocking collectives  53.7 us
    all_gather x1, waiting for transfers between devices, on_device(): part_rows = lax.all_gather(tgt_slots, 'blk', axis=0, tiled=True)  53 us
    dot_general x16, matrix products, first_inner_step(): jnp.dot(weight.astype(jnp.bfloat16), rows_block, preferred_element_type=j...  36.7 us
    all_to_all x1, blocking collectives, on_device(): lax.all_to_all(tgt_pack, 'pair', split_axis=0, concat_axis=0, tiled=True)  25 us
    all_gather x1, blocking collectives, on_device(): part_live = lax.all_gather(move_live, 'blk', axis=0, tiled=True)  19.5 us
    all_to_all x1, waiting for transfers between devices, on_device(): lax.all_to_all(partner.reshape(buckets, capacity, width), 'pair', split_a...  16.1 us
  transfers between devices with their start and end apart: 7, of which 6 were waited for; matrix products, arithmetic and copies ran while one was open for 3% of the time, Pallas kernels for 0%

commit v1 on v0

v1 whole, which is shorter than its diff:
```python
from functools import partial

import jax
import jax.numpy as jnp
from jax import lax
from jax.experimental import pallas as pl
from jax.experimental.pallas import tpu as pltpu
from jax.sharding import Mesh, PartitionSpec as P

F32, BF16, I32 = jnp.float32, jnp.bfloat16, jnp.int32
SHARP = 12.0
WIDTH = 1024
ROWS = 256
SLOTS = 64
PACK = 512
EXTRA = 128
VMEM_LIMIT = 56 * 2**20
AXES = ("zh", "y", "zl", "x", "c")
ROUTE = ("zh", "y", "zl")
PLANE = ("zl", "x")
RIGHT = [(i, (i + 1) % 4) for i in range(4)]
LEFT = [(i, (i + 3) % 4) for i in range(4)]
SWAP = [(0, 1), (1, 0)]


def params():
    return pltpu.CompilerParams(vmem_limit_bytes=VMEM_LIMIT)


def vm():
    return pl.BlockSpec(memory_space=pltpu.VMEM)


def sm():
    return pl.BlockSpec(memory_space=pltpu.SMEM)


def hbm():
    return pl.BlockSpec(memory_space=pl.ANY)


def route_matrix(labels, half):
    mine = lax.broadcasted_iota(I32, (8, ROWS), 0) == labels
    upper = lax.broadcasted_iota(I32, (ROWS, ROWS), 0) < lax.broadcasted_iota(I32, (ROWS, ROWS), 1)
    before = jnp.dot(mine.astype(BF16), upper.astype(BF16), preferred_element_type=F32)
    rank = jnp.sum(jnp.where(mine, before, 0.0), axis=0, keepdims=True).astype(I32)
    slot = labels * SLOTS + jnp.where(half == 0, rank, SLOTS - 1 - rank)
    return (lax.broadcasted_iota(I32, (PACK, ROWS), 0) == slot).astype(BF16)


def pack_kernel(idx, labels, rows, out):
    values = rows[...].astype(F32)
    square = jnp.mean(values * values, axis=-1, keepdims=True)
    normed = (values * lax.rsqrt(square + 1e-06)).astype(BF16)
    out[...] = jnp.dot(route_matrix(labels[...], idx[0]), normed, preferred_element_type=F32).astype(BF16)


def pack(idx, labels, rows):
    return pl.pallas_call(
        pack_kernel,
        out_shape=jax.ShapeDtypeStruct((PACK, WIDTH), BF16),
        in_specs=[sm(), vm(), vm()],
        out_specs=vm(),
        compiler_params=params(),
        cost_estimate=pl.CostEstimate(flops=2 * PACK * ROWS * WIDTH, bytes_accessed=3 * 2**19, transcendentals=ROWS),
    )(idx, labels, rows)


def score_kernel(sib_first, own, sib, *refs):
    halves = refs[:16]
    weight, fwd, tot, wsum, partner = refs[16:21]
    targets, srcs, weight_bf, acc_t, acc_s, sems = refs[21:]
    for n, half in enumerate(halves):
        pltpu.make_async_copy(half, targets.at[n // 2, pl.ds(128 * (n % 2), 128)], sems.at[n // 2]).start()
    srcs[pl.ds(0, ROWS)] = own[...]
    srcs[pl.ds(ROWS, ROWS)] = sib[...]
    acc_t[...] = jnp.zeros_like(acc_t)
    acc_s[...] = jnp.zeros_like(acc_s)

    def block(n, carry):
        pltpu.make_async_copy(targets.at[n], targets.at[n], sems.at[n]).wait()
        cols_t, cols_s = jnp.zeros((1, ROWS), F32), jnp.zeros((1, ROWS), F32)
        for m in range(2):
            part = pl.ds(ROWS * m, ROWS)
            similar = lax.dot_general(
                srcs[part], targets[n], (((1,), (1,)), ((), ())), preferred_element_type=F32
            ) * (1.0 / WIDTH)
            w = jnp.exp(SHARP * similar)
            weighted = w * similar
            weight[n, part] = w
            weight_bf[n, part] = w.astype(BF16)
            acc_t[part] += w[:, :128] + w[:, 128:]
            acc_s[part] += weighted[:, :128] + weighted[:, 128:]
            cols_t += jnp.sum(w, axis=0, keepdims=True)
            cols_s += jnp.sum(weighted, axis=0, keepdims=True)
        tot[pl.ds(n, 1)] = cols_t
        wsum[pl.ds(n, 1)] = cols_s
        return carry

    lax.fori_loop(0, 8, block, 0)
    first = lax.broadcasted_iota(I32, (2 * ROWS, 128), 1) < 64
    fwd[...] = jnp.where(
        first, jnp.sum(acc_t[...], axis=1, keepdims=True), jnp.sum(acc_s[...], axis=1, keepdims=True)
    )
    for m in range(2):
        part = pl.ds(ROWS * m, ROWS)
        total = jnp.zeros((ROWS, WIDTH), F32)
        for n in range(8):
            total += jnp.dot(weight_bf[n, part], targets[n], preferred_element_type=F32)
        partner[part] = total


def score(idx, own, sib, halves):
    return pl.pallas_call(
        score_kernel,
        out_shape=(
            jax.ShapeDtypeStruct((8, 2 * ROWS, ROWS), F32),
            jax.ShapeDtypeStruct((2 * ROWS, 128), F32),
            jax.ShapeDtypeStruct((8, ROWS), F32),
            jax.ShapeDtypeStruct((8, ROWS), F32),
            jax.ShapeDtypeStruct((2 * ROWS, WIDTH), F32),
        ),
        in_specs=[sm(), vm(), vm()] + [hbm()] * 16,
        out_specs=(vm(),) * 5,
        scratch_shapes=[
            pltpu.VMEM((8, ROWS, WIDTH), BF16),
            pltpu.VMEM((2 * ROWS, WIDTH), BF16),
            pltpu.VMEM((8, 2 * ROWS, ROWS), BF16),
            pltpu.VMEM((2 * ROWS, 128), F32),
            pltpu.VMEM((2 * ROWS, 128), F32),
            pltpu.SemaphoreType.DMA((8,)),
        ],
        compiler_params=params(),
        cost_estimate=pl.CostEstimate(flops=2**33, bytes_accessed=12 * 2**20, transcendentals=2**20),
    )(idx, own, sib, *halves)


def fore_kernel(order, weight, mine, other, tot, wsum, payload):
    both = mine[...] + jnp.concatenate([other[ROWS:], other[:ROWS]], axis=0)
    stat = both[:, 64:65] / both[:, 0:1]
    for n in range(8):
        place = order[n]
        fore = jnp.sum(weight[n] * stat, axis=0, keepdims=True)
        payload[place, pl.ds(16, 1)] = fore
        t, s = tot[pl.ds(n, 1)], wsum[pl.ds(n, 1)]
        for d in range(8):
            payload[d, pl.ds(place, 1)] = t
            payload[d, pl.ds(8 + place, 1)] = s


def fore(order, weight, mine, other, tot, wsum):
    return pl.pallas_call(
        fore_kernel,
        out_shape=jax.ShapeDtypeStruct((8, 24, ROWS), F32),
        in_specs=[sm()] + [vm()] * 5,
        out_specs=vm(),
        compiler_params=params(),
        cost_estimate=pl.CostEstimate(flops=2**22, bytes_accessed=5 * 2**20, transcendentals=0),
    )(order, weight, mine, other, tot, wsum)


def back_kernel(order, weight, heard, back, target):
    sums = heard[0]
    for d in range(1, 8):
        sums = sums + heard[d]
    stat = sums[8:16] / sums[0:8]
    place = order[0]
    picked = lax.broadcasted_iota(I32, (8, ROWS), 0) == place
    own_total = jnp.sum(jnp.where(picked, sums[0:8], 0.0), axis=0, keepdims=True)
    own_stat = jnp.sum(jnp.where(picked, stat, 0.0), axis=0, keepdims=True)
    margin = own_stat - 0.5 * (own_stat + sums[16:17] / own_total)
    target[...] = jnp.transpose(jnp.broadcast_to(margin, (128, ROWS)))
    acc = jnp.zeros((2 * ROWS, 128), F32)
    for n in range(8):
        there = lax.broadcasted_iota(I32, (8, ROWS), 0) == order[n]
        row = jnp.sum(jnp.where(there, stat, 0.0), axis=0, keepdims=True)
        prod = weight[n] * row
        acc = acc + (prod[:, :128] + prod[:, 128:])
    back[...] = jnp.broadcast_to(jnp.sum(acc, axis=1, keepdims=True), (2 * ROWS, 128))


def back(order, weight, heard):
    return pl.pallas_call(
        back_kernel,
        out_shape=(jax.ShapeDtypeStruct((2 * ROWS, 128), F32), jax.ShapeDtypeStruct((ROWS, 128), F32)),
        in_specs=[sm(), vm(), vm()],
        out_specs=(vm(), vm()),
        compiler_params=params(),
        cost_estimate=pl.CostEstimate(flops=2**22, bytes_accessed=5 * 2**20, transcendentals=0),
    )(order, weight, heard)


def home_kernel(mine, other, partner, partner_in, back_ref, back_in, target, out):
    total = mine[...] + other[...]
    denom, stat = total[:, 0:1], total[:, 64:65] / total[:, 0:1]
    margin = stat - 0.5 * (stat + (back_ref[:, 0:1] + back_in[:, 0:1]) / denom)
    lane = lax.broadcasted_iota(I32, (ROWS, EXTRA), 1)
    value = jnp.where(lane < 2, margin, target[...])
    high = value.astype(BF16)
    low = (value - high.astype(F32)).astype(BF16)
    extra = jnp.where((lane & 1) == 0, high.astype(F32), low.astype(F32)).astype(BF16)
    rows = ((partner[...] + partner_in[...]) / denom).astype(BF16)
    for i in range(8):
        for z in range(2):
            place = pl.ds((2 * i + z) * 32, 32)
            out[place, pl.ds(0, WIDTH)] = rows[32 * i : 32 * i + 32]
            out[place, pl.ds(WIDTH, EXTRA)] = extra[32 * i : 32 * i + 32]


def home(mine, other, partner, partner_in, back_part, back_in, target):
    return pl.pallas_call(
        home_kernel,
        out_shape=jax.ShapeDtypeStruct((PACK, WIDTH + EXTRA), BF16),
        in_specs=[vm()] * 7,
        out_specs=vm(),
        compiler_params=params(),
        cost_estimate=pl.CostEstimate(flops=2**20, bytes_accessed=4 * 2**20, transcendentals=0),
    )(mine, other, partner, partner_in, back_part, back_in, target)


def finish_kernel(idx, src_labels, tgt_labels, got, partner, margins):
    src = route_matrix(src_labels[...], idx[0])
    tgt = route_matrix(tgt_labels[...], idx[0])
    contract = (((0,), (0,)), ((), ()))
    partner[...] = lax.dot_general(src, got[:, :WIDTH], contract, preferred_element_type=F32)
    extra = got[:, WIDTH:]
    by_src = lax.dot_general(extra, src, contract, preferred_element_type=F32)
    by_tgt = lax.dot_general(extra, tgt, contract, preferred_element_type=F32)
    margins[0:1] = by_src[0:1] + by_src[1:2]
    margins[1:2] = by_tgt[2:3] + by_tgt[3:4]


def finish(idx, src_labels, tgt_labels, got):
    return pl.pallas_call(
        finish_kernel,
        out_shape=(jax.ShapeDtypeStruct((ROWS, WIDTH), F32), jax.ShapeDtypeStruct((2, ROWS), F32)),
        in_specs=[sm(), vm(), vm(), vm()],
        out_specs=(vm(), vm()),
        compiler_params=params(),
        cost_estimate=pl.CostEstimate(flops=2 * PACK * ROWS * WIDTH, bytes_accessed=3 * 2**20, transcendentals=0),
    )(idx, src_labels, tgt_labels, got)


def route(packed):
    return lax.all_to_all(packed.reshape(16, 32, -1), ROUTE, 0, 0, tiled=True)


def merge(arrived):
    pairs = arrived.reshape(8, 2, 32, WIDTH)
    return (pairs[:, 0] + pairs[:, 1]).reshape(ROWS, WIDTH)


def gather_plane(rows):
    b0, b1 = rows[:128], rows[128:]
    p0, m1, z0 = lax.ppermute(b0, "x", RIGHT), lax.ppermute(b1, "x", LEFT), lax.ppermute(b0, "zl", SWAP)
    p1, m0, z1 = lax.ppermute(b1, "x", RIGHT), lax.ppermute(b0, "x", LEFT), lax.ppermute(b1, "zl", SWAP)
    x0, x1 = lax.ppermute(p0, "x", RIGHT), lax.ppermute(m1, "x", LEFT)
    zp0, zm0 = lax.ppermute(z0, "x", RIGHT), lax.ppermute(z0, "x", LEFT)
    zp1, zm1 = lax.ppermute(z1, "x", RIGHT), lax.ppermute(z1, "x", LEFT)
    zx0, zx1 = lax.ppermute(x0, "zl", SWAP), lax.ppermute(x1, "zl", SWAP)
    return [b0, b1, p0, p1, m0, m1, z0, z1, x0, x1, zp0, zp1, zm0, zm1, zx0, zx1]


def on_device(source, source_label, target, target_label):
    zl, x = lax.axis_index("zl"), lax.axis_index("x")
    idx = zl.reshape(1).astype(I32)
    src_labels, tgt_labels = source_label.reshape(1, ROWS), target_label.reshape(1, ROWS)
    places = [(0, 0), (0, 3), (0, 1), (1, 0), (0, 2), (1, 3), (1, 1), (1, 2)]
    order = jnp.stack([(zl + dz) % 2 * 4 + (x + dx) % 4 for dz, dx in places]).astype(I32)

    tgt_rows = merge(route(pack(idx, tgt_labels, target)))
    halves = gather_plane(tgt_rows)
    src_own = merge(route(pack(idx, src_labels, source)))
    src_sib = lax.ppermute(src_own, "c", SWAP)

    weight, fwd, tot, wsum, partner = score(idx, src_own, src_sib, halves)
    fwd_in = lax.ppermute(fwd, "c", SWAP)
    partner_in = lax.ppermute(partner[ROWS:], "c", SWAP)
    payload = fore(order, weight, fwd, fwd_in, tot, wsum)
    heard = lax.all_to_all(payload, PLANE, 0, 0, tiled=True)
    back_part, tgt_margin = back(order, weight, heard)
    back_in = lax.ppermute(back_part[ROWS:], "c", SWAP)
    packed = home(fwd[:ROWS], fwd_in[ROWS:], partner[:ROWS], partner_in, back_part[:ROWS], back_in, tgt_margin)
    got = route(packed).reshape(PACK, WIDTH + EXTRA)
    partner_out, margins = finish(idx, src_labels, tgt_labels, got)
    return (partner_out, margins[0], margins[1])


def solution(mesh):
    fine = Mesh(mesh.devices.reshape(2, 4, 2, 4, 2), AXES)
    return jax.shard_map(
        on_device,
        mesh=fine,
        in_specs=(P(AXES, None), P(AXES), P(AXES, None), P(AXES)),
        out_specs=(P(AXES, None), P(AXES), P(AXES)),
        check_vma=False,
    )
```

time: 532 us -> 156 us (0.29)
  waiting for transfers between devices: 192 us -> 42.2 us
  matrix products: 142 us -> 0 us
  blocking collectives: 109 us -> 36.6 us
  Pallas kernels: 0 us -> 30.5 us
  other arithmetic: 20.6 us -> 0.11 us
  local copies, waits for them, and re-layouts: 27.3 us -> 10.2 us
  starting transfers between devices: 21.2 us -> 34.6 us
  between operations: 14.3 us -> 0.92 us
    dot_general x80 -> x0, matrix products: 142 us -> none  [the longest x32 79 us: tile_weight(): lax.dot_general(src_slots, rows_block, (((1,), (1,)), ((), ())), preferre...]
    psum x1 -> x0, waiting for transfers between devices: 106 us -> none  [on_device(): summed_total, summed_weighted = lax.psum((part_total, part_sum), 'blk')]
    unnamed x1 -> x0, blocking collectives: 53.7 us -> none
    all_gather x1 -> x0, waiting for transfers between devices: 53 us -> none  [on_device(): part_rows = lax.all_gather(tgt_slots, 'blk', axis=0, tiled=True)]
    pallas_call x0 -> x7, Pallas kernels: none -> 30.5 us  [the longest x1 12.3 us: score(): pl.pallas_call(score_kernel, out_shape=(jax.ShapeDtypeStruct((8, 2 * ROWS...]
    ppermute x0 -> x18, starting transfers between devices: none -> 22.8 us  [the longest x2 5.18 us: gather_plane(): x0, x1 = (lax.ppermute(p0, 'x', RIGHT), lax.ppermute(m1, 'x', LEFT))]
    all_gather x1 -> x0, blocking collectives: 19.5 us -> none  [on_device(): part_live = lax.all_gather(move_live, 'blk', axis=0, tiled=True)]
    ppermute x0 -> x18, waiting for transfers between devices: none -> 15.7 us  [the longest x2 4.66 us: gather_plane(): zp1, zm1 = (lax.ppermute(z1, 'x', RIGHT), lax.ppermute(z1, 'x', LEFT))]
  transfers between devices with their start and end apart: 7 -> 20, of which waited for: 6 -> 12; matrix products, arithmetic and copies ran while one was open for 3% -> 2% of each run, Pallas kernels for 0% -> 6%
where the time goes in v1:
time: 156 us; the launch traced here: 155 us
  waiting for transfers between devices  42.2 us (27%)
  blocking collectives  36.6 us (23%)
  starting transfers between devices  34.6 us (22%)
  Pallas kernels  30.5 us (20%)
  local copies, waits for them, and re-layouts  10.2 us (7%)
    all_to_all x2, waiting for transfers between devices, route(): return lax.all_to_all(packed.reshape(16, 32, -1), ROUTE, 0, 0, tiled=True)  26.5 us
    all_to_all x1, blocking collectives, route(): return lax.all_to_all(packed.reshape(16, 32, -1), ROUTE, 0, 0, tiled=True)  25.4 us
    pallas_call x1, Pallas kernels, score(): pl.pallas_call(score_kernel, out_shape=(jax.ShapeDtypeStruct((8, 2 * ROWS...  12.3 us
    all_to_all x2, starting transfers between devices, route(): return lax.all_to_all(packed.reshape(16, 32, -1), ROUTE, 0, 0, tiled=True)  11.8 us
    all_to_all x1, blocking collectives, on_device(): heard = lax.all_to_all(payload, PLANE, 0, 0, tiled=True)  11.2 us
    pallas_call x2, Pallas kernels, pack(): pl.pallas_call(pack_kernel, out_shape=jax.ShapeDtypeStruct((PACK, WIDTH),...  5.36 us
    ppermute x2, starting transfers between devices, gather_plane(): x0, x1 = (lax.ppermute(p0, 'x', RIGHT), lax.ppermute(m1, 'x', LEFT))  5.18 us
    ppermute x2, waiting for transfers between devices, gather_plane(): zp1, zm1 = (lax.ppermute(z1, 'x', RIGHT), lax.ppermute(z1, 'x', LEFT))  4.66 us
  transfers between devices with their start and end apart: 20, of which 12 were waited for; matrix products, arithmetic and copies ran while one was open for 2% of the time, Pallas kernels for 6%

profile of v1, /device:TPU:0, one launch (start us, length us, event | category | flops | bytes accessed | tf_op | source)
XLA Modules:
  0.0 155.2 jit_solution(6413404921432060893)
XLA Ops:
  0.6 2.7 %shard_map.68 = bf16[512,1024]{1,0:T(8,128)(2,1)} custom-call(s32[1]{0:T(128)} %bitcast.idx.sib_first, s32[1,256]{1,0:T(1,128)} %bitcast.40, bf16[256,1024]{1,0:T(8,128)(2,1)} %rows.3), custom_call_target="tpu_custom_call" | custom-call | flops 268435456 | bytes 1572864 | tf_op jit(solution)/shard_map/pallas_call | solution.py:59
  3.3 8.1 %all-to-all-start.1 = ((bf16[16,32,1024]{2,1,0:T(8,128)(2,1)}), bf16[16,32,1024]{2,1,0:T(8,128)(2,1)S(1)}, u32[]{:S(2)}, u32[]{:S(2)}) async-start(bf16[16,32,1024]{2,1,0:T(8,128)(2,1)} %bitcast.27), calls=%async_computation.1 | async-start | bytes 2097152 | tf_op jit(solution)/shard_map/all_to_all | solution.py:245
  11.5 2.7 %shard_map.67 = bf16[512,1024]{1,0:T(8,128)(2,1)} custom-call(s32[1]{0:T(128)} %bitcast.idx.sib_first, s32[1,256]{1,0:T(1,128)} %bitcast.38, bf16[256,1024]{1,0:T(8,128)(2,1)} %rows.2), custom_call_target="tpu_custom_call" | custom-call | flops 268435456 | bytes 1572864 | tf_op jit(solution)/shard_map/pallas_call | solution.py:59
  14.1 15.1 %all-to-all-done.1 = bf16[16,32,1024]{2,1,0:T(8,128)(2,1)S(1)} async-done(((bf16[16,32,1024]{2,1,0:T(8,128)(2,1)}), bf16[16,32,1024]{2,1,0:T(8,128)(2,1)S(1)}, u32[]{:S(2)}, u32[]{:S(2)}) %all-to-all-start.1) | async-done | bytes 1048608 | tf_op jit(solution)/shard_map/all_to_all | solution.py:245
  29.3 3.7 %all-to-all-start = ((bf16[16,32,1024]{2,1,0:T(8,128)(2,1)}), bf16[16,32,1024]{2,1,0:T(8,128)(2,1)S(1)}, u32[]{:S(2)}, u32[]{:S(2)}) async-start(bf16[16,32,1024]{2,1,0:T(8,128)(2,1)} %bitcast.24), calls=%async_computation | async-start | bytes 2097152 | tf_op jit(solution)/shard_map/all_to_all | solution.py:245
  33.1 1.9 %collective-permute-start.5 = (bf16[128,1024]{1,0:T(8,128)(2,1)S(1)}, bf16[128,1024]{1,0:T(8,128)(2,1)S(1)}, u32[]{:S(2)}, u32[]{:S(2)}) collective-permute-start(bf16[128,1024]{1,0:T(8,128)(2,1)S(1)} %bitcast.34), channel_id=1, source_target_pairs={{0,8},{8,0},{1,9},{9,1},{2,10},{10,2},{3,11},{11,3},{4,12},{12,4},... | collective-permute-start | bytes 786440 | tf_op jit(solution)/shard_map/ppermute | solution.py:255
  35.0 2.8 %collective-permute-start.3 = (bf16[128,1024]{1,0:T(8,128)(2,1)S(1)}, bf16[128,1024]{1,0:T(8,128)(2,1)S(1)}, u32[]{:S(2)}, u32[]{:S(2)}) collective-permute-start(bf16[128,1024]{1,0:T(8,128)(2,1)S(1)} %bitcast.35), channel_id=1, source_target_pairs={{0,6},{2,0},{4,2},{6,4},{1,7},{3,1},{5,3},{7,5},{8,14},{10,8},{12,... | collective-permute-start | bytes 786440 | tf_op jit(solution)/shard_map/ppermute | solution.py:256
  37.7 11.3 %all-to-all-done = bf16[16,32,1024]{2,1,0:T(8,128)(2,1)S(1)} async-done(((bf16[16,32,1024]{2,1,0:T(8,128)(2,1)}), bf16[16,32,1024]{2,1,0:T(8,128)(2,1)S(1)}, u32[]{:S(2)}, u32[]{:S(2)}) %all-to-all-start) | async-done | bytes 1048608 | tf_op jit(solution)/shard_map/all_to_all | solution.py:245
  50.4 2.8 %collective-permute-start.4 = (bf16[128,1024]{1,0:T(8,128)(2,1)S(1)}, bf16[128,1024]{1,0:T(8,128)(2,1)S(1)}, u32[]{:S(2)}, u32[]{:S(2)}) collective-permute-start(bf16[128,1024]{1,0:T(8,128)(2,1)S(1)} %bitcast.31), channel_id=1, source_target_pairs={{0,6},{2,0},{4,2},{6,4},{1,7},{3,1},{5,3},{7,5},{8,14},{10,8},{12,... | collective-permute-start | bytes 786440 | tf_op jit(solution)/shard_map/ppermute | solution.py:255
  53.2 3.2 %collective-permute-start.11 = (bf16[128,1024]{1,0:T(8,128)(2,1)S(1)}, bf16[128,1024]{1,0:T(8,128)(2,1)S(1)}, u32[]{:S(2)}, u32[]{:S(2)}) collective-permute-start(bf16[128,1024]{1,0:T(8,128)(2,1)S(1)} %collective-permute-done.5.refs_6_), channel_id=1, source_target_pairs={{0,6},{2,0},{4,2},{6,4},{1,7},{3,1},{5,3},{7,5},{8,14},{10,8},{12,... | collective-permute-start | bytes 786440 | tf_op jit(solution)/shard_map/ppermute | solution.py:258
  60.0 3.7 %collective-permute-start.8 = (bf16[128,1024]{1,0:T(8,128)(2,1)S(1)}, bf16[128,1024]{1,0:T(8,128)(2,1)S(1)}, u32[]{:S(2)}, u32[]{:S(2)}) collective-permute-start(bf16[128,1024]{1,0:T(8,128)(2,1)S(1)} %collective-permute-done.4.refs_5_), channel_id=1, source_target_pairs={{0,6},{2,0},{4,2},{6,4},{1,7},{3,1},{5,3},{7,5},{8,14},{10,8},{12,... | collective-permute-start | bytes 786440 | tf_op jit(solution)/shard_map/ppermute | solution.py:257
  63.7 3.2 %collective-permute-start.12 = (bf16[128,1024]{1,0:T(8,128)(2,1)S(1)}, bf16[128,1024]{1,0:T(8,128)(2,1)S(1)}, u32[]{:S(2)}, u32[]{:S(2)}) collective-permute-start(bf16[128,1024]{1,0:T(8,128)(2,1)S(1)} %collective-permute-done.6.refs_7_), channel_id=1, source_target_pairs={{0,6},{2,0},{4,2},{6,4},{1,7},{3,1},{5,3},{7,5},{8,14},{10,8},{12,... | collective-permute-start | bytes 786440 | tf_op jit(solution)/shard_map/ppermute | solution.py:259
  72.0 2.1 %collective-permute-done.9.refs_10_ = bf16[128,1024]{1,0:T(8,128)(2,1)S(1)} collective-permute-done((bf16[128,1024]{1,0:T(8,128)(2,1)S(1)}, bf16[128,1024]{1,0:T(8,128)(2,1)S(1)}, u32[]{:S(2)}, u32[]{:S(2)}) %collective-permute-start.9) | collective-permute-done | bytes 262176 | tf_op jit(solution)/shard_map/ppermute | solution.py:258
  75.4 3.4 %collective-permute-done.10.refs_11_ = bf16[128,1024]{1,0:T(8,128)(2,1)S(1)} collective-permute-done((bf16[128,1024]{1,0:T(8,128)(2,1)S(1)}, bf16[128,1024]{1,0:T(8,128)(2,1)S(1)}, u32[]{:S(2)}, u32[]{:S(2)}) %collective-permute-start.10) | collective-permute-done | bytes 262176 | tf_op jit(solution)/shard_map/ppermute | solution.py:259
  78.8 1.9 %collective-permute-done.14.refs_15_ = bf16[128,1024]{1,0:T(8,128)(2,1)S(1)} collective-permute-done((bf16[128,1024]{1,0:T(8,128)(2,1)S(1)}, bf16[128,1024]{1,0:T(8,128)(2,1)S(1)}, u32[]{:S(2)}, u32[]{:S(2)}) %collective-permute-start.14) | collective-permute-done | bytes 262176 | tf_op jit(solution)/shard_map/ppermute | solution.py:260
  81.5 12.3 %shard_map.69 = (f32[8,512,256]{2,1,0:T(8,128)}, f32[512,128]{1,0:T(8,128)}, f32[8,256]{1,0:T(8,128)}, f32[8,256]{1,0:T(8,128)}, f32[512,1024]{1,0:T(8,128)}) custom-call(s32[1]{0:T(128)} %bitcast.idx.sib_first, bf16[256,1024]{1,0:T(8,128)(2,1)} %bitcast.29, bf16[256,1024]{1,0:T(8,128)(2,1)} %copy-done.9, bf16[128,1024]{1,0:T(8,128)(2,1)} %bitcast.37, ...), custom_call_target="tpu_custom_call" | custom-call | flops 8589934592 | bytes 12582912 | tf_op jit(solution)/shard_map/pallas_call | solution.py:114
  93.8 2.8 %fusion = (f32[256,1024]{1,0:T(8,128)S(1)}, f32[256,1024]{1,0:T(8,128)}) fusion(f32[512,1024]{1,0:T(8,128)} %get-tuple-element.13), kind=kLoop, calls=%fused_computation.2 | loop fusion | bytes 4194304 | tf_op jit(solution)/shard_map/slice | solution.py:278
  97.7 1.9 %collective-permute-done.15.other = f32[512,128]{1,0:T(8,128)S(1)} collective-permute-done((f32[512,128]{1,0:T(8,128)S(1)}, f32[512,128]{1,0:T(8,128)S(1)}, u32[]{:S(2)}, u32[]{:S(2)}) %collective-permute-start.15) | collective-permute-done | bytes 262176 | tf_op jit(solution)/shard_map/ppermute | solution.py:277
  100.4 3.5 %shard_map.70 = f32[8,24,256]{2,1,0:T(8,128)} custom-call(s32[8]{0:T(128)} %stack.35.order, f32[8,512,256]{2,1,0:T(8,128)} %get-tuple-element.14.weight, f32[512,128]{1,0:T(8,128)} %get-tuple-element.12.mine, f32[512,128]{1,0:T(8,128)} %copy-done.3, f32[8,256]{1,0:T(8,128)} %get-tuple-element.15.tot, f32[8,256]{1,0:T(8,128)} %get-tuple-element.16.wsum), custom_call_target="tpu_custom_call" | custom-call | flops 4194304 | bytes 5242880 | tf_op jit(solution)/shard_map/pallas_call | solution.py:152
  103.9 11.2 %all_to_all.20.heard = f32[8,24,256]{2,1,0:T(8,128)} all-to-all(f32[8,24,256]{2,1,0:T(8,128)} %shard_map.70), channel_id=1, replica_groups=mesh['zh'=2,'y'=4,'zl'=2,'x'=4,'c'=2] {'zl','x'}, dimensions={0} | all-to-all | bytes 393216 | tf_op jit(solution)/shard_map/all_to_all | solution.py:280
  115.1 3.3 %shard_map.71 = (f32[512,128]{1,0:T(8,128)}, f32[256,128]{1,0:T(8,128)}) custom-call(s32[8]{0:T(128)} %stack.35.order, f32[8,512,256]{2,1,0:T(8,128)} %get-tuple-element.14.weight, f32[8,24,256]{2,1,0:T(8,128)} %all_to_all.20.heard), custom_call_target="tpu_custom_call" | custom-call | flops 4194304 | bytes 5242880 | tf_op jit(solution)/shard_map/pallas_call | solution.py:183
  122.4 3.1 %shard_map.72 = bf16[512,1152]{1,0:T(8,128)(2,1)} custom-call(f32[256,128]{1,0:T(8,128)} %slice.58.mine, f32[256,128]{1,0:T(8,128)} %slice.72.other, f32[256,1024]{1,0:T(8,128)} %get-tuple-element.22.partner, f32[256,1024]{1,0:T(8,128)} %copy-done, f32[256,128]{1,0:T(8,128)} %get-tuple-element.26.back_ref, f32[256,128]{1,0:T(8,128)} %copy-done.8, ...), custom_call_target="tpu_custom_call" | custom-call | flops 1048576 | bytes 4194304 | tf_op jit(solution)/shard_map/pallas_call | solution.py:211
  125.5 25.4 %all_to_all.21 = bf16[16,32,1152]{2,1,0:T(8,128)(2,1)} all-to-all(bf16[16,32,1152]{2,1,0:T(8,128)(2,1)} %bitcast.23), channel_id=1, replica_groups=mesh['zh'=2,'y'=4,'zl'=2,'x'=4,'c'=2] {'zh','y','zl'}, dimensions={0} | all-to-all | bytes 2359296 | tf_op jit(solution)/shard_map/all_to_all | solution.py:245
  150.9 2.9 %shard_map.73 = (f32[256,1024]{1,0:T(8,128)}, f32[2,256]{1,0:T(2,128)}) custom-call(s32[1]{0:T(128)} %bitcast.idx.sib_first, s32[1,256]{1,0:T(1,128)} %bitcast.39, s32[1,256]{1,0:T(1,128)} %bitcast.41, bf16[512,1152]{1,0:T(8,128)(2,1)} %bitcast.22), custom_call_target="tpu_custom_call" | custom-call | flops 268435456 | bytes 3145728 | tf_op jit(solution)/shard_map/pallas_call | solution.py:234
  (82 shorter events, 19.2 us)
Async XLA Ops:
  3.3 26.0 %all-to-all-start.1 = ((bf16[16,32,1024]{2,1,0:T(8,128)(2,1)}), bf16[16,32,1024]{2,1,0:T(8,128)(2,1)S(1)}, u32[]{:S(2)}, u32[]{:S(2)}) async-start(bf16[16,32,1024]{2,1,0:T(8,128)(2,1)} %bitcast.27), calls=%async_computation.1 | async-start | bytes 2097152 | tf_op jit(solution)/shard_map/all_to_all | solution.py:245
  29.3 19.7 %all-to-all-start = ((bf16[16,32,1024]{2,1,0:T(8,128)(2,1)}), bf16[16,32,1024]{2,1,0:T(8,128)(2,1)S(1)}, u32[]{:S(2)}, u32[]{:S(2)}) async-start(bf16[16,32,1024]{2,1,0:T(8,128)(2,1)} %bitcast.24), calls=%async_computation | async-start | bytes 2097152 | tf_op jit(solution)/shard_map/all_to_all | solution.py:245
  33.1 47.6 %copy-start.6 = (bf16[4,1,32,1024]{3,2,1,0:T(8,128)(2,1)}, bf16[4,1,32,1024]{3,2,1,0:T(8,128)(2,1)S(1)}, u32[]{:S(2)}) copy-start(bf16[4,1,32,1024]{3,2,1,0:T(8,128)(2,1)S(1)} %get-tuple-element.23) | copy-start | bytes 786436
  33.1 47.6 %copy-start.7 = (bf16[4,1,32,1024]{3,2,1,0:T(8,128)(2,1)}, bf16[4,1,32,1024]{3,2,1,0:T(8,128)(2,1)S(1)}, u32[]{:S(2)}) copy-start(bf16[4,1,32,1024]{3,2,1,0:T(8,128)(2,1)S(1)} %get-tuple-element.24) | copy-start | bytes 786436
  33.1 17.4 %collective-permute-start.5 = (bf16[128,1024]{1,0:T(8,128)(2,1)S(1)}, bf16[128,1024]{1,0:T(8,128)(2,1)S(1)}, u32[]{:S(2)}, u32[]{:S(2)}) collective-permute-start(bf16[128,1024]{1,0:T(8,128)(2,1)S(1)} %bitcast.34), channel_id=1, source_target_pairs={{0,8},{8,0},{1,9},{9,1},{2,10},{10,2},{3,11},{11,3},{4,12},{12,4},... | collective-permute-start | bytes 786440 | tf_op jit(solution)/shard_map/ppermute | solution.py:255
  35.0 18.3 %collective-permute-start.3 = (bf16[128,1024]{1,0:T(8,128)(2,1)S(1)}, bf16[128,1024]{1,0:T(8,128)(2,1)S(1)}, u32[]{:S(2)}, u32[]{:S(2)}) collective-permute-start(bf16[128,1024]{1,0:T(8,128)(2,1)S(1)} %bitcast.35), channel_id=1, source_target_pairs={{0,6},{2,0},{4,2},{6,4},{1,7},{3,1},{5,3},{7,5},{8,14},{10,8},{12,... | collective-permute-start | bytes 786440 | tf_op jit(solution)/shard_map/ppermute | solution.py:256
  37.7 15.5 %collective-permute-start.1 = (bf16[128,1024]{1,0:T(8,128)(2,1)S(1)}, bf16[128,1024]{1,0:T(8,128)(2,1)S(1)}, u32[]{:S(2)}, u32[]{:S(2)}) collective-permute-start(bf16[128,1024]{1,0:T(8,128)(2,1)S(1)} %bitcast.36), channel_id=1, source_target_pairs={{0,2},{2,4},{4,6},{6,0},{1,3},{3,5},{5,7},{7,1},{8,10},{10,12},{12... | collective-permute-start | bytes 786440 | tf_op jit(solution)/shard_map/ppermute | solution.py:255
  49.1 31.6 %copy-start.5 = (bf16[8,1,32,1024]{3,2,1,0:T(8,128)(2,1)}, bf16[8,1,32,1024]{3,2,1,0:T(8,128)(2,1)S(1)}, u32[]{:S(2)}) copy-start(bf16[8,1,32,1024]{3,2,1,0:T(8,128)(2,1)S(1)} %slice_add_fusion.1) | copy-start | bytes 1572868
  49.1 14.6 %collective-permute-start = (bf16[256,1024]{1,0:T(8,128)(2,1)S(1)}, bf16[256,1024]{1,0:T(8,128)(2,1)S(1)}, u32[]{:S(2)}, u32[]{:S(2)}) collective-permute-start(bf16[256,1024]{1,0:T(8,128)(2,1)S(1)} %bitcast.28), channel_id=1, source_target_pairs={{0,1},{1,0},{2,3},{3,2},{4,5},{5,4},{6,7},{7,6},{8,9},{9,8},{10,11... | collective-permute-start | bytes 1572872 | tf_op jit(solution)/shard_map/ppermute | solution.py:274
  49.2 8.7 %collective-permute-start.6 = (bf16[128,1024]{1,0:T(8,128)(2,1)S(1)}, bf16[128,1024]{1,0:T(8,128)(2,1)S(1)}, u32[]{:S(2)}, u32[]{:S(2)}) collective-permute-start(bf16[128,1024]{1,0:T(8,128)(2,1)S(1)} %bitcast.30), channel_id=1, source_target_pairs={{0,8},{8,0},{1,9},{9,1},{2,10},{10,2},{3,11},{11,3},{4,12},{12,4},... | collective-permute-start | bytes 786440 | tf_op jit(solution)/shard_map/ppermute | solution.py:256
  50.4 30.3 %copy-start.10 = (bf16[128,1024]{1,0:T(8,128)(2,1)}, bf16[128,1024]{1,0:T(8,128)(2,1)S(1)}, u32[]{:S(2)}) copy-start(bf16[128,1024]{1,0:T(8,128)(2,1)S(1)} %collective-permute-done.5.refs_6_) | copy-start | bytes 786436
  50.4 9.5 %collective-permute-start.4 = (bf16[128,1024]{1,0:T(8,128)(2,1)S(1)}, bf16[128,1024]{1,0:T(8,128)(2,1)S(1)}, u32[]{:S(2)}, u32[]{:S(2)}) collective-permute-start(bf16[128,1024]{1,0:T(8,128)(2,1)S(1)} %bitcast.31), channel_id=1, source_target_pairs={{0,6},{2,0},{4,2},{6,4},{1,7},{3,1},{5,3},{7,5},{8,14},{10,8},{12,... | collective-permute-start | bytes 786440 | tf_op jit(solution)/shard_map/ppermute | solution.py:255
  53.2 10.4 %collective-permute-start.2 = (bf16[128,1024]{1,0:T(8,128)(2,1)S(1)}, bf16[128,1024]{1,0:T(8,128)(2,1)S(1)}, u32[]{:S(2)}, u32[]{:S(2)}) collective-permute-start(bf16[128,1024]{1,0:T(8,128)(2,1)S(1)} %bitcast.32), channel_id=1, source_target_pairs={{0,2},{2,4},{4,6},{6,0},{1,3},{3,5},{5,7},{7,1},{8,10},{10,12},{12... | collective-permute-start | bytes 786440 | tf_op jit(solution)/shard_map/ppermute | solution.py:256
  53.2 13.7 %collective-permute-start.11 = (bf16[128,1024]{1,0:T(8,128)(2,1)S(1)}, bf16[128,1024]{1,0:T(8,128)(2,1)S(1)}, u32[]{:S(2)}, u32[]{:S(2)}) collective-permute-start(bf16[128,1024]{1,0:T(8,128)(2,1)S(1)} %collective-permute-done.5.refs_6_), channel_id=1, source_target_pairs={{0,6},{2,0},{4,2},{6,4},{1,7},{3,1},{5,3},{7,5},{8,14},{10,8},{12,... | collective-permute-start | bytes 786440 | tf_op jit(solution)/shard_map/ppermute | solution.py:258
  57.9 10.4 %collective-permute-start.7 = (bf16[128,1024]{1,0:T(8,128)(2,1)S(1)}, bf16[128,1024]{1,0:T(8,128)(2,1)S(1)}, u32[]{:S(2)}, u32[]{:S(2)}) collective-permute-start(bf16[128,1024]{1,0:T(8,128)(2,1)S(1)} %collective-permute-done.1.refs_2_), channel_id=1, source_target_pairs={{0,2},{2,4},{4,6},{6,0},{1,3},{3,5},{5,7},{7,1},{8,10},{10,12},{12... | collective-permute-start | bytes 786440 | tf_op jit(solution)/shard_map/ppermute | solution.py:257
  60.0 11.2 %collective-permute-start.8 = (bf16[128,1024]{1,0:T(8,128)(2,1)S(1)}, bf16[128,1024]{1,0:T(8,128)(2,1)S(1)}, u32[]{:S(2)}, u32[]{:S(2)}) collective-permute-start(bf16[128,1024]{1,0:T(8,128)(2,1)S(1)} %collective-permute-done.4.refs_5_), channel_id=1, source_target_pairs={{0,6},{2,0},{4,2},{6,4},{1,7},{3,1},{5,3},{7,5},{8,14},{10,8},{12,... | collective-permute-start | bytes 786440 | tf_op jit(solution)/shard_map/ppermute | solution.py:257
  63.7 10.5 %collective-permute-start.9 = (bf16[128,1024]{1,0:T(8,128)(2,1)S(1)}, bf16[128,1024]{1,0:T(8,128)(2,1)S(1)}, u32[]{:S(2)}, u32[]{:S(2)}) collective-permute-start(bf16[128,1024]{1,0:T(8,128)(2,1)S(1)} %collective-permute-done.5.refs_6_), channel_id=1, source_target_pairs={{0,2},{2,4},{4,6},{6,0},{1,3},{3,5},{5,7},{7,1},{8,10},{10,12},{12... | collective-permute-start | bytes 786440 | tf_op jit(solution)/shard_map/ppermute | solution.py:258
  63.7 11.7 %collective-permute-start.12 = (bf16[128,1024]{1,0:T(8,128)(2,1)S(1)}, bf16[128,1024]{1,0:T(8,128)(2,1)S(1)}, u32[]{:S(2)}, u32[]{:S(2)}) collective-permute-start(bf16[128,1024]{1,0:T(8,128)(2,1)S(1)} %collective-permute-done.6.refs_7_), channel_id=1, source_target_pairs={{0,6},{2,0},{4,2},{6,4},{1,7},{3,1},{5,3},{7,5},{8,14},{10,8},{12,... | collective-permute-start | bytes 786440 | tf_op jit(solution)/shard_map/ppermute | solution.py:259
  66.9 11.9 %collective-permute-start.10 = (bf16[128,1024]{1,0:T(8,128)(2,1)S(1)}, bf16[128,1024]{1,0:T(8,128)(2,1)S(1)}, u32[]{:S(2)}, u32[]{:S(2)}) collective-permute-start(bf16[128,1024]{1,0:T(8,128)(2,1)S(1)} %collective-permute-done.6.refs_7_), channel_id=1, source_target_pairs={{0,2},{2,4},{4,6},{6,0},{1,3},{3,5},{5,7},{7,1},{8,10},{10,12},{12... | collective-permute-start | bytes 786440 | tf_op jit(solution)/shard_map/ppermute | solution.py:259
  68.4 10.4 %collective-permute-start.13 = (bf16[128,1024]{1,0:T(8,128)(2,1)S(1)}, bf16[128,1024]{1,0:T(8,128)(2,1)S(1)}, u32[]{:S(2)}, u32[]{:S(2)}) collective-permute-start(bf16[128,1024]{1,0:T(8,128)(2,1)S(1)} %collective-permute-done.7.refs_8_), channel_id=1, source_target_pairs={{0,8},{8,0},{1,9},{9,1},{2,10},{10,2},{3,11},{11,3},{4,12},{12,4},... | collective-permute-start | bytes 786440 | tf_op jit(solution)/shard_map/ppermute | solution.py:260
  71.2 9.5 %collective-permute-start.14 = (bf16[128,1024]{1,0:T(8,128)(2,1)S(1)}, bf16[128,1024]{1,0:T(8,128)(2,1)S(1)}, u32[]{:S(2)}, u32[]{:S(2)}) collective-permute-start(bf16[128,1024]{1,0:T(8,128)(2,1)S(1)} %collective-permute-done.8.refs_9_), channel_id=1, source_target_pairs={{0,8},{8,0},{1,9},{9,1},{2,10},{10,2},{3,11},{11,3},{4,12},{12,4},... | collective-permute-start | bytes 786440 | tf_op jit(solution)/shard_map/ppermute | solution.py:260
  96.6 24.8 %collective-permute-start.16 = (f32[256,1024]{1,0:T(8,128)S(1)}, f32[256,1024]{1,0:T(8,128)S(1)}, u32[]{:S(2)}, u32[]{:S(2)}) collective-permute-start(f32[256,1024]{1,0:T(8,128)S(1)} %get-tuple-element.21), channel_id=1, source_target_pairs={{0,1},{1,0},{2,3},{3,2},{4,5},{5,4},{6,7},{7,6},{8,9},{9,8},{10,11... | collective-permute-start | bytes 3145736 | tf_op jit(solution)/shard_map/ppermute | solution.py:278
  96.6 3.0 %collective-permute-start.15 = (f32[512,128]{1,0:T(8,128)S(1)}, f32[512,128]{1,0:T(8,128)S(1)}, u32[]{:S(2)}, u32[]{:S(2)}) collective-permute-start(f32[512,128]{1,0:T(8,128)S(1)} %copy-done.1), channel_id=1, source_target_pairs={{0,1},{1,0},{2,3},{3,2},{4,5},{5,4},{6,7},{7,6},{8,9},{9,8},{10,11... | collective-permute-start | bytes 786440 | tf_op jit(solution)/shard_map/ppermute | solution.py:277
  120.0 1.3 collective-permute-start.17
  (20 other events, 201.3 us)

commit v2 on v1

v2 whole, which is shorter than its diff:
```python
from functools import partial

import jax
import jax.numpy as jnp
from jax import lax
from jax.experimental import pallas as pl
from jax.experimental.pallas import tpu as pltpu
from jax.sharding import Mesh, PartitionSpec as P

F32, BF16, I32 = jnp.float32, jnp.bfloat16, jnp.int32
SHARP = 12.0
WIDTH = 1024
ROWS = 256
SLOTS = 64
PACK = 512
SCALE = SHARP * 1.4426950408889634 / WIDTH
VMEM_LIMIT = 20 * 2**20
AXES = ("zh", "y", "zl", "x", "c")
ROUTE = ("zh", "y", "zl")
PLANE = ("zl", "x")
RIGHT = [(i, (i + 1) % 4) for i in range(4)]
LEFT = [(i, (i + 3) % 4) for i in range(4)]
SWAP = [(0, 1), (1, 0)]
PLACES = [(0, 0), (0, 3), (0, 1), (1, 0), (0, 2), (1, 3), (1, 1), (1, 2)]
EXTRA = 128


def params():
    return pltpu.CompilerParams(vmem_limit_bytes=VMEM_LIMIT)


def vm():
    return pl.BlockSpec(memory_space=pltpu.VMEM)


def hbm():
    return pl.BlockSpec(memory_space=pl.ANY)


def slot_row(labels, half):
    mine = lax.broadcasted_iota(I32, (8, ROWS), 0) == labels
    upper = lax.broadcasted_iota(I32, (ROWS, ROWS), 0) < lax.broadcasted_iota(I32, (ROWS, ROWS), 1)
    before = jnp.dot(mine.astype(BF16), upper.astype(BF16), preferred_element_type=F32)
    rank = jnp.sum(jnp.where(mine, before, 0.0), axis=0, keepdims=True).astype(I32)
    return labels * SLOTS + jnp.where(half == 0, rank, SLOTS - 1 - rank)


def route_matrix(labels, half):
    return (lax.broadcasted_iota(I32, (PACK, ROWS), 0) == slot_row(labels, half)).astype(BF16)


def position(place):
    dz, dx = PLACES[place]
    return (lax.axis_index("zl") + dz) % 2 * 4 + (lax.axis_index("x") + dx) % 4


def pack_kernel(labels, rows, *refs):
    out = refs[-1]
    values = rows[...].astype(F32)
    square = jnp.mean(values * values, axis=-1, keepdims=True)
    normed = (values * lax.rsqrt(square + 1e-06)).astype(BF16)
    slots = route_matrix(labels[...], lax.axis_index("zl"))
    out[...] = jnp.dot(slots, normed, preferred_element_type=F32).astype(BF16)


def pack(labels, rows, *after):
    return pl.pallas_call(
        pack_kernel,
        out_shape=jax.ShapeDtypeStruct((PACK, WIDTH), BF16),
        in_specs=[vm()] * 2 + [hbm()] * len(after),
        out_specs=vm(),
        compiler_params=params(),
        cost_estimate=pl.CostEstimate(flops=2 * PACK * ROWS * WIDTH, bytes_accessed=3 * 2**19, transcendentals=ROWS),
    )(labels, rows, *after).reshape(16, 32, WIDTH)


def merge_kernel(arrived, *refs):
    out = refs[-1]
    for i in range(8):
        out[pl.ds(32 * i, 32)] = arrived[2 * i] + arrived[2 * i + 1]


def merge(arrived, *after):
    return pl.pallas_call(
        merge_kernel,
        out_shape=jax.ShapeDtypeStruct((ROWS, WIDTH), BF16),
        in_specs=[vm()] + [hbm()] * len(after),
        out_specs=vm(),
        compiler_params=params(),
        cost_estimate=pl.CostEstimate(flops=2**18, bytes_accessed=3 * 2**19, transcendentals=0),
    )(arrived, *after)


def regroup_kernel(picks, *refs):
    outs = refs[len(refs) - len(picks) :]
    for out, halves in zip(outs, picks):
        for n, (which, half) in enumerate(halves):
            out[pl.ds(128 * n, 128)] = refs[which][pl.ds(128 * half, 128)]


def regroup(arrays, picks):
    return pl.pallas_call(
        partial(regroup_kernel, picks),
        out_shape=tuple(jax.ShapeDtypeStruct((128 * len(halves), WIDTH), BF16) for halves in picks),
        in_specs=[vm()] * len(arrays),
        out_specs=(vm(),) * len(picks),
        compiler_params=params(),
        cost_estimate=pl.CostEstimate(flops=0, bytes_accessed=2**20, transcendentals=0),
    )(*arrays)


def tie_kernel(value, after, out):
    del value, after, out


def tie(value, after):
    return pl.pallas_call(
        tie_kernel,
        out_shape=jax.ShapeDtypeStruct(value.shape, value.dtype),
        in_specs=[hbm(), hbm()],
        out_specs=hbm(),
        input_output_aliases={0: 0},
        compiler_params=params(),
    )(value, after)


def score_kernel(pieces, count, carry, last, own, sib, *refs):
    arrays, refs = refs[:count], refs[count:]
    blocks = len(pieces) // 2
    halves = [arrays[which].at[pl.ds(128 * half, 128)] for which, half in pieces]
    if carry:
        (total_in, sum_in, own_in, sib_in), refs = refs[:4], refs[4:]
    weight, tot, wsum, partner_own, partner_sib, *fwd, weight_bf = refs
    for m, rows in enumerate((own, sib)):
        part = pl.ds(ROWS * m, ROWS)
        acc_t = total_in[part] if carry else jnp.zeros((ROWS, 128), F32)
        acc_s = sum_in[part] if carry else jnp.zeros((ROWS, 128), F32)
        for n in range(blocks):
            block = jnp.concatenate([halves[2 * n][...], halves[2 * n + 1][...]], axis=0)
            inner = lax.dot_general(rows[...], block, (((1,), (1,)), ((), ())), preferred_element_type=F32)
            w = jnp.exp2(SCALE * inner)
            weighted = w * inner
            weight[n, part] = w
            weight_bf[part, pl.ds(ROWS * n, ROWS)] = w.astype(BF16)
            acc_t = acc_t + (w[:, :128] + w[:, 128:])
            acc_s = acc_s + (weighted[:, :128] + weighted[:, 128:])
            cols_t = jnp.sum(w, axis=0, keepdims=True)
            cols_s = jnp.sum(weighted, axis=0, keepdims=True)
            tot[pl.ds(n, 1)] = cols_t if m == 0 else tot[pl.ds(n, 1)] + cols_t
            wsum[pl.ds(n, 1)] = cols_s if m == 0 else wsum[pl.ds(n, 1)] + cols_s
        if last:
            acc_t = jnp.sum(acc_t, axis=1, keepdims=True)
            acc_s = jnp.sum(acc_s, axis=1, keepdims=True) * (1.0 / WIDTH)
            fwd[0][part] = jnp.where(lax.broadcasted_iota(I32, (ROWS, 128), 1) < 64, acc_t, acc_s)
        else:
            fwd[0][part] = acc_t
            fwd[1][part] = acc_s
    for c in range(4):
        cols = pl.ds(256 * c, 256)
        block = jnp.concatenate([half[:, cols] for half in halves], axis=0)
        for m, out in enumerate((partner_own, partner_sib)):
            value = jnp.dot(weight_bf[pl.ds(ROWS * m, ROWS)], block, preferred_element_type=F32)
            if carry:
                value = value + (own_in, sib_in)[m][:, cols]
            out[:, cols] = value


def score(own, sib, arrays, pieces, carry, last):
    blocks = len(pieces) // 2
    row_sums = 1 if last else 2
    return pl.pallas_call(
        partial(score_kernel, pieces, len(arrays), bool(carry), last),
        out_shape=(
            jax.ShapeDtypeStruct((blocks, 2 * ROWS, ROWS), F32),
            jax.ShapeDtypeStruct((blocks, ROWS), F32),
            jax.ShapeDtypeStruct((blocks, ROWS), F32),
            jax.ShapeDtypeStruct((ROWS, WIDTH), F32),
            jax.ShapeDtypeStruct((ROWS, WIDTH), F32),
        )
        + (jax.ShapeDtypeStruct((2 * ROWS, 128), F32),) * row_sums,
        in_specs=[vm()] * (2 + len(arrays) + len(carry)),
        out_specs=(vm(),) * (5 + row_sums),
        scratch_shapes=[pltpu.VMEM((2 * ROWS, ROWS * blocks), BF16)],
        compiler_params=params(),
        cost_estimate=pl.CostEstimate(
            flops=blocks * 2**29, bytes_accessed=blocks * 2**20 + 2**22, transcendentals=blocks * 2**17
        ),
    )(own, sib, *arrays, *carry)


def fore_kernel(mine, other, *refs):
    out, refs = refs[-1], refs[:-1]
    both = mine[...] + jnp.concatenate([other[ROWS:], other[:ROWS]], axis=0)
    stat = both[:, 64:65] / both[:, 0:1]
    place = 0
    for weight, tot, wsum in zip(refs[0::3], refs[1::3], refs[2::3]):
        for n in range(weight.shape[0]):
            at = position(place)
            out[0, pl.ds(at, 1)] = tot[pl.ds(n, 1)]
            out[0, pl.ds(8 + at, 1)] = wsum[pl.ds(n, 1)] * (1.0 / WIDTH)
            out[0, pl.ds(16 + at, 1)] = jnp.sum(weight[n] * stat, axis=0, keepdims=True)
            place += 1
    for d in range(1, 8):
        out[d] = out[0]


def fore(mine, other, parts):
    flat = [a for part in parts for a in part]
    return pl.pallas_call(
        fore_kernel,
        out_shape=jax.ShapeDtypeStruct((8, 24, ROWS), F32),
        in_specs=[vm()] * (2 + len(flat)),
        out_specs=vm(),
        compiler_params=params(),
        cost_estimate=pl.CostEstimate(flops=2**22, bytes_accessed=5 * 2**20, transcendentals=0),
    )(mine, other, *flat)


def back_kernel(heard, *refs):
    weights, (back_own, back_sib, target) = refs[:-3], refs[-3:]
    sums = heard[0]
    for d in range(1, 8):
        sums = sums + heard[d]
    stat = sums[8:16] / sums[0:8]
    row_of = lax.broadcasted_iota(I32, (8, ROWS), 0)

    def pick(values, at):
        return jnp.sum(jnp.where(row_of == at, values, 0.0), axis=0, keepdims=True)

    own_stat = pick(stat, position(0))
    mean = pick(sums[16:24], position(0)) / pick(sums[0:8], position(0))
    margin = own_stat - 0.5 * (own_stat + mean)
    target[...] = jnp.transpose(jnp.broadcast_to(margin, (128, ROWS)))
    acc = jnp.zeros((2 * ROWS, 128), F32)
    place = 0
    for weight in weights:
        for n in range(weight.shape[0]):
            prod = weight[n] * pick(stat, position(place))
            acc = acc + (prod[:, :128] + prod[:, 128:])
            place += 1
    total = jnp.broadcast_to(jnp.sum(acc, axis=1, keepdims=True), (2 * ROWS, 128))
    back_own[...] = total[:ROWS]
    back_sib[...] = total[ROWS:]


def back(heard, weights):
    return pl.pallas_call(
        back_kernel,
        out_shape=(jax.ShapeDtypeStruct((ROWS, 128), F32),) * 3,
        in_specs=[vm()] * (1 + len(weights)),
        out_specs=(vm(),) * 3,
        compiler_params=params(),
        cost_estimate=pl.CostEstimate(flops=2**22, bytes_accessed=5 * 2**20, transcendentals=0),
    )(heard, *weights)


def home_kernel(mine, other, partner, partner_in, back_own, back_in, target, out):
    total = mine[:ROWS] + other[ROWS:]
    denom = total[:, 0:1]
    stat = total[:, 64:65] / denom
    margin = stat - 0.5 * (stat + (back_own[:, 0:1] + back_in[:, 0:1]) / denom)
    lane = lax.broadcasted_iota(I32, (ROWS, EXTRA), 1)
    value = jnp.where(lane < 2, margin, target[...])
    high = value.astype(BF16).astype(F32)
    extra = jnp.where((lane & 1) == 0, high, value - high).astype(BF16)
    rows = ((partner[...] + partner_in[...]) / denom).astype(BF16)
    for i in range(8):
        for z in range(2):
            place = pl.ds((2 * i + z) * 32, 32)
            out[place, pl.ds(0, WIDTH)] = rows[32 * i : 32 * i + 32]
            out[place, pl.ds(WIDTH, EXTRA)] = extra[32 * i : 32 * i + 32]


def home(mine, other, partner, partner_in, back_own, back_in, target):
    return pl.pallas_call(
        home_kernel,
        out_shape=jax.ShapeDtypeStruct((PACK, WIDTH + EXTRA), BF16),
        in_specs=[vm()] * 7,
        out_specs=vm(),
        compiler_params=params(),
        cost_estimate=pl.CostEstimate(flops=2**20, bytes_accessed=3 * 2**20, transcendentals=0),
    )(mine, other, partner, partner_in, back_own, back_in, target)


def slots_kernel(src_labels, tgt_labels, src, tgt):
    for labels, out in ((src_labels, src), (tgt_labels, tgt)):
        slots = route_matrix(labels[...], lax.axis_index("zl")).astype(F32)
        out[...] = jnp.transpose(slots).astype(BF16)


def slots(src_labels, tgt_labels):
    return pl.pallas_call(
        slots_kernel,
        out_shape=(jax.ShapeDtypeStruct((ROWS, PACK), BF16),) * 2,
        in_specs=[vm()] * 2,
        out_specs=(vm(),) * 2,
        compiler_params=params(),
        cost_estimate=pl.CostEstimate(flops=2**24, bytes_accessed=2**19, transcendentals=0),
    )(src_labels, tgt_labels)


def unpack_kernel(src, tgt, got, extra, partner, src_out, tgt_out):
    partner[...] = jnp.dot(src[...], got[...], preferred_element_type=F32)

    @pl.when(pl.program_id(0) == 0)
    def _():
        for slots, first, out in ((src, 0, src_out), (tgt, 2, tgt_out)):
            found = jnp.transpose(jnp.dot(slots[...], extra[...], preferred_element_type=F32))
            out[...] = found[first : first + 1] + found[first + 1 : first + 2]


def unpack(src_slots, tgt_slots, got):
    whole = pl.BlockSpec((ROWS, PACK), lambda g: (0, 0))
    row = pl.BlockSpec((1, ROWS), lambda g: (0, 0))
    return pl.pallas_call(
        unpack_kernel,
        out_shape=(
            jax.ShapeDtypeStruct((ROWS, WIDTH), F32),
            jax.ShapeDtypeStruct((1, ROWS), F32),
            jax.ShapeDtypeStruct((1, ROWS), F32),
        ),
        grid=(4,),
        in_specs=[
            whole,
            whole,
            pl.BlockSpec((PACK, 256), lambda g: (0, g)),
            pl.BlockSpec((PACK, EXTRA), lambda g: (0, WIDTH // EXTRA)),
        ],
        out_specs=(pl.BlockSpec((ROWS, 256), lambda g: (0, g)), row, row),
        compiler_params=params(),
        cost_estimate=pl.CostEstimate(flops=2 * PACK * ROWS * WIDTH, bytes_accessed=2**21, transcendentals=0),
    )(src_slots, tgt_slots, got, got)


def route(packed):
    return lax.all_to_all(packed, ROUTE, 0, 0, tiled=True)


def on_device(source, source_label, target, target_label):
    src_labels, tgt_labels = source_label.reshape(1, ROWS), target_label.reshape(1, ROWS)
    src_slots, tgt_slots = slots(src_labels, tgt_labels)

    base = merge(route(pack(tgt_labels, target)))
    left, right = lax.ppermute(base, "x", RIGHT), lax.ppermute(base, "x", LEFT)
    across = lax.ppermute(base, "zl", SWAP)
    go_right, go_left = regroup((left, right), (((0, 0),), ((1, 1),)))
    far_first, far_second = lax.ppermute(go_right, "x", RIGHT), lax.ppermute(go_left, "x", LEFT)
    across_left, across_right = lax.ppermute(across, "x", RIGHT), lax.ppermute(across, "x", LEFT)
    (far,) = regroup((far_first, far_second), (((0, 0), (1, 0)),))
    last = lax.ppermute(far, "zl", SWAP)

    src_own = merge(route(pack(src_labels, source, base)), far_first, far_second)
    src_sib = lax.ppermute(src_own, "c", SWAP)
    calls = (
        (
            (base, left, right, across, far),
            ((0, 0), (0, 1), (1, 0), (1, 1), (2, 0), (2, 1), (3, 0), (3, 1), (4, 0), (4, 1)),
        ),
        (
            (across_left, across_right, last),
            ((0, 0), (0, 1), (1, 0), (1, 1), (2, 0), (2, 1)),
        ),
    )
    parts, carry = [], ()
    for n, (arrays, pieces) in enumerate(calls):
        weight, tot, wsum, own, sib, *fwd = score(src_own, src_sib, arrays, pieces, carry, n == 1)
        parts.append((weight, tot, wsum))
        carry = (*fwd, own, sib)
    (fwd,) = fwd
    fwd_in = lax.ppermute(fwd, "c", SWAP)
    partner_in = lax.ppermute(tie(sib, fwd_in), "c", SWAP)
    heard = lax.all_to_all(fore(fwd, fwd_in, parts), PLANE, 0, 0, tiled=True)
    back_own, back_sib, tgt_margin = back(heard, [part[0] for part in parts])
    back_in = lax.ppermute(back_sib, "c", SWAP)
    packed = home(fwd, fwd_in, own, partner_in, back_own, back_in, tgt_margin)
    got = route(packed.reshape(16, 32, -1)).reshape(PACK, WIDTH + EXTRA)
    partner_out, src_margin, tgt_margin = unpack(src_slots, tgt_slots, got)
    return (partner_out, src_margin.reshape(ROWS), tgt_margin.reshape(ROWS))


def solution(mesh):
    fine = Mesh(mesh.devices.reshape(2, 4, 2, 4, 2), AXES)
    return jax.shard_map(
        on_device,
        mesh=fine,
        in_specs=(P(AXES, None), P(AXES), P(AXES, None), P(AXES)),
        out_specs=(P(AXES, None), P(AXES), P(AXES)),
        check_vma=False,
    )
```

time: 156 us -> 122 us (0.78)
  Pallas kernels: 30.5 us -> 14 us
  starting transfers between devices: 34.6 us -> 23.4 us
  local copies, waits for them, and re-layouts: 10.2 us -> 1.73 us
  waiting for transfers between devices: 42.2 us -> 45.4 us
    ppermute x16 -> x10, waiting for transfers between devices: 13.8 us -> 24.2 us  [the longest x1 8.46 us: on_device(): lax.ppermute(base, 'x', RIGHT)]
    ppermute x16 -> x10, starting transfers between devices: 22.3 us -> 12.2 us  [the longest x1 2.02 us: on_device(): lax.ppermute(across, 'x', LEFT)]
    pallas_call x3 -> x10, Pallas kernels: 18.5 us -> 9.8 us  [the longest x2 6.25 us: score(): pl.pallas_call(partial(score_kernel, pieces, len(arrays), bool(carry), la...]
    slice x6 -> x0, local copies, waits for them, and re-layouts: 7.1 us -> none  [the longest x1 2.8 us: on_device(): partner_in = lax.ppermute(partner[ROWS:], 'c', SWAP)]
    all_to_all x2, waiting for transfers between devices: 26.5 us -> 19.7 us  [route(): return lax.all_to_all(packed, ROUTE, 0, 0, tiled=True)]
    pallas_call x2, Pallas kernels: 5.36 us -> 2.25 us  [pack(): pl.pallas_call(pack_kernel, out_shape=jax.ShapeDtypeStruct((PACK, WIDTH),...]
    pallas_call x1, Pallas kernels: 3.52 us -> 0.51 us  [fore(): pl.pallas_call(fore_kernel, out_shape=jax.ShapeDtypeStruct((8, 24, ROWS),...]
    pallas_call x1, Pallas kernels: 3.1 us -> 1.4 us  [home(): pl.pallas_call(home_kernel, out_shape=jax.ShapeDtypeStruct((PACK, WIDTH +...]
  transfers between devices with their start and end apart: 20 -> 14, of which waited for: 12 -> 9; matrix products, arithmetic and copies ran while one was open for 2% -> 0% of each run, Pallas kernels for 6% -> 5%
where the time goes in v2:
time: 122 us; the launch traced here: 121 us
  waiting for transfers between devices  45.4 us (37%)
  blocking collectives  35.4 us (29%)
  starting transfers between devices  23.4 us (19%)
  Pallas kernels  14 us (11%)
  local copies, waits for them, and re-layouts  1.73 us (1%)
    all_to_all x1, blocking collectives, route(): return lax.all_to_all(packed, ROUTE, 0, 0, tiled=True)  25.2 us
    all_to_all x2, waiting for transfers between devices, route(): return lax.all_to_all(packed, ROUTE, 0, 0, tiled=True)  19.7 us
    all_to_all x2, starting transfers between devices, route(): return lax.all_to_all(packed, ROUTE, 0, 0, tiled=True)  11 us
    all_to_all x1, blocking collectives, on_device(): heard = lax.all_to_all(fore(fwd, fwd_in, parts), PLANE, 0, 0, tiled=True)  10.3 us
    ppermute x1, waiting for transfers between devices, on_device(): lax.ppermute(base, 'x', RIGHT)  8.46 us
    pallas_call x2, Pallas kernels, score(): pl.pallas_call(partial(score_kernel, pieces, len(arrays), bool(carry), la...  6.25 us
    ppermute x1, waiting for transfers between devices, on_device(): lax.ppermute(across, 'x', RIGHT)  6.03 us
    ppermute x1, waiting for transfers between devices, on_device(): lax.ppermute(go_right, 'x', RIGHT)  4.35 us
  transfers between devices with their start and end apart: 14, of which 9 were waited for; matrix products, arithmetic and copies ran while one was open for 0% of the time, Pallas kernels for 5%

profile of v2, /device:TPU:0, one launch (start us, length us, event | category | flops | bytes accessed | tf_op | source)
XLA Modules:
  0.0 120.7 jit_solution(12146167803395008764)
XLA Ops:
  3.0 25.2 %all_to_all.20.arrived = bf16[16,32,1024]{2,1,0:T(8,128)(2,1)S(1)} all-to-all(bf16[16,32,1024]{2,1,0:T(8,128)(2,1)S(1)} %bitcast.10), channel_id=1, replica_groups=mesh['zh'=2,'y'=4,'zl'=2,'x'=4,'c'=2] {'zh','y','zl'}, dimensions={0} | all-to-all | bytes 2097152 | tf_op jit(solution)/shard_map/all_to_all | solution.py:336
  28.3 1.6 %shard_map.70 = bf16[512,1024]{1,0:T(8,128)(2,1)} custom-call(s32[1,256]{1,0:T(1,128)S(1)} %bitcast.11, bf16[256,1024]{1,0:T(8,128)(2,1)S(1)} %copy-done.1, bf16[256,1024]{1,0:T(8,128)(2,1)S(1)} %shard_map.69.refs_0_), custom_call_target="tpu_custom_call" | custom-call | flops 268435456 | bytes 1572864 | tf_op jit(solution)/shard_map/pallas_call | solution.py:67
  29.9 3.7 %all-to-all-start.1 = ((bf16[16,32,1024]{2,1,0:T(8,128)(2,1)}), bf16[16,32,1024]{2,1,0:T(8,128)(2,1)S(1)}, u32[]{:S(2)}, u32[]{:S(2)}) async-start(bf16[16,32,1024]{2,1,0:T(8,128)(2,1)} %bitcast.3), calls=%async_computation.1 | async-start | bytes 2097152 | tf_op jit(solution)/shard_map/all_to_all | solution.py:336
  33.5 1.6 %collective-permute-start = (bf16[256,1024]{1,0:T(8,128)(2,1)S(1)}, bf16[256,1024]{1,0:T(8,128)(2,1)S(1)}, u32[]{:S(2)}, u32[]{:S(2)}) collective-permute-start(bf16[256,1024]{1,0:T(8,128)(2,1)S(1)} %shard_map.69.refs_0_), channel_id=1, source_target_pairs={{0,2},{2,4},{4,6},{6,0},{1,3},{3,5},{5,7},{7,1},{8,10},{10,12},{12... | collective-permute-start | bytes 1572872 | tf_op jit(solution)/shard_map/ppermute | solution.py:344
  35.1 1.7 %collective-permute-start.1 = (bf16[256,1024]{1,0:T(8,128)(2,1)S(1)}, bf16[256,1024]{1,0:T(8,128)(2,1)S(1)}, u32[]{:S(2)}, u32[]{:S(2)}) collective-permute-start(bf16[256,1024]{1,0:T(8,128)(2,1)S(1)} %shard_map.69.refs_0_), channel_id=1, source_target_pairs={{0,6},{2,0},{4,2},{6,4},{1,7},{3,1},{5,3},{7,5},{8,14},{10,8},{12,... | collective-permute-start | bytes 1572872 | tf_op jit(solution)/shard_map/ppermute | solution.py:344
  36.9 1.7 %collective-permute-start.5 = (bf16[256,1024]{1,0:T(8,128)(2,1)S(1)}, bf16[256,1024]{1,0:T(8,128)(2,1)}, u32[]{:S(2)}, u32[]{:S(2)}) collective-permute-start(bf16[256,1024]{1,0:T(8,128)(2,1)S(1)} %shard_map.69.refs_0_), channel_id=1, source_target_pairs={{0,8},{8,0},{1,9},{9,1},{2,10},{10,2},{3,11},{11,3},{4,12},{12,4},... | collective-permute-start | bytes 1572872 | tf_op jit(solution)/shard_map/ppermute | solution.py:345
  38.6 8.5 %collective-permute-done.refs_0_.refs_1_ = bf16[256,1024]{1,0:T(8,128)(2,1)S(1)} collective-permute-done((bf16[256,1024]{1,0:T(8,128)(2,1)S(1)}, bf16[256,1024]{1,0:T(8,128)(2,1)S(1)}, u32[]{:S(2)}, u32[]{:S(2)}) %collective-permute-start) | collective-permute-done | bytes 524320 | tf_op jit(solution)/shard_map/ppermute | solution.py:344
  47.1 1.6 %collective-permute-start.2 = (bf16[128,1024]{1,0:T(8,128)(2,1)S(1)}, bf16[128,1024]{1,0:T(8,128)(2,1)S(1)}, u32[]{:S(2)}, u32[]{:S(2)}) collective-permute-start(bf16[128,1024]{1,0:T(8,128)(2,1)S(1)} %get-tuple-element.28), channel_id=1, source_target_pairs={{0,2},{2,4},{4,6},{6,0},{1,3},{3,5},{5,7},{7,1},{8,10},{10,12},{12... | collective-permute-start | bytes 786440 | tf_op jit(solution)/shard_map/ppermute | solution.py:347
  48.6 1.8 %collective-permute-start.3 = (bf16[128,1024]{1,0:T(8,128)(2,1)S(1)}, bf16[128,1024]{1,0:T(8,128)(2,1)S(1)}, u32[]{:S(2)}, u32[]{:S(2)}) collective-permute-start(bf16[128,1024]{1,0:T(8,128)(2,1)S(1)} %get-tuple-element.29), channel_id=1, source_target_pairs={{0,6},{2,0},{4,2},{6,4},{1,7},{3,1},{5,3},{7,5},{8,14},{10,8},{12,... | collective-permute-start | bytes 786440 | tf_op jit(solution)/shard_map/ppermute | solution.py:347
  50.4 4.3 %collective-permute-done.2.refs_0_ = bf16[128,1024]{1,0:T(8,128)(2,1)S(1)} collective-permute-done((bf16[128,1024]{1,0:T(8,128)(2,1)S(1)}, bf16[128,1024]{1,0:T(8,128)(2,1)S(1)}, u32[]{:S(2)}, u32[]{:S(2)}) %collective-permute-start.2) | collective-permute-done | bytes 262176 | tf_op jit(solution)/shard_map/ppermute | solution.py:347
  55.2 2.3 %collective-permute-done.5.refs_3_ = bf16[256,1024]{1,0:T(8,128)(2,1)} collective-permute-done((bf16[256,1024]{1,0:T(8,128)(2,1)S(1)}, bf16[256,1024]{1,0:T(8,128)(2,1)}, u32[]{:S(2)}, u32[]{:S(2)}) %collective-permute-start.5) | collective-permute-done | bytes 524320 | tf_op jit(solution)/shard_map/ppermute | solution.py:345
  57.5 1.2 %collective-permute-start.6 = (bf16[256,1024]{1,0:T(8,128)(2,1)}, bf16[256,1024]{1,0:T(8,128)(2,1)S(1)}, u32[]{:S(2)}, u32[]{:S(2)}) collective-permute-start(bf16[256,1024]{1,0:T(8,128)(2,1)} %collective-permute-done.5.refs_3_), channel_id=1, source_target_pairs={{0,2},{2,4},{4,6},{6,0},{1,3},{3,5},{5,7},{7,1},{8,10},{10,12},{12... | collective-permute-start | bytes 1572872 | tf_op jit(solution)/shard_map/ppermute | solution.py:348
  58.7 2.0 %collective-permute-start.7 = (bf16[256,1024]{1,0:T(8,128)(2,1)}, bf16[256,1024]{1,0:T(8,128)(2,1)S(1)}, u32[]{:S(2)}, u32[]{:S(2)}) collective-permute-start(bf16[256,1024]{1,0:T(8,128)(2,1)} %collective-permute-done.5.refs_3_), channel_id=1, source_target_pairs={{0,6},{2,0},{4,2},{6,4},{1,7},{3,1},{5,3},{7,5},{8,14},{10,8},{12,... | collective-permute-start | bytes 1572872 | tf_op jit(solution)/shard_map/ppermute | solution.py:348
  61.2 4.2 %shard_map.74 = (f32[5,512,256]{2,1,0:T(8,128)S(1)}, f32[5,256]{1,0:T(8,128)S(1)}, f32[5,256]{1,0:T(8,128)S(1)}, f32[256,1024]{1,0:T(8,128)S(1)}, f32[256,1024]{...) custom-call(bf16[256,1024]{1,0:T(8,128)(2,1)S(1)} %shard_map.72.own, ...), custom_call_target="tpu_custom_call" | custom-call | flops 2684354560 | bytes 9437184 | tf_op jit(solution)/shard_map/pallas_call | solution.py:171
  65.5 6.0 %collective-permute-done.6.refs_0_ = bf16[256,1024]{1,0:T(8,128)(2,1)S(1)} collective-permute-done((bf16[256,1024]{1,0:T(8,128)(2,1)}, bf16[256,1024]{1,0:T(8,128)(2,1)S(1)}, u32[]{:S(2)}, u32[]{:S(2)}) %collective-permute-start.6) | collective-permute-done | bytes 524320 | tf_op jit(solution)/shard_map/ppermute | solution.py:348
  71.5 1.4 %collective-permute-done.8.refs_2_ = bf16[256,1024]{1,0:T(8,128)(2,1)S(1)} collective-permute-done((bf16[256,1024]{1,0:T(8,128)(2,1)S(1)}, bf16[256,1024]{1,0:T(8,128)(2,1)S(1)}, u32[]{:S(2)}, u32[]{:S(2)}) %collective-permute-start.8) | collective-permute-done | bytes 524320 | tf_op jit(solution)/shard_map/ppermute | solution.py:350
  72.9 2.0 %shard_map.75 = (f32[3,512,256]{2,1,0:T(8,128)S(1)}, f32[3,256]{1,0:T(4,128)S(1)}, f32[3,256]{1,0:T(4,128)S(1)}, f32[256,1024]{1,0:T(8,128)S(1)}, f32[256,1024]{1,0:T(8,128)S(1)}, /*index=5*/f32[512,128]{1,0:T(8,128)S(1)}) custom-call(bf16[256,1024]{1,0:T(8,128)(2,1)S(1)} %shard_map.72.own, bf16[256,1024]{1,0:T(8,128)(2,1)S(1)} %collective-permute-done.4.sib, ...), custom_call_target="tpu_custom_call" | custom-call | flops 1610612736 | bytes 7340032 | tf_op jit(solution)/shard_map/pallas_call | solution.py:171
  75.0 1.5 %collective-permute-done.9.after.other = f32[512,128]{1,0:T(8,128)S(1)} collective-permute-done((f32[512,128]{1,0:T(8,128)S(1)}, f32[512,128]{1,0:T(8,128)S(1)}, u32[]{:S(2)}, u32[]{:S(2)}) %collective-permute-start.9) | collective-permute-done | bytes 262176 | tf_op jit(solution)/shard_map/ppermute | solution.py:370
  77.2 10.3 %all_to_all.21.heard = f32[8,24,256]{2,1,0:T(8,128)S(1)} all-to-all(f32[8,24,256]{2,1,0:T(8,128)S(1)} %shard_map.77), channel_id=1, replica_groups=mesh['zh'=2,'y'=4,'zl'=2,'x'=4,'c'=2] {'zl','x'}, dimensions={0} | all-to-all | bytes 393216 | tf_op jit(solution)/shard_map/all_to_all | solution.py:372
  87.9 1.3 %collective-permute-done.11.back_in = f32[256,128]{1,0:T(8,128)S(1)} collective-permute-done((f32[256,128]{1,0:T(8,128)S(1)}, f32[256,128]{1,0:T(8,128)S(1)}, u32[]{:S(2)}, u32[]{:S(2)}) %collective-permute-start.11) | collective-permute-done | bytes 131104 | tf_op jit(solution)/shard_map/ppermute | solution.py:374
  89.3 1.4 %shard_map.79 = bf16[512,1152]{1,0:T(8,128)(2,1)} custom-call(f32[512,128]{1,0:T(8,128)S(1)} %get-tuple-element.34.mine, f32[512,128]{1,0:T(8,128)S(1)} %collective-permute-done.9.after.other, f32[256,1024]{1,0:T(8,128)S(1)} %get-tuple-element.35.partner, f32[256,1024]{1,0:T(8,128)S(1)} %collective-permute-done.10.partner_in, ...), custom_call_target="tpu_custom_call" | custom-call | flops 1048576 | bytes 3145728 | tf_op jit(solution)/shard_map/pallas_call | solution.py:275
  90.7 7.4 %all-to-all-start.3 = ((bf16[16,32,1152]{2,1,0:T(8,128)(2,1)}), bf16[16,32,1152]{2,1,0:T(8,128)(2,1)S(1)}, u32[]{:S(2)}, u32[]{:S(2)}) async-start(bf16[16,32,1152]{2,1,0:T(8,128)(2,1)} %bitcast.4), calls=%async_computation.3 | async-start | bytes 2359296 | tf_op jit(solution)/shard_map/all_to_all | solution.py:336
  98.4 19.7 %all-to-all-done.3 = bf16[16,32,1152]{2,1,0:T(8,128)(2,1)S(1)} async-done(((bf16[16,32,1152]{2,1,0:T(8,128)(2,1)}), bf16[16,32,1152]{2,1,0:T(8,128)(2,1)S(1)}, u32[]{:S(2)}, u32[]{:S(2)}) %all-to-all-start.3) | async-done | bytes 1179680 | tf_op jit(solution)/shard_map/all_to_all | solution.py:336
  118.2 2.6 %shard_map.80 = (f32[256,1024]{1,0:T(8,128)}, f32[1,256]{1,0:T(1,128)}, f32[1,256]{1,0:T(1,128)}) custom-call(bf16[256,512]{1,0:T(8,128)(2,1)S(1)} %get-tuple-element.26.src, bf16[256,512]{1,0:T(8,128)(2,1)S(1)} %get-tuple-element.27.tgt, bf16[512,1152]{1,0:T(8,128)(2,1)S(1)} %bitcast.8, bf16[512,1152]{1,0:T(8,128)(2,1)S(1)} %bitcast.9), custom_call_target="tpu_custom_call" | custom-call | flops 268435456 | bytes 2097152 | tf_op jit(solution)/shard_map/pallas_call | solution.py:315
  (30 shorter events, 4.9 us)
Async XLA Ops:
  0.6 1.0 copy-start
  1.7 0.7 copy-start.3
  3.0 25.3 %copy-start.1 = (bf16[256,1024]{1,0:T(8,128)(2,1)S(1)}, bf16[256,1024]{1,0:T(8,128)(2,1)}, u32[]{:S(2)}) copy-start(bf16[256,1024]{1,0:T(8,128)(2,1)} %rows.3) | copy-start | bytes 1572868
  3.0 25.3 %copy-start.2 = (s32[256]{0:T(256)S(1)}, s32[256]{0:T(256)}, u32[]{:S(2)}) copy-start(s32[256]{0:T(256)} %param.5) | copy-start | bytes 3076
  29.9 25.1 %all-to-all-start.1 = ((bf16[16,32,1024]{2,1,0:T(8,128)(2,1)}), bf16[16,32,1024]{2,1,0:T(8,128)(2,1)S(1)}, u32[]{:S(2)}, u32[]{:S(2)}) async-start(bf16[16,32,1024]{2,1,0:T(8,128)(2,1)} %bitcast.3), calls=%async_computation.1 | async-start | bytes 2097152 | tf_op jit(solution)/shard_map/all_to_all | solution.py:336
  33.5 13.5 %collective-permute-start = (bf16[256,1024]{1,0:T(8,128)(2,1)S(1)}, bf16[256,1024]{1,0:T(8,128)(2,1)S(1)}, u32[]{:S(2)}, u32[]{:S(2)}) collective-permute-start(bf16[256,1024]{1,0:T(8,128)(2,1)S(1)} %shard_map.69.refs_0_), channel_id=1, source_target_pairs={{0,2},{2,4},{4,6},{6,0},{1,3},{3,5},{5,7},{7,1},{8,10},{10,12},{12... | collective-permute-start | bytes 1572872 | tf_op jit(solution)/shard_map/ppermute | solution.py:344
  35.1 11.9 %collective-permute-start.1 = (bf16[256,1024]{1,0:T(8,128)(2,1)S(1)}, bf16[256,1024]{1,0:T(8,128)(2,1)S(1)}, u32[]{:S(2)}, u32[]{:S(2)}) collective-permute-start(bf16[256,1024]{1,0:T(8,128)(2,1)S(1)} %shard_map.69.refs_0_), channel_id=1, source_target_pairs={{0,6},{2,0},{4,2},{6,4},{1,7},{3,1},{5,3},{7,5},{8,14},{10,8},{12,... | collective-permute-start | bytes 1572872 | tf_op jit(solution)/shard_map/ppermute | solution.py:344
  36.9 20.7 %collective-permute-start.5 = (bf16[256,1024]{1,0:T(8,128)(2,1)S(1)}, bf16[256,1024]{1,0:T(8,128)(2,1)}, u32[]{:S(2)}, u32[]{:S(2)}) collective-permute-start(bf16[256,1024]{1,0:T(8,128)(2,1)S(1)} %shard_map.69.refs_0_), channel_id=1, source_target_pairs={{0,8},{8,0},{1,9},{9,1},{2,10},{10,2},{3,11},{11,3},{4,12},{12,4},... | collective-permute-start | bytes 1572872 | tf_op jit(solution)/shard_map/ppermute | solution.py:345
  47.1 7.7 %collective-permute-start.2 = (bf16[128,1024]{1,0:T(8,128)(2,1)S(1)}, bf16[128,1024]{1,0:T(8,128)(2,1)S(1)}, u32[]{:S(2)}, u32[]{:S(2)}) collective-permute-start(bf16[128,1024]{1,0:T(8,128)(2,1)S(1)} %get-tuple-element.28), channel_id=1, source_target_pairs={{0,2},{2,4},{4,6},{6,0},{1,3},{3,5},{5,7},{7,1},{8,10},{10,12},{12... | collective-permute-start | bytes 786440 | tf_op jit(solution)/shard_map/ppermute | solution.py:347
  48.6 6.4 %collective-permute-start.3 = (bf16[128,1024]{1,0:T(8,128)(2,1)S(1)}, bf16[128,1024]{1,0:T(8,128)(2,1)S(1)}, u32[]{:S(2)}, u32[]{:S(2)}) collective-permute-start(bf16[128,1024]{1,0:T(8,128)(2,1)S(1)} %get-tuple-element.29), channel_id=1, source_target_pairs={{0,6},{2,0},{4,2},{6,4},{1,7},{3,1},{5,3},{7,5},{8,14},{10,8},{12,... | collective-permute-start | bytes 786440 | tf_op jit(solution)/shard_map/ppermute | solution.py:347
  55.1 6.1 %collective-permute-start.4 = (bf16[256,1024]{1,0:T(8,128)(2,1)S(1)}, bf16[256,1024]{1,0:T(8,128)(2,1)S(1)}, u32[]{:S(2)}, u32[]{:S(2)}) collective-permute-start(bf16[256,1024]{1,0:T(8,128)(2,1)S(1)} %shard_map.72.own), channel_id=1, source_target_pairs={{0,1},{1,0},{2,3},{3,2},{4,5},{5,4},{6,7},{7,6},{8,9},{9,8},{10,11... | collective-permute-start | bytes 1572872 | tf_op jit(solution)/shard_map/ppermute | solution.py:353
  57.5 14.0 %collective-permute-start.6 = (bf16[256,1024]{1,0:T(8,128)(2,1)}, bf16[256,1024]{1,0:T(8,128)(2,1)S(1)}, u32[]{:S(2)}, u32[]{:S(2)}) collective-permute-start(bf16[256,1024]{1,0:T(8,128)(2,1)} %collective-permute-done.5.refs_3_), channel_id=1, source_target_pairs={{0,2},{2,4},{4,6},{6,0},{1,3},{3,5},{5,7},{7,1},{8,10},{10,12},{12... | collective-permute-start | bytes 1572872 | tf_op jit(solution)/shard_map/ppermute | solution.py:348
  58.7 12.8 %collective-permute-start.7 = (bf16[256,1024]{1,0:T(8,128)(2,1)}, bf16[256,1024]{1,0:T(8,128)(2,1)S(1)}, u32[]{:S(2)}, u32[]{:S(2)}) collective-permute-start(bf16[256,1024]{1,0:T(8,128)(2,1)} %collective-permute-done.5.refs_3_), channel_id=1, source_target_pairs={{0,6},{2,0},{4,2},{6,4},{1,7},{3,1},{5,3},{7,5},{8,14},{10,8},{12,... | collective-permute-start | bytes 1572872 | tf_op jit(solution)/shard_map/ppermute | solution.py:348
  60.8 12.1 %collective-permute-start.8 = (bf16[256,1024]{1,0:T(8,128)(2,1)S(1)}, bf16[256,1024]{1,0:T(8,128)(2,1)S(1)}, u32[]{:S(2)}, u32[]{:S(2)}) collective-permute-start(bf16[256,1024]{1,0:T(8,128)(2,1)S(1)} %shard_map.73.refs_4_), channel_id=1, source_target_pairs={{0,8},{8,0},{1,9},{9,1},{2,10},{10,2},{3,11},{11,3},{4,12},{12,4},... | collective-permute-start | bytes 1572872 | tf_op jit(solution)/shard_map/ppermute | solution.py:350
  74.9 1.6 %collective-permute-start.9 = (f32[512,128]{1,0:T(8,128)S(1)}, f32[512,128]{1,0:T(8,128)S(1)}, u32[]{:S(2)}, u32[]{:S(2)}) collective-permute-start(f32[512,128]{1,0:T(8,128)S(1)} %get-tuple-element.34.mine), channel_id=1, source_target_pairs={{0,1},{1,0},{2,3},{3,2},{4,5},{5,4},{6,7},{7,6},{8,9},{9,8},{10,11... | collective-permute-start | bytes 786440 | tf_op jit(solution)/shard_map/ppermute | solution.py:370
  76.5 12.8 %collective-permute-start.10 = (f32[256,1024]{1,0:T(8,128)S(1)}, f32[256,1024]{1,0:T(8,128)S(1)}, u32[]{:S(2)}, u32[]{:S(2)}) collective-permute-start(f32[256,1024]{1,0:T(8,128)S(1)} %shard_map.76), channel_id=1, source_target_pairs={{0,1},{1,0},{2,3},{3,2},{4,5},{5,4},{6,7},{7,6},{8,9},{9,8},{10,11... | collective-permute-start | bytes 3145736 | tf_op jit(solution)/shard_map/ppermute | solution.py:371
  87.9 1.4 %collective-permute-start.11 = (f32[256,128]{1,0:T(8,128)S(1)}, f32[256,128]{1,0:T(8,128)S(1)}, u32[]{:S(2)}, u32[]{:S(2)}) collective-permute-start(f32[256,128]{1,0:T(8,128)S(1)} %get-tuple-element.44), channel_id=1, source_target_pairs={{0,1},{1,0},{2,3},{3,2},{4,5},{5,4},{6,7},{7,6},{8,9},{9,8},{10,11... | collective-permute-start | bytes 393224 | tf_op jit(solution)/shard_map/ppermute | solution.py:374
  90.7 7.4 %copy-start.4 = (s32[256]{0:T(256)S(1)}, s32[256]{0:T(256)}, u32[]{:S(2)}) copy-start(s32[256]{0:T(256)} %param.7) | copy-start | bytes 3076
  90.7 27.5 %all-to-all-start.3 = ((bf16[16,32,1152]{2,1,0:T(8,128)(2,1)}), bf16[16,32,1152]{2,1,0:T(8,128)(2,1)S(1)}, u32[]{:S(2)}, u32[]{:S(2)}) async-start(bf16[16,32,1152]{2,1,0:T(8,128)(2,1)} %bitcast.4), calls=%async_computation.3 | async-start | bytes 2359296 | tf_op jit(solution)/shard_map/all_to_all | solution.py:336

commit v3 on v2

--- a/solution.py
+++ b/solution.py
@@ -22,7 +22,6 @@
 LEFT = [(i, (i + 3) % 4) for i in range(4)]
 SWAP = [(0, 1), (1, 0)]
 PLACES = [(0, 0), (0, 3), (0, 1), (1, 0), (0, 2), (1, 3), (1, 1), (1, 2)]
-EXTRA = 128
 
 
 def params():
@@ -107,21 +106,6 @@
         compiler_params=params(),
         cost_estimate=pl.CostEstimate(flops=0, bytes_accessed=2**20, transcendentals=0),
     )(*arrays)
-
-
-def tie_kernel(value, after, out):
-    del value, after, out
-
-
-def tie(value, after):
-    return pl.pallas_call(
-        tie_kernel,
-        out_shape=jax.ShapeDtypeStruct(value.shape, value.dtype),
-        in_specs=[hbm(), hbm()],
-        out_specs=hbm(),
-        input_output_aliases={0: 0},
-        compiler_params=params(),
-    )(value, after)
 
 
 def score_kernel(pieces, count, carry, last, own, sib, *refs):
@@ -188,7 +172,8 @@
     )(own, sib, *arrays, *carry)
 
 
-def fore_kernel(mine, other, *refs):
+def fore_kernel(mine, other, after, *refs):
+    del after
     out, refs = refs[-1], refs[:-1]
     both = mine[...] + jnp.concatenate([other[ROWS:], other[:ROWS]], axis=0)
     stat = both[:, 64:65] / both[:, 0:1]
@@ -204,16 +189,16 @@
         out[d] = out[0]
 
 
-def fore(mine, other, parts):
+def fore(mine, other, after, parts):
     flat = [a for part in parts for a in part]
     return pl.pallas_call(
         fore_kernel,
         out_shape=jax.ShapeDtypeStruct((8, 24, ROWS), F32),
-        in_specs=[vm()] * (2 + len(flat)),
+        in_specs=[vm()] * 2 + [hbm()] + [vm()] * len(flat),
         out_specs=vm(),
         compiler_params=params(),
         cost_estimate=pl.CostEstimate(flops=2**22, bytes_accessed=5 * 2**20, transcendentals=0),
-    )(mine, other, *flat)
+    )(mine, other, after, *flat)
 
 
 def back_kernel(heard, *refs):
@@ -230,7 +215,7 @@
     own_stat = pick(stat, position(0))
     mean = pick(sums[16:24], position(0)) / pick(sums[0:8], position(0))
     margin = own_stat - 0.5 * (own_stat + mean)
-    target[...] = jnp.transpose(jnp.broadcast_to(margin, (128, ROWS)))
+    target[...] = margin
     acc = jnp.zeros((2 * ROWS, 128), F32)
     place = 0
     for weight in weights:
@@ -246,7 +231,11 @@
 def back(heard, weights):
     return pl.pallas_call(
         back_kernel,
-        out_shape=(jax.ShapeDtypeStruct((ROWS, 128), F32),) * 3,
+        out_shape=(
+            jax.ShapeDtypeStruct((ROWS, 128), F32),
+            jax.ShapeDtypeStruct((ROWS, 128), F32),
+            jax.ShapeDtypeStruct((1, ROWS), F32),
+        ),
         in_specs=[vm()] * (1 + len(weights)),
         out_specs=(vm(),) * 3,
         compiler_params=params(),
@@ -254,91 +243,144 @@
     )(heard, *weights)
 
 
-def home_kernel(mine, other, partner, partner_in, back_own, back_in, target, out):
+def home_kernel(mine, other, partner, partner_in, *refs):
+    outs, rows = refs[:4], refs[4]
+    denom = mine[:ROWS, 0:1] + other[ROWS:, 0:1]
+    rows[...] = ((partner[...] + partner_in[...]) / denom).astype(BF16)
+    zh, y = lax.axis_index("zh"), lax.axis_index("y")
+    for d in range(4):
+        for u in range(2):
+            block = ((zh + u) % 2) * 4 + (y + d) % 4
+            outs[d][pl.ds(32 * u, 32)] = rows[pl.ds(pl.multiple_of(block * 32, 32), 32)]
+
+
+def home(mine, other, partner, partner_in):
+    return pl.pallas_call(
+        home_kernel,
+        out_shape=(jax.ShapeDtypeStruct((64, WIDTH), BF16),) * 4,
+        in_specs=[vm()] * 4,
+        out_specs=(vm(),) * 4,
+        scratch_shapes=[pltpu.VMEM((ROWS, WIDTH), BF16)],
+        compiler_params=params(),
+        cost_estimate=pl.CostEstimate(flops=2**20, bytes_accessed=3 * 2**20, transcendentals=0),
+    )(mine, other, partner, partner_in)
+
+
+def turn_kernel(r0, r1, r2, r3, *outs):
+    for u, out in enumerate(outs):
+        for d, r in enumerate((r0, r1, r2, r3)):
+            out[pl.ds(32 * d, 32)] = r[pl.ds(32 * u, 32)]
+
+
+def turn(rows):
+    return pl.pallas_call(
+        turn_kernel,
+        out_shape=(jax.ShapeDtypeStruct((128, WIDTH), BF16),) * 2,
+        in_specs=[vm()] * 4,
+        out_specs=(vm(),) * 2,
+        compiler_params=params(),
+        cost_estimate=pl.CostEstimate(flops=0, bytes_accessed=2**20, transcendentals=0),
+    )(*rows)
+
+
+def margin_kernel(mine, other, back_own, back_in, target, out):
     total = mine[:ROWS] + other[ROWS:]
     denom = total[:, 0:1]
     stat = total[:, 64:65] / denom
     margin = stat - 0.5 * (stat + (back_own[:, 0:1] + back_in[:, 0:1]) / denom)
-    lane = lax.broadcasted_iota(I32, (ROWS, EXTRA), 1)
-    value = jnp.where(lane < 2, margin, target[...])
-    high = value.astype(BF16).astype(F32)
-    extra = jnp.where((lane & 1) == 0, high, value - high).astype(BF16)
-    rows = ((partner[...] + partner_in[...]) / denom).astype(BF16)
-    for i in range(8):
-        for z in range(2):
-            place = pl.ds((2 * i + z) * 32, 32)
-            out[place, pl.ds(0, WIDTH)] = rows[32 * i : 32 * i + 32]
-            out[place, pl.ds(WIDTH, EXTRA)] = extra[32 * i : 32 * i + 32]
-
-
-def home(mine, other, partner, partner_in, back_own, back_in, target):
-    return pl.pallas_call(
-        home_kernel,
-        out_shape=jax.ShapeDtypeStruct((PACK, WIDTH + EXTRA), BF16),
-        in_specs=[vm()] * 7,
+    row = jnp.transpose(jnp.broadcast_to(margin, (ROWS, 128)))
+    both = jnp.concatenate([row[0:1], target[...]], axis=0)
+    for d in range(16):
+        out[d] = both
+
+
+def margins(mine, other, back_own, back_in, target):
+    return pl.pallas_call(
+        margin_kernel,
+        out_shape=jax.ShapeDtypeStruct((16, 2, ROWS), F32),
+        in_specs=[vm()] * 5,
         out_specs=vm(),
         compiler_params=params(),
-        cost_estimate=pl.CostEstimate(flops=2**20, bytes_accessed=3 * 2**20, transcendentals=0),
-    )(mine, other, partner, partner_in, back_own, back_in, target)
-
-
-def slots_kernel(src_labels, tgt_labels, src, tgt):
-    for labels, out in ((src_labels, src), (tgt_labels, tgt)):
-        slots = route_matrix(labels[...], lax.axis_index("zl")).astype(F32)
-        out[...] = jnp.transpose(slots).astype(BF16)
-
-
-def slots(src_labels, tgt_labels):
+        cost_estimate=pl.CostEstimate(flops=2**18, bytes_accessed=2**20, transcendentals=0),
+    )(mine, other, back_own, back_in, target)
+
+
+def slots_kernel(labels, out):
+    zh, y, zl = lax.axis_index("zh"), lax.axis_index("y"), lax.axis_index("zl")
+    slot = slot_row(labels[...], zl)
+    bucket = slot >> 6
+    peer = ((bucket >> 2) ^ zh) * 8 + (((slot >> 5) & 1) ^ zl) * 4 + ((y - (bucket & 3)) & 3)
+    place = peer * 32 + (slot & 31)
+    out[...] = jnp.transpose((lax.broadcasted_iota(I32, (PACK, ROWS), 0) == place).astype(F32)).astype(BF16)
+
+
+def slots(labels):
     return pl.pallas_call(
         slots_kernel,
-        out_shape=(jax.ShapeDtypeStruct((ROWS, PACK), BF16),) * 2,
-        in_specs=[vm()] * 2,
-        out_specs=(vm(),) * 2,
+        out_shape=jax.ShapeDtypeStruct((ROWS, PACK), BF16),
+        in_specs=[vm()],
+        out_specs=vm(),
         compiler_params=params(),
         cost_estimate=pl.CostEstimate(flops=2**24, bytes_accessed=2**19, transcendentals=0),
-    )(src_labels, tgt_labels)
-
-
-def unpack_kernel(src, tgt, got, extra, partner, src_out, tgt_out):
-    partner[...] = jnp.dot(src[...], got[...], preferred_element_type=F32)
-
-    @pl.when(pl.program_id(0) == 0)
-    def _():
-        for slots, first, out in ((src, 0, src_out), (tgt, 2, tgt_out)):
-            found = jnp.transpose(jnp.dot(slots[...], extra[...], preferred_element_type=F32))
-            out[...] = found[first : first + 1] + found[first + 1 : first + 2]
-
-
-def unpack(src_slots, tgt_slots, got):
-    whole = pl.BlockSpec((ROWS, PACK), lambda g: (0, 0))
-    row = pl.BlockSpec((1, ROWS), lambda g: (0, 0))
+    )(labels)
+
+
+def unpack_kernel(place, g0, g1, g2, g3, partner, token):
+    got = jnp.concatenate([g[...] for g in (g0, g1, g2, g3)], axis=0)
+    partner[...] = jnp.dot(place[...], got, preferred_element_type=F32)
+    token[...] = jnp.zeros_like(token)
+
+
+def unpack(place, got):
     return pl.pallas_call(
         unpack_kernel,
-        out_shape=(
-            jax.ShapeDtypeStruct((ROWS, WIDTH), F32),
-            jax.ShapeDtypeStruct((1, ROWS), F32),
-            jax.ShapeDtypeStruct((1, ROWS), F32),
-        ),
+        out_shape=(jax.ShapeDtypeStruct((ROWS, WIDTH), F32), jax.ShapeDtypeStruct((8, 128), F32)),
         grid=(4,),
-        in_specs=[
-            whole,
-            whole,
-            pl.BlockSpec((PACK, 256), lambda g: (0, g)),
-            pl.BlockSpec((PACK, EXTRA), lambda g: (0, WIDTH // EXTRA)),
-        ],
-        out_specs=(pl.BlockSpec((ROWS, 256), lambda g: (0, g)), row, row),
+        in_specs=[pl.BlockSpec((ROWS, PACK), lambda g: (0, 0))] + [pl.BlockSpec((128, 256), lambda g: (0, g))] * 4,
+        out_specs=(pl.BlockSpec((ROWS, 256), lambda g: (0, g)), pl.BlockSpec((8, 128), lambda g: (0, 0))),
         compiler_params=params(),
         cost_estimate=pl.CostEstimate(flops=2 * PACK * ROWS * WIDTH, bytes_accessed=2**21, transcendentals=0),
-    )(src_slots, tgt_slots, got, got)
+    )(place, *got)
+
+
+def finish_kernel(src_labels, tgt_labels, got, after, src_out, tgt_out):
+    del after
+    for kind, labels, out in ((0, src_labels, src_out), (1, tgt_labels, tgt_out)):
+        slot = slot_row(labels[...], lax.axis_index("zl"))
+        column = lax.axis_index(("zh", "y")) * 32 + (slot & 31)
+        place = (lax.broadcasted_iota(I32, (ROWS, ROWS), 0) == column).astype(BF16)
+        values = jnp.concatenate([got[s, kind : kind + 1] for s in range(16)], axis=0)
+        found = jnp.zeros((16, ROWS), F32)
+        for _ in range(3):
+            piece = values.astype(BF16)
+            values = values - piece.astype(F32)
+            found = found + jnp.dot(piece, place, preferred_element_type=F32)
+        here = lax.broadcasted_iota(I32, (16, ROWS), 0) == (slot >> 5)
+        out[...] = jnp.sum(jnp.where(here, found, 0.0), axis=0, keepdims=True)
+
+
+def finish(src_labels, tgt_labels, got, after):
+    return pl.pallas_call(
+        finish_kernel,
+        out_shape=(jax.ShapeDtypeStruct((1, ROWS), F32),) * 2,
+        in_specs=[vm()] * 3 + [hbm()],
+        out_specs=(vm(), vm()),
+        compiler_params=params(),
+        cost_estimate=pl.CostEstimate(flops=2**24, bytes_accessed=2**16, transcendentals=0),
+    )(src_labels, tgt_labels, got, after)
 
 
 def route(packed):
     return lax.all_to_all(packed, ROUTE, 0, 0, tiled=True)
 
 
+def shift(d):
+    return [(i, (i + d) % 4) for i in range(4)]
+
+
 def on_device(source, source_label, target, target_label):
     src_labels, tgt_labels = source_label.reshape(1, ROWS), target_label.reshape(1, ROWS)
-    src_slots, tgt_slots = slots(src_labels, tgt_labels)
+    place = slots(src_labels)
 
     base = merge(route(pack(tgt_labels, target)))
     left, right = lax.ppermute(base, "x", RIGHT), lax.ppermute(base, "x", LEFT)
@@ -368,13 +410,21 @@
         carry = (*fwd, own, sib)
     (fwd,) = fwd
     fwd_in = lax.ppermute(fwd, "c", SWAP)
-    partner_in = lax.ppermute(tie(sib, fwd_in), "c", SWAP)
-    heard = lax.all_to_all(fore(fwd, fwd_in, parts), PLANE, 0, 0, tiled=True)
+    partner_in = lax.ppermute(sib, "c", SWAP)
+
+    by_y = home(fwd, fwd_in, own, partner_in)
+    by_y = (by_y[0],) + tuple(lax.ppermute(by_y[d], "y", shift(d)) for d in (1, 2, 3))
+    same, flip = turn(by_y)
+    got = [same] + [
+        lax.ppermute(rows, ("zh", "zl"), [(i, i ^ z) for i in range(4)]) for z, rows in ((1, same), (2, flip), (3, flip))
+    ]
+    partner_out, token = unpack(place, got)
+
+    heard = lax.all_to_all(fore(fwd, fwd_in, by_y[0], parts), PLANE, 0, 0, tiled=True)
     back_own, back_sib, tgt_margin = back(heard, [part[0] for part in parts])
     back_in = lax.ppermute(back_sib, "c", SWAP)
-    packed = home(fwd, fwd_in, own, partner_in, back_own, back_in, tgt_margin)
-    got = route(packed.reshape(16, 32, -1)).reshape(PACK, WIDTH + EXTRA)
-    partner_out, src_margin, tgt_margin = unpack(src_slots, tgt_slots, got)
+    both = route(margins(fwd, fwd_in, back_own, back_in, tgt_margin))
+    src_margin, tgt_margin = finish(src_labels, tgt_labels, both, token)
     return (partner_out, src_margin.reshape(ROWS), tgt_margin.reshape(ROWS))
 
 

time: 122 us -> 116 us (0.951)
  waiting for transfers between devices: 45.4 us -> 29.8 us
  starting transfers between devices: 23.4 us -> 36.7 us
  blocking collectives: 35.4 us -> 25 us
  Pallas kernels: 14 us -> 18.8 us
  local copies, waits for them, and re-layouts: 1.73 us -> 3.94 us
    all_to_all x2, waiting for transfers between devices: 19.7 us -> 0.39 us  [route(): return lax.all_to_all(packed, ROUTE, 0, 0, tiled=True)]
    ppermute x1 -> x7, starting transfers between devices: 0.14 us -> 11 us  [the longest x3 6.18 us: on_device(): lax.ppermute(by_y[d], 'y', shift(d))]
    all_to_all x1 -> x0, blocking collectives: 10.3 us -> none  [on_device(): heard = lax.all_to_all(fore(fwd, fwd_in, parts), PLANE, 0, 0, tiled=True)]
    all_to_all x0 -> x1, starting transfers between devices: none -> 3.57 us  [on_device(): lax.all_to_all(fore(fwd, fwd_in, by_y[0], parts), PLANE, 0, 0, tiled=True)]
    pallas_call x3 -> x5, Pallas kernels: 1.78 us -> 4.95 us  [the longest x1 1.84 us: turn(): pl.pallas_call(turn_kernel, out_shape=(jax.ShapeDtypeStruct((128, WIDTH),...]
    ppermute x1 -> x7, waiting for transfers between devices: 0.01 us -> 3.13 us  [the longest x3 3.12 us: on_device(): lax.ppermute(rows, ('zh', 'zl'), [(i, i ^ z) for i in range(4)])]
    unnamed x10 -> x22, local copies, waits for them, and re-layouts: 1.73 us -> 3.94 us
    all_to_all x2, starting transfers between devices: 11 us -> 9.57 us  [route(): return lax.all_to_all(packed, ROUTE, 0, 0, tiled=True)]
  transfers between devices with their start and end apart: 14 -> 21, of which waited for: 9 -> 11; matrix products, arithmetic and copies ran while one was open for 0% -> 0% of each run, Pallas kernels for 5% -> 11%
where the time goes in v3:
time: 116 us; the launch traced here: 115 us
  starting transfers between devices  36.7 us (32%)
  waiting for transfers between devices  29.8 us (26%)
  blocking collectives  25 us (22%)
  Pallas kernels  18.8 us (16%)
  local copies, waits for them, and re-layouts  3.94 us (3%)
    all_to_all x1, blocking collectives, route(): return lax.all_to_all(packed, ROUTE, 0, 0, tiled=True)  25 us
    all_to_all x2, starting transfers between devices, route(): return lax.all_to_all(packed, ROUTE, 0, 0, tiled=True)  9.57 us
    ppermute x1, waiting for transfers between devices, on_device(): lax.ppermute(base, 'x', RIGHT)  8.47 us
    ppermute x1, waiting for transfers between devices, on_device(): lax.ppermute(across, 'x', RIGHT)  6.24 us
    ppermute x3, starting transfers between devices, on_device(): lax.ppermute(by_y[d], 'y', shift(d))  6.18 us
    pallas_call x2, Pallas kernels, score(): pl.pallas_call(partial(score_kernel, pieces, len(arrays), bool(carry), la...  6.18 us
    ppermute x3, starting transfers between devices, on_device(): lax.ppermute(rows, ('zh', 'zl'), [(i, i ^ z) for i in range(4)])  4.7 us
    ppermute x1, waiting for transfers between devices, on_device(): lax.ppermute(go_right, 'x', RIGHT)  4.35 us
  transfers between devices with their start and end apart: 21, of which 11 were waited for; matrix products, arithmetic and copies ran while one was open for 0% of the time, Pallas kernels for 11%

profile of v3, /device:TPU:0, one launch (start us, length us, event | category | flops | bytes accessed | tf_op | source)
XLA Modules:
  0.0 115.2 jit_solution(152441105498703500)
XLA Ops:
  3.0 25.0 %all_to_all.20.arrived = bf16[16,32,1024]{2,1,0:T(8,128)(2,1)S(1)} all-to-all(bf16[16,32,1024]{2,1,0:T(8,128)(2,1)S(1)} %bitcast.6), channel_id=1, replica_groups=mesh['zh'=2,'y'=4,'zl'=2,'x'=4,'c'=2] {'zh','y','zl'}, dimensions={0} | all-to-all | bytes 2097152 | tf_op jit(solution)/shard_map/all_to_all | solution.py:374
  28.1 1.6 %shard_map.70 = bf16[512,1024]{1,0:T(8,128)(2,1)} custom-call(s32[1,256]{1,0:T(1,128)S(1)} %bitcast.7, bf16[256,1024]{1,0:T(8,128)(2,1)S(1)} %copy-done.7, bf16[256,1024]{1,0:T(8,128)(2,1)S(1)} %shard_map.69.refs_0_), custom_call_target="tpu_custom_call" | custom-call | flops 268435456 | bytes 1572864 | tf_op jit(solution)/shard_map/pallas_call | solution.py:66
  29.7 3.7 %all-to-all-start.1 = ((bf16[16,32,1024]{2,1,0:T(8,128)(2,1)}), bf16[16,32,1024]{2,1,0:T(8,128)(2,1)S(1)}, u32[]{:S(2)}, u32[]{:S(2)}) async-start(bf16[16,32,1024]{2,1,0:T(8,128)(2,1)} %bitcast.3), calls=%async_computation.1 | async-start | bytes 2097152 | tf_op jit(solution)/shard_map/all_to_all | solution.py:374
  35.0 1.7 %collective-permute-start.1 = (bf16[256,1024]{1,0:T(8,128)(2,1)S(1)}, bf16[256,1024]{1,0:T(8,128)(2,1)S(1)}, u32[]{:S(2)}, u32[]{:S(2)}) collective-permute-start(bf16[256,1024]{1,0:T(8,128)(2,1)S(1)} %shard_map.69.refs_0_), channel_id=1, source_target_pairs={{0,6},{2,0},{4,2},{6,4},{1,7},{3,1},{5,3},{7,5},{8,14},{10,8},{12,... | collective-permute-start | bytes 1572872 | tf_op jit(solution)/shard_map/ppermute | solution.py:386
  36.7 1.7 %collective-permute-start.5 = (bf16[256,1024]{1,0:T(8,128)(2,1)S(1)}, bf16[256,1024]{1,0:T(8,128)(2,1)}, u32[]{:S(2)}, u32[]{:S(2)}) collective-permute-start(bf16[256,1024]{1,0:T(8,128)(2,1)S(1)} %shard_map.69.refs_0_), channel_id=1, source_target_pairs={{0,8},{8,0},{1,9},{9,1},{2,10},{10,2},{3,11},{11,3},{4,12},{12,4},... | collective-permute-start | bytes 1572872 | tf_op jit(solution)/shard_map/ppermute | solution.py:387
  38.4 8.5 %collective-permute-done.refs_0_.refs_1_ = bf16[256,1024]{1,0:T(8,128)(2,1)S(1)} collective-permute-done((bf16[256,1024]{1,0:T(8,128)(2,1)S(1)}, bf16[256,1024]{1,0:T(8,128)(2,1)S(1)}, u32[]{:S(2)}, u32[]{:S(2)}) %collective-permute-start) | collective-permute-done | bytes 524320 | tf_op jit(solution)/shard_map/ppermute | solution.py:386
  48.5 2.5 %collective-permute-start.3 = (bf16[128,1024]{1,0:T(8,128)(2,1)S(1)}, bf16[128,1024]{1,0:T(8,128)(2,1)S(1)}, u32[]{:S(2)}, u32[]{:S(2)}) collective-permute-start(bf16[128,1024]{1,0:T(8,128)(2,1)S(1)} %get-tuple-element.32), channel_id=1, source_target_pairs={{0,6},{2,0},{4,2},{6,4},{1,7},{3,1},{5,3},{7,5},{8,14},{10,8},{12,... | collective-permute-start | bytes 786440 | tf_op jit(solution)/shard_map/ppermute | solution.py:389
  51.0 4.3 %collective-permute-done.2.refs_0_ = bf16[128,1024]{1,0:T(8,128)(2,1)S(1)} collective-permute-done((bf16[128,1024]{1,0:T(8,128)(2,1)S(1)}, bf16[128,1024]{1,0:T(8,128)(2,1)S(1)}, u32[]{:S(2)}, u32[]{:S(2)}) %collective-permute-start.2) | collective-permute-done | bytes 262176 | tf_op jit(solution)/shard_map/ppermute | solution.py:389
  55.5 1.9 %collective-permute-done.5.refs_3_ = bf16[256,1024]{1,0:T(8,128)(2,1)} collective-permute-done((bf16[256,1024]{1,0:T(8,128)(2,1)S(1)}, bf16[256,1024]{1,0:T(8,128)(2,1)}, u32[]{:S(2)}, u32[]{:S(2)}) %collective-permute-start.5) | collective-permute-done | bytes 524320 | tf_op jit(solution)/shard_map/ppermute | solution.py:387
  58.6 2.0 %collective-permute-start.7 = (bf16[256,1024]{1,0:T(8,128)(2,1)}, bf16[256,1024]{1,0:T(8,128)(2,1)S(1)}, u32[]{:S(2)}, u32[]{:S(2)}) collective-permute-start(bf16[256,1024]{1,0:T(8,128)(2,1)} %collective-permute-done.5.refs_3_), channel_id=1, source_target_pairs={{0,6},{2,0},{4,2},{6,4},{1,7},{3,1},{5,3},{7,5},{8,14},{10,8},{12,... | collective-permute-start | bytes 1572872 | tf_op jit(solution)/shard_map/ppermute | solution.py:390
  61.1 4.2 %shard_map.74 = (f32[5,512,256]{2,1,0:T(8,128)S(1)}, f32[5,256]{1,0:T(8,128)S(1)}, f32[5,256]{1,0:T(8,128)S(1)}, f32[256,1024]{1,0:T(8,128)S(1)}, f32[256,1024]{...) custom-call(bf16[256,1024]{1,0:T(8,128)(2,1)S(1)} %shard_map.72.own, ...), custom_call_target="tpu_custom_call" | custom-call | flops 2684354560 | bytes 9437184 | tf_op jit(solution)/shard_map/pallas_call | solution.py:155
  65.3 6.2 %collective-permute-done.6.refs_0_ = bf16[256,1024]{1,0:T(8,128)(2,1)S(1)} collective-permute-done((bf16[256,1024]{1,0:T(8,128)(2,1)}, bf16[256,1024]{1,0:T(8,128)(2,1)S(1)}, u32[]{:S(2)}, u32[]{:S(2)}) %collective-permute-start.6) | collective-permute-done | bytes 524320 | tf_op jit(solution)/shard_map/ppermute | solution.py:390
  72.9 2.0 %shard_map.75 = (f32[3,512,256]{2,1,0:T(8,128)S(1)}, f32[3,256]{1,0:T(4,128)S(1)}, f32[3,256]{1,0:T(4,128)S(1)}, f32[256,1024]{1,0:T(8,128)S(1)}, f32[256,1024]{1,0:T(8,128)S(1)}, /*index=5*/f32[512,128]{1,0:T(8,128)S(1)}) custom-call(bf16[256,1024]{1,0:T(8,128)(2,1)S(1)} %shard_map.72.own, bf16[256,1024]{1,0:T(8,128)(2,1)S(1)} %collective-permute-done.4.sib, ...), custom_call_target="tpu_custom_call" | custom-call | flops 1610612736 | bytes 7340032 | tf_op jit(solution)/shard_map/pallas_call | solution.py:155
  75.5 2.5 %collective-permute-done.9.other = f32[512,128]{1,0:T(8,128)S(1)} collective-permute-done((f32[512,128]{1,0:T(8,128)S(1)}, f32[512,128]{1,0:T(8,128)S(1)}, u32[]{:S(2)}, u32[]{:S(2)}) %collective-permute-start.9) | collective-permute-done | bytes 262176 | tf_op jit(solution)/shard_map/ppermute | solution.py:412
  79.0 2.5 %collective-permute-start.11 = (bf16[64,1024]{1,0:T(8,128)(2,1)}, bf16[64,1024]{1,0:T(8,128)(2,1)}, u32[]{:S(2)}, u32[]{:S(2)}) collective-permute-start(bf16[64,1024]{1,0:T(8,128)(2,1)} %get-tuple-element.41), channel_id=1, source_target_pairs={{0,16},{16,32},{32,48},{48,0},{1,17},{17,33},{33,49},{49,1},{2,18}... | collective-permute-start | bytes 393224 | tf_op jit(solution)/shard_map/ppermute | solution.py:416
  81.5 1.7 %collective-permute-start.12 = (bf16[64,1024]{1,0:T(8,128)(2,1)}, bf16[64,1024]{1,0:T(8,128)(2,1)}, u32[]{:S(2)}, u32[]{:S(2)}) collective-permute-start(bf16[64,1024]{1,0:T(8,128)(2,1)} %get-tuple-element.42), channel_id=1, source_target_pairs={{0,32},{16,48},{32,0},{48,16},{1,33},{17,49},{33,1},{49,17},{2,34}... | collective-permute-start | bytes 393224 | tf_op jit(solution)/shard_map/ppermute | solution.py:416
  83.2 2.0 %collective-permute-start.13 = (bf16[64,1024]{1,0:T(8,128)(2,1)}, bf16[64,1024]{1,0:T(8,128)(2,1)}, u32[]{:S(2)}, u32[]{:S(2)}) collective-permute-start(bf16[64,1024]{1,0:T(8,128)(2,1)} %get-tuple-element.43), channel_id=1, source_target_pairs={{0,48},{16,0},{32,16},{48,32},{1,49},{17,1},{33,17},{49,33},{2,50}... | collective-permute-start | bytes 393224 | tf_op jit(solution)/shard_map/ppermute | solution.py:416
  86.3 3.6 %all-to-all-start.2 = ((f32[8,24,256]{2,1,0:T(8,128)}), f32[8,24,256]{2,1,0:T(8,128)S(1)}, u32[]{:S(2)}, u32[]{:S(2)}) async-start(f32[8,24,256]{2,1,0:T(8,128)} %shard_map.79), calls=%async_computation.2 | async-start | bytes 393216 | tf_op jit(solution)/shard_map/all_to_all | solution.py:423
  89.9 1.8 %shard_map.77 = (bf16[128,1024]{1,0:T(8,128)(2,1)}, bf16[128,1024]{1,0:T(8,128)(2,1)}) custom-call(bf16[64,1024]{1,0:T(8,128)(2,1)S(1)} %get-tuple-element.40.r0.after, bf16[64,1024]{1,0:T(8,128)(2,1)} %collective-permute-done.11.r1, bf16[64,1024]{1,0:T(8,128)(2,1)} %collective-permute-done.12.r2, bf16[64,1024]{1,0:T(8,128)(2,1)} %collective-permute-done.13.r3), custom_call_target="tpu_custom_call" | custom-call | bytes 1048576 | tf_op jit(solution)/shard_map/pallas_call | solution.py:276
  91.8 1.8 %collective-permute-start.14 = (bf16[128,1024]{1,0:T(8,128)(2,1)}, bf16[128,1024]{1,0:T(8,128)(2,1)}, u32[]{:S(2)}, u32[]{:S(2)}) collective-permute-start(bf16[128,1024]{1,0:T(8,128)(2,1)} %get-tuple-element.44.g0), channel_id=1, source_target_pairs={{0,8},{8,0},{64,72},{72,64},{1,9},{9,1},{65,73},{73,65},{2,10},{10... | collective-permute-start | bytes 786440 | tf_op jit(solution)/shard_map/ppermute | solution.py:419
  93.6 2.7 %collective-permute-start.15 = (bf16[128,1024]{1,0:T(8,128)(2,1)}, bf16[128,1024]{1,0:T(8,128)(2,1)}, u32[]{:S(2)}, u32[]{:S(2)}) collective-permute-start(bf16[128,1024]{1,0:T(8,128)(2,1)} %get-tuple-element.45), channel_id=1, source_target_pairs={{0,64},{8,72},{64,0},{72,8},{1,65},{9,73},{65,1},{73,9},{2,66},{10... | collective-permute-start | bytes 786440 | tf_op jit(solution)/shard_map/ppermute | solution.py:419
  100.7 5.9 %all-to-all-start.3 = ((f32[16,2,256]{2,1,0:T(2,128)}), f32[16,2,256]{2,1,0:T(2,128)S(1)}, u32[]{:S(2)}, u32[]{:S(2)}) async-start(f32[16,2,256]{2,1,0:T(2,128)} %shard_map.81), calls=%async_computation.3 | async-start | bytes 65536 | tf_op jit(solution)/shard_map/all_to_all | solution.py:374
  108.4 1.7 %collective-permute-done.16.g3 = bf16[128,1024]{1,0:T(8,128)(2,1)} collective-permute-done((bf16[128,1024]{1,0:T(8,128)(2,1)}, bf16[128,1024]{1,0:T(8,128)(2,1)}, u32[]{:S(2)}, u32[]{:S(2)}) %collective-permute-start.16) | collective-permute-done | bytes 262176 | tf_op jit(solution)/shard_map/ppermute | solution.py:419
  110.1 3.8 %shard_map.78 = (f32[256,1024]{1,0:T(8,128)}, f32[8,128]{1,0:T(8,128)S(1)}) custom-call(bf16[256,512]{1,0:T(8,128)(2,1)S(1)} %shard_map.67.place, bf16[128,1024]{1,0:T(8,128)(2,1)} %get-tuple-element.44.g0, bf16[128,1024]{1,0:T(8,128)(2,1)} %collective-permute-done.14.g1, bf16[128,1024]{1,0:T(8,128)(2,1)} %collective-permute-done.15.g2, ...), custom_call_target="tpu_custom_call" | custom-call | flops 268435456 | bytes 2097152 | tf_op jit(solution)/shard_map/pallas_call | solution.py:335
  (57 shorter events, 19.0 us)
Async XLA Ops:
  2.4 25.8 %copy-start.7 = (bf16[256,1024]{1,0:T(8,128)(2,1)S(1)}, bf16[256,1024]{1,0:T(8,128)(2,1)}, u32[]{:S(2)}) copy-start(bf16[256,1024]{1,0:T(8,128)(2,1)} %rows.3) | copy-start | bytes 1572868
  2.4 25.8 %copy-start.8 = (s32[256]{0:T(256)S(1)}, s32[256]{0:T(256)}, u32[]{:S(2)}) copy-start(s32[256]{0:T(256)} %param.5) | copy-start | bytes 3076
  29.7 25.6 %all-to-all-start.1 = ((bf16[16,32,1024]{2,1,0:T(8,128)(2,1)}), bf16[16,32,1024]{2,1,0:T(8,128)(2,1)S(1)}, u32[]{:S(2)}, u32[]{:S(2)}) async-start(bf16[16,32,1024]{2,1,0:T(8,128)(2,1)} %bitcast.3), calls=%async_computation.1 | async-start | bytes 2097152 | tf_op jit(solution)/shard_map/all_to_all | solution.py:374
  33.4 13.5 %collective-permute-start = (bf16[256,1024]{1,0:T(8,128)(2,1)S(1)}, bf16[256,1024]{1,0:T(8,128)(2,1)S(1)}, u32[]{:S(2)}, u32[]{:S(2)}) collective-permute-start(bf16[256,1024]{1,0:T(8,128)(2,1)S(1)} %shard_map.69.refs_0_), channel_id=1, source_target_pairs={{0,2},{2,4},{4,6},{6,0},{1,3},{3,5},{5,7},{7,1},{8,10},{10,12},{12... | collective-permute-start | bytes 1572872 | tf_op jit(solution)/shard_map/ppermute | solution.py:386
  35.0 12.0 %collective-permute-start.1 = (bf16[256,1024]{1,0:T(8,128)(2,1)S(1)}, bf16[256,1024]{1,0:T(8,128)(2,1)S(1)}, u32[]{:S(2)}, u32[]{:S(2)}) collective-permute-start(bf16[256,1024]{1,0:T(8,128)(2,1)S(1)} %shard_map.69.refs_0_), channel_id=1, source_target_pairs={{0,6},{2,0},{4,2},{6,4},{1,7},{3,1},{5,3},{7,5},{8,14},{10,8},{12,... | collective-permute-start | bytes 1572872 | tf_op jit(solution)/shard_map/ppermute | solution.py:386
  36.7 20.7 %collective-permute-start.5 = (bf16[256,1024]{1,0:T(8,128)(2,1)S(1)}, bf16[256,1024]{1,0:T(8,128)(2,1)}, u32[]{:S(2)}, u32[]{:S(2)}) collective-permute-start(bf16[256,1024]{1,0:T(8,128)(2,1)S(1)} %shard_map.69.refs_0_), channel_id=1, source_target_pairs={{0,8},{8,0},{1,9},{9,1},{2,10},{10,2},{3,11},{11,3},{4,12},{12,4},... | collective-permute-start | bytes 1572872 | tf_op jit(solution)/shard_map/ppermute | solution.py:387
  47.8 7.6 %collective-permute-start.2 = (bf16[128,1024]{1,0:T(8,128)(2,1)S(1)}, bf16[128,1024]{1,0:T(8,128)(2,1)S(1)}, u32[]{:S(2)}, u32[]{:S(2)}) collective-permute-start(bf16[128,1024]{1,0:T(8,128)(2,1)S(1)} %get-tuple-element.31), channel_id=1, source_target_pairs={{0,2},{2,4},{4,6},{6,0},{1,3},{3,5},{5,7},{7,1},{8,10},{10,12},{12... | collective-permute-start | bytes 786440 | tf_op jit(solution)/shard_map/ppermute | solution.py:389
  48.5 6.8 %collective-permute-start.3 = (bf16[128,1024]{1,0:T(8,128)(2,1)S(1)}, bf16[128,1024]{1,0:T(8,128)(2,1)S(1)}, u32[]{:S(2)}, u32[]{:S(2)}) collective-permute-start(bf16[128,1024]{1,0:T(8,128)(2,1)S(1)} %get-tuple-element.32), channel_id=1, source_target_pairs={{0,6},{2,0},{4,2},{6,4},{1,7},{3,1},{5,3},{7,5},{8,14},{10,8},{12,... | collective-permute-start | bytes 786440 | tf_op jit(solution)/shard_map/ppermute | solution.py:389
  55.4 5.7 %collective-permute-start.4 = (bf16[256,1024]{1,0:T(8,128)(2,1)S(1)}, bf16[256,1024]{1,0:T(8,128)(2,1)S(1)}, u32[]{:S(2)}, u32[]{:S(2)}) collective-permute-start(bf16[256,1024]{1,0:T(8,128)(2,1)S(1)} %shard_map.72.own), channel_id=1, source_target_pairs={{0,1},{1,0},{2,3},{3,2},{4,5},{5,4},{6,7},{7,6},{8,9},{9,8},{10,11... | collective-permute-start | bytes 1572872 | tf_op jit(solution)/shard_map/ppermute | solution.py:395
  57.4 14.1 %collective-permute-start.6 = (bf16[256,1024]{1,0:T(8,128)(2,1)}, bf16[256,1024]{1,0:T(8,128)(2,1)S(1)}, u32[]{:S(2)}, u32[]{:S(2)}) collective-permute-start(bf16[256,1024]{1,0:T(8,128)(2,1)} %collective-permute-done.5.refs_3_), channel_id=1, source_target_pairs={{0,2},{2,4},{4,6},{6,0},{1,3},{3,5},{5,7},{7,1},{8,10},{10,12},{12... | collective-permute-start | bytes 1572872 | tf_op jit(solution)/shard_map/ppermute | solution.py:390
  58.6 12.9 %collective-permute-start.7 = (bf16[256,1024]{1,0:T(8,128)(2,1)}, bf16[256,1024]{1,0:T(8,128)(2,1)S(1)}, u32[]{:S(2)}, u32[]{:S(2)}) collective-permute-start(bf16[256,1024]{1,0:T(8,128)(2,1)} %collective-permute-done.5.refs_3_), channel_id=1, source_target_pairs={{0,6},{2,0},{4,2},{6,4},{1,7},{3,1},{5,3},{7,5},{8,14},{10,8},{12,... | collective-permute-start | bytes 1572872 | tf_op jit(solution)/shard_map/ppermute | solution.py:390
  60.7 12.2 %collective-permute-start.8 = (bf16[256,1024]{1,0:T(8,128)(2,1)S(1)}, bf16[256,1024]{1,0:T(8,128)(2,1)S(1)}, u32[]{:S(2)}, u32[]{:S(2)}) collective-permute-start(bf16[256,1024]{1,0:T(8,128)(2,1)S(1)} %shard_map.73.refs_4_), channel_id=1, source_target_pairs={{0,8},{8,0},{1,9},{9,1},{2,10},{10,2},{3,11},{11,3},{4,12},{12,4},... | collective-permute-start | bytes 1572872 | tf_op jit(solution)/shard_map/ppermute | solution.py:392
  74.9 3.1 %collective-permute-start.10 = (f32[256,1024]{1,0:T(8,128)S(1)}, f32[256,1024]{1,0:T(8,128)S(1)}, u32[]{:S(2)}, u32[]{:S(2)}) collective-permute-start(f32[256,1024]{1,0:T(8,128)S(1)} %get-tuple-element.39), channel_id=1, source_target_pairs={{0,1},{1,0},{2,3},{3,2},{4,5},{5,4},{6,7},{7,6},{8,9},{9,8},{10,11... | collective-permute-start | bytes 3145736 | tf_op jit(solution)/shard_map/ppermute | solution.py:413
  75.0 3.0 %collective-permute-start.9 = (f32[512,128]{1,0:T(8,128)S(1)}, f32[512,128]{1,0:T(8,128)S(1)}, u32[]{:S(2)}, u32[]{:S(2)}) collective-permute-start(f32[512,128]{1,0:T(8,128)S(1)} %get-tuple-element.37.mine), channel_id=1, source_target_pairs={{0,1},{1,0},{2,3},{3,2},{4,5},{5,4},{6,7},{7,6},{8,9},{9,8},{10,11... | collective-permute-start | bytes 786440 | tf_op jit(solution)/shard_map/ppermute | solution.py:412
  79.0 10.9 %collective-permute-start.11 = (bf16[64,1024]{1,0:T(8,128)(2,1)}, bf16[64,1024]{1,0:T(8,128)(2,1)}, u32[]{:S(2)}, u32[]{:S(2)}) collective-permute-start(bf16[64,1024]{1,0:T(8,128)(2,1)} %get-tuple-element.41), channel_id=1, source_target_pairs={{0,16},{16,32},{32,48},{48,0},{1,17},{17,33},{33,49},{49,1},{2,18}... | collective-permute-start | bytes 393224 | tf_op jit(solution)/shard_map/ppermute | solution.py:416
  81.5 8.4 %collective-permute-start.12 = (bf16[64,1024]{1,0:T(8,128)(2,1)}, bf16[64,1024]{1,0:T(8,128)(2,1)}, u32[]{:S(2)}, u32[]{:S(2)}) collective-permute-start(bf16[64,1024]{1,0:T(8,128)(2,1)} %get-tuple-element.42), channel_id=1, source_target_pairs={{0,32},{16,48},{32,0},{48,16},{1,33},{17,49},{33,1},{49,17},{2,34}... | collective-permute-start | bytes 393224 | tf_op jit(solution)/shard_map/ppermute | solution.py:416
  83.2 6.7 %collective-permute-start.13 = (bf16[64,1024]{1,0:T(8,128)(2,1)}, bf16[64,1024]{1,0:T(8,128)(2,1)}, u32[]{:S(2)}, u32[]{:S(2)}) collective-permute-start(bf16[64,1024]{1,0:T(8,128)(2,1)} %get-tuple-element.43), channel_id=1, source_target_pairs={{0,48},{16,0},{32,16},{48,32},{1,49},{17,1},{33,17},{49,33},{2,50}... | collective-permute-start | bytes 393224 | tf_op jit(solution)/shard_map/ppermute | solution.py:416
  86.3 10.3 %all-to-all-start.2 = ((f32[8,24,256]{2,1,0:T(8,128)}), f32[8,24,256]{2,1,0:T(8,128)S(1)}, u32[]{:S(2)}, u32[]{:S(2)}) async-start(f32[8,24,256]{2,1,0:T(8,128)} %shard_map.79), calls=%async_computation.2 | async-start | bytes 393216 | tf_op jit(solution)/shard_map/all_to_all | solution.py:423
  91.8 15.2 %collective-permute-start.14 = (bf16[128,1024]{1,0:T(8,128)(2,1)}, bf16[128,1024]{1,0:T(8,128)(2,1)}, u32[]{:S(2)}, u32[]{:S(2)}) collective-permute-start(bf16[128,1024]{1,0:T(8,128)(2,1)} %get-tuple-element.44.g0), channel_id=1, source_target_pairs={{0,8},{8,0},{64,72},{72,64},{1,9},{9,1},{65,73},{73,65},{2,10},{10... | collective-permute-start | bytes 786440 | tf_op jit(solution)/shard_map/ppermute | solution.py:419
  93.6 20.7 %copy-start.10 = (s32[256]{0:T(256)S(1)}, s32[256]{0:T(256)}, u32[]{:S(2)}) copy-start(s32[256]{0:T(256)} %param.7) | copy-start | bytes 3076
  93.6 14.8 %collective-permute-start.15 = (bf16[128,1024]{1,0:T(8,128)(2,1)}, bf16[128,1024]{1,0:T(8,128)(2,1)}, u32[]{:S(2)}, u32[]{:S(2)}) collective-permute-start(bf16[128,1024]{1,0:T(8,128)(2,1)} %get-tuple-element.45), channel_id=1, source_target_pairs={{0,64},{8,72},{64,0},{72,8},{1,65},{9,73},{65,1},{73,9},{2,66},{10... | collective-permute-start | bytes 786440 | tf_op jit(solution)/shard_map/ppermute | solution.py:419
  96.3 13.8 %collective-permute-start.16 = (bf16[128,1024]{1,0:T(8,128)(2,1)}, bf16[128,1024]{1,0:T(8,128)(2,1)}, u32[]{:S(2)}, u32[]{:S(2)}) collective-permute-start(bf16[128,1024]{1,0:T(8,128)(2,1)} %get-tuple-element.45), channel_id=1, source_target_pairs={{0,72},{8,64},{64,8},{72,0},{1,73},{9,65},{65,9},{73,1},{2,74},{10... | collective-permute-start | bytes 786440 | tf_op jit(solution)/shard_map/ppermute | solution.py:419
  98.4 1.4 %collective-permute-start.17 = (f32[256,128]{1,0:T(8,128)S(1)}, f32[256,128]{1,0:T(8,128)S(1)}, u32[]{:S(2)}, u32[]{:S(2)}) collective-permute-start(f32[256,128]{1,0:T(8,128)S(1)} %get-tuple-element.54), channel_id=1, source_target_pairs={{0,1},{1,0},{2,3},{3,2},{4,5},{5,4},{6,7},{7,6},{8,9},{9,8},{10,11... | collective-permute-start | bytes 393224 | tf_op jit(solution)/shard_map/ppermute | solution.py:425
  100.7 13.5 %all-to-all-start.3 = ((f32[16,2,256]{2,1,0:T(2,128)}), f32[16,2,256]{2,1,0:T(2,128)S(1)}, u32[]{:S(2)}, u32[]{:S(2)}) async-start(f32[16,2,256]{2,1,0:T(2,128)} %shard_map.81), calls=%async_computation.3 | async-start | bytes 65536 | tf_op jit(solution)/shard_map/all_to_all | solution.py:374
  (8 other events, 34.1 us)

commit v4 on v3

--- a/solution.py
+++ b/solution.py
@@ -21,7 +21,7 @@
 RIGHT = [(i, (i + 1) % 4) for i in range(4)]
 LEFT = [(i, (i + 3) % 4) for i in range(4)]
 SWAP = [(0, 1), (1, 0)]
-PLACES = [(0, 0), (0, 3), (0, 1), (1, 0), (0, 2), (1, 3), (1, 1), (1, 2)]
+PLACES = [(0, 0), (0, 3), (0, 1), (1, 0), (0, 2), (1, 2), (1, 3), (1, 1)]
 
 
 def params():
@@ -146,7 +146,7 @@
             value = jnp.dot(weight_bf[pl.ds(ROWS * m, ROWS)], block, preferred_element_type=F32)
             if carry:
                 value = value + (own_in, sib_in)[m][:, cols]
-            out[:, cols] = value
+            out[:, cols] = value.astype(out.dtype)
 
 
 def score(own, sib, arrays, pieces, carry, last):
@@ -159,7 +159,7 @@
             jax.ShapeDtypeStruct((blocks, ROWS), F32),
             jax.ShapeDtypeStruct((blocks, ROWS), F32),
             jax.ShapeDtypeStruct((ROWS, WIDTH), F32),
-            jax.ShapeDtypeStruct((ROWS, WIDTH), F32),
+            jax.ShapeDtypeStruct((ROWS, WIDTH), BF16 if last else F32),
         )
         + (jax.ShapeDtypeStruct((2 * ROWS, 128), F32),) * row_sums,
         in_specs=[vm()] * (2 + len(arrays) + len(carry)),
@@ -246,7 +246,7 @@
 def home_kernel(mine, other, partner, partner_in, *refs):
     outs, rows = refs[:4], refs[4]
     denom = mine[:ROWS, 0:1] + other[ROWS:, 0:1]
-    rows[...] = ((partner[...] + partner_in[...]) / denom).astype(BF16)
+    rows[...] = ((partner[...] + partner_in[...].astype(F32)) / denom).astype(BF16)
     zh, y = lax.axis_index("zh"), lax.axis_index("y")
     for d in range(4):
         for u in range(2):
@@ -335,9 +335,8 @@
     return pl.pallas_call(
         unpack_kernel,
         out_shape=(jax.ShapeDtypeStruct((ROWS, WIDTH), F32), jax.ShapeDtypeStruct((8, 128), F32)),
-        grid=(4,),
-        in_specs=[pl.BlockSpec((ROWS, PACK), lambda g: (0, 0))] + [pl.BlockSpec((128, 256), lambda g: (0, g))] * 4,
-        out_specs=(pl.BlockSpec((ROWS, 256), lambda g: (0, g)), pl.BlockSpec((8, 128), lambda g: (0, 0))),
+        in_specs=[vm()] * 5,
+        out_specs=(vm(), vm()),
         compiler_params=params(),
         cost_estimate=pl.CostEstimate(flops=2 * PACK * ROWS * WIDTH, bytes_accessed=2**21, transcendentals=0),
     )(place, *got)
@@ -399,7 +398,7 @@
             ((0, 0), (0, 1), (1, 0), (1, 1), (2, 0), (2, 1), (3, 0), (3, 1), (4, 0), (4, 1)),
         ),
         (
-            (across_left, across_right, last),
+            (last, across_left, across_right),
             ((0, 0), (0, 1), (1, 0), (1, 1), (2, 0), (2, 1)),
         ),
     )

time: 116 us -> 115 us (level)
    pallas_call x1, Pallas kernels: 3.77 us -> 2.61 us  [unpack(): pl.pallas_call(unpack_kernel, out_shape=(jax.ShapeDtypeStruct((ROWS, WIDT...]
    all_to_all x2, waiting for transfers between devices: 0.39 us -> 1.55 us  [route(): return lax.all_to_all(packed, ROUTE, 0, 0, tiled=True)]
  transfers between devices with their start and end apart: 21 -> 21, of which waited for: 11 -> 11; matrix products, arithmetic and copies ran while one was open for 0% -> 0% of each run, Pallas kernels for 11% -> 10%
where the time goes in v4:
time: 115 us; the launch traced here: 114 us
  starting transfers between devices  36.7 us (32%)
  waiting for transfers between devices  30.3 us (26%)
  blocking collectives  25 us (22%)
  Pallas kernels  17.7 us (15%)
  local copies, waits for them, and re-layouts  3.94 us (3%)
    all_to_all x1, blocking collectives, route(): return lax.all_to_all(packed, ROUTE, 0, 0, tiled=True)  25 us
    all_to_all x2, starting transfers between devices, route(): return lax.all_to_all(packed, ROUTE, 0, 0, tiled=True)  9.57 us
    ppermute x1, waiting for transfers between devices, on_device(): lax.ppermute(base, 'x', RIGHT)  8.47 us
    ppermute x1, waiting for transfers between devices, on_device(): lax.ppermute(across, 'x', RIGHT)  6.24 us
    pallas_call x2, Pallas kernels, score(): pl.pallas_call(partial(score_kernel, pieces, len(arrays), bool(carry), la...  6.18 us
    ppermute x3, starting transfers between devices, on_device(): lax.ppermute(by_y[d], 'y', shift(d))  6.18 us
    ppermute x3, starting transfers between devices, on_device(): lax.ppermute(rows, ('zh', 'zl'), [(i, i ^ z) for i in range(4)])  4.7 us
    ppermute x1, waiting for transfers between devices, on_device(): lax.ppermute(go_right, 'x', RIGHT)  4.35 us
  transfers between devices with their start and end apart: 21, of which 11 were waited for; matrix products, arithmetic and copies ran while one was open for 0% of the time, Pallas kernels for 10%

profile of v4, /device:TPU:0, one launch (start us, length us, event | category | flops | bytes accessed | tf_op | source)
XLA Modules:
  0.0 114.4 jit_solution(11940922758341990326)
XLA Ops:
  3.0 25.0 %all_to_all.20.arrived = bf16[16,32,1024]{2,1,0:T(8,128)(2,1)S(1)} all-to-all(bf16[16,32,1024]{2,1,0:T(8,128)(2,1)S(1)} %bitcast.6), channel_id=1, replica_groups=mesh['zh'=2,'y'=4,'zl'=2,'x'=4,'c'=2] {'zh','y','zl'}, dimensions={0} | all-to-all | bytes 2097152 | tf_op jit(solution)/shard_map/all_to_all | solution.py:373
  28.1 1.6 %shard_map.70 = bf16[512,1024]{1,0:T(8,128)(2,1)} custom-call(s32[1,256]{1,0:T(1,128)S(1)} %bitcast.7, bf16[256,1024]{1,0:T(8,128)(2,1)S(1)} %copy-done.7, bf16[256,1024]{1,0:T(8,128)(2,1)S(1)} %shard_map.69.refs_0_), custom_call_target="tpu_custom_call" | custom-call | flops 268435456 | bytes 1572864 | tf_op jit(solution)/shard_map/pallas_call | solution.py:66
  29.7 3.7 %all-to-all-start.1 = ((bf16[16,32,1024]{2,1,0:T(8,128)(2,1)}), bf16[16,32,1024]{2,1,0:T(8,128)(2,1)S(1)}, u32[]{:S(2)}, u32[]{:S(2)}) async-start(bf16[16,32,1024]{2,1,0:T(8,128)(2,1)} %bitcast.3), calls=%async_computation.1 | async-start | bytes 2097152 | tf_op jit(solution)/shard_map/all_to_all | solution.py:373
  35.0 1.7 %collective-permute-start.1 = (bf16[256,1024]{1,0:T(8,128)(2,1)S(1)}, bf16[256,1024]{1,0:T(8,128)(2,1)S(1)}, u32[]{:S(2)}, u32[]{:S(2)}) collective-permute-start(bf16[256,1024]{1,0:T(8,128)(2,1)S(1)} %shard_map.69.refs_0_), channel_id=1, source_target_pairs={{0,6},{2,0},{4,2},{6,4},{1,7},{3,1},{5,3},{7,5},{8,14},{10,8},{12,... | collective-permute-start | bytes 1572872 | tf_op jit(solution)/shard_map/ppermute | solution.py:385
  36.7 1.7 %collective-permute-start.6 = (bf16[256,1024]{1,0:T(8,128)(2,1)S(1)}, bf16[256,1024]{1,0:T(8,128)(2,1)}, u32[]{:S(2)}, u32[]{:S(2)}) collective-permute-start(bf16[256,1024]{1,0:T(8,128)(2,1)S(1)} %shard_map.69.refs_0_), channel_id=1, source_target_pairs={{0,8},{8,0},{1,9},{9,1},{2,10},{10,2},{3,11},{11,3},{4,12},{12,4},... | collective-permute-start | bytes 1572872 | tf_op jit(solution)/shard_map/ppermute | solution.py:386
  38.4 8.5 %collective-permute-done.refs_0_.refs_1_ = bf16[256,1024]{1,0:T(8,128)(2,1)S(1)} collective-permute-done((bf16[256,1024]{1,0:T(8,128)(2,1)S(1)}, bf16[256,1024]{1,0:T(8,128)(2,1)S(1)}, u32[]{:S(2)}, u32[]{:S(2)}) %collective-permute-start) | collective-permute-done | bytes 524320 | tf_op jit(solution)/shard_map/ppermute | solution.py:385
  48.5 2.5 %collective-permute-start.3 = (bf16[128,1024]{1,0:T(8,128)(2,1)S(1)}, bf16[128,1024]{1,0:T(8,128)(2,1)S(1)}, u32[]{:S(2)}, u32[]{:S(2)}) collective-permute-start(bf16[128,1024]{1,0:T(8,128)(2,1)S(1)} %get-tuple-element.32), channel_id=1, source_target_pairs={{0,6},{2,0},{4,2},{6,4},{1,7},{3,1},{5,3},{7,5},{8,14},{10,8},{12,... | collective-permute-start | bytes 786440 | tf_op jit(solution)/shard_map/ppermute | solution.py:388
  51.0 4.3 %collective-permute-done.2.refs_0_ = bf16[128,1024]{1,0:T(8,128)(2,1)S(1)} collective-permute-done((bf16[128,1024]{1,0:T(8,128)(2,1)S(1)}, bf16[128,1024]{1,0:T(8,128)(2,1)S(1)}, u32[]{:S(2)}, u32[]{:S(2)}) %collective-permute-start.2) | collective-permute-done | bytes 262176 | tf_op jit(solution)/shard_map/ppermute | solution.py:388
  55.5 1.9 %collective-permute-done.6.refs_3_ = bf16[256,1024]{1,0:T(8,128)(2,1)} collective-permute-done((bf16[256,1024]{1,0:T(8,128)(2,1)S(1)}, bf16[256,1024]{1,0:T(8,128)(2,1)}, u32[]{:S(2)}, u32[]{:S(2)}) %collective-permute-start.6) | collective-permute-done | bytes 524320 | tf_op jit(solution)/shard_map/ppermute | solution.py:386
  58.6 2.0 %collective-permute-start.8 = (bf16[256,1024]{1,0:T(8,128)(2,1)}, bf16[256,1024]{1,0:T(8,128)(2,1)S(1)}, u32[]{:S(2)}, u32[]{:S(2)}) collective-permute-start(bf16[256,1024]{1,0:T(8,128)(2,1)} %collective-permute-done.6.refs_3_), channel_id=1, source_target_pairs={{0,6},{2,0},{4,2},{6,4},{1,7},{3,1},{5,3},{7,5},{8,14},{10,8},{12,... | collective-permute-start | bytes 1572872 | tf_op jit(solution)/shard_map/ppermute | solution.py:389
  61.1 4.2 %shard_map.74 = (f32[5,512,256]{2,1,0:T(8,128)S(1)}, f32[5,256]{1,0:T(8,128)S(1)}, f32[5,256]{1,0:T(8,128)S(1)}, f32[256,1024]{1,0:T(8,128)S(1)}, f32[256,1024]{...) custom-call(bf16[256,1024]{1,0:T(8,128)(2,1)S(1)} %shard_map.72.own, ...), custom_call_target="tpu_custom_call" | custom-call | flops 2684354560 | bytes 9437184 | tf_op jit(solution)/shard_map/pallas_call | solution.py:155
  65.3 6.2 %collective-permute-done.7.refs_1_ = bf16[256,1024]{1,0:T(8,128)(2,1)S(1)} collective-permute-done((bf16[256,1024]{1,0:T(8,128)(2,1)}, bf16[256,1024]{1,0:T(8,128)(2,1)S(1)}, u32[]{:S(2)}, u32[]{:S(2)}) %collective-permute-start.7) | collective-permute-done | bytes 524320 | tf_op jit(solution)/shard_map/ppermute | solution.py:389
  72.9 2.0 %shard_map.75 = (f32[3,512,256]{2,1,0:T(8,128)S(1)}, f32[3,256]{1,0:T(4,128)S(1)}, f32[3,256]{1,0:T(4,128)S(1)}, f32[256,1024]{1,0:T(8,128)S(1)}, bf16[256,1024]{1,0:T(8,128)(2,1)S(1)}, /*index=5*/f32[512,128]{1,0:T(8,128)S(1)}) custom-call(bf16[256,1024]{1,0:T(8,128)(2,1)S(1)} %shard_map.72.own, bf16[256,1024]{1,0:T(8,128)(2,1)S(1)} %collective-permute-done.4.sib, ...), custom_call_target="tpu_custom_call" | custom-call | flops 1610612736 | bytes 7340032 | tf_op jit(solution)/shard_map/pallas_call | solution.py:155
  75.5 1.8 %collective-permute-done.9.other = f32[512,128]{1,0:T(8,128)S(1)} collective-permute-done((f32[512,128]{1,0:T(8,128)S(1)}, f32[512,128]{1,0:T(8,128)S(1)}, u32[]{:S(2)}, u32[]{:S(2)}) %collective-permute-start.9) | collective-permute-done | bytes 262176 | tf_op jit(solution)/shard_map/ppermute | solution.py:411
  78.2 2.5 %collective-permute-start.11 = (bf16[64,1024]{1,0:T(8,128)(2,1)}, bf16[64,1024]{1,0:T(8,128)(2,1)}, u32[]{:S(2)}, u32[]{:S(2)}) collective-permute-start(bf16[64,1024]{1,0:T(8,128)(2,1)} %get-tuple-element.41), channel_id=1, source_target_pairs={{0,16},{16,32},{32,48},{48,0},{1,17},{17,33},{33,49},{49,1},{2,18}... | collective-permute-start | bytes 393224 | tf_op jit(solution)/shard_map/ppermute | solution.py:415
  80.7 1.7 %collective-permute-start.12 = (bf16[64,1024]{1,0:T(8,128)(2,1)}, bf16[64,1024]{1,0:T(8,128)(2,1)}, u32[]{:S(2)}, u32[]{:S(2)}) collective-permute-start(bf16[64,1024]{1,0:T(8,128)(2,1)} %get-tuple-element.42), channel_id=1, source_target_pairs={{0,32},{16,48},{32,0},{48,16},{1,33},{17,49},{33,1},{49,17},{2,34}... | collective-permute-start | bytes 393224 | tf_op jit(solution)/shard_map/ppermute | solution.py:415
  82.4 2.0 %collective-permute-start.13 = (bf16[64,1024]{1,0:T(8,128)(2,1)}, bf16[64,1024]{1,0:T(8,128)(2,1)}, u32[]{:S(2)}, u32[]{:S(2)}) collective-permute-start(bf16[64,1024]{1,0:T(8,128)(2,1)} %get-tuple-element.43), channel_id=1, source_target_pairs={{0,48},{16,0},{32,16},{48,32},{1,49},{17,1},{33,17},{49,33},{2,50}... | collective-permute-start | bytes 393224 | tf_op jit(solution)/shard_map/ppermute | solution.py:415
  85.5 3.6 %all-to-all-start.2 = ((f32[8,24,256]{2,1,0:T(8,128)}), f32[8,24,256]{2,1,0:T(8,128)S(1)}, u32[]{:S(2)}, u32[]{:S(2)}) async-start(f32[8,24,256]{2,1,0:T(8,128)} %shard_map.79), calls=%async_computation.2 | async-start | bytes 393216 | tf_op jit(solution)/shard_map/all_to_all | solution.py:422
  89.2 1.8 %shard_map.77 = (bf16[128,1024]{1,0:T(8,128)(2,1)}, bf16[128,1024]{1,0:T(8,128)(2,1)}) custom-call(bf16[64,1024]{1,0:T(8,128)(2,1)S(1)} %get-tuple-element.40.r0.after, bf16[64,1024]{1,0:T(8,128)(2,1)} %collective-permute-done.11.r1, bf16[64,1024]{1,0:T(8,128)(2,1)} %collective-permute-done.12.r2, bf16[64,1024]{1,0:T(8,128)(2,1)} %collective-permute-done.13.r3), custom_call_target="tpu_custom_call" | custom-call | bytes 1048576 | tf_op jit(solution)/shard_map/pallas_call | solution.py:276
  91.0 1.8 %collective-permute-start.14 = (bf16[128,1024]{1,0:T(8,128)(2,1)}, bf16[128,1024]{1,0:T(8,128)(2,1)}, u32[]{:S(2)}, u32[]{:S(2)}) collective-permute-start(bf16[128,1024]{1,0:T(8,128)(2,1)} %get-tuple-element.44.g0), channel_id=1, source_target_pairs={{0,8},{8,0},{64,72},{72,64},{1,9},{9,1},{65,73},{73,65},{2,10},{10... | collective-permute-start | bytes 786440 | tf_op jit(solution)/shard_map/ppermute | solution.py:418
  92.8 2.7 %collective-permute-start.15 = (bf16[128,1024]{1,0:T(8,128)(2,1)}, bf16[128,1024]{1,0:T(8,128)(2,1)}, u32[]{:S(2)}, u32[]{:S(2)}) collective-permute-start(bf16[128,1024]{1,0:T(8,128)(2,1)} %get-tuple-element.45), channel_id=1, source_target_pairs={{0,64},{8,72},{64,0},{72,8},{1,65},{9,73},{65,1},{73,9},{2,66},{10... | collective-permute-start | bytes 786440 | tf_op jit(solution)/shard_map/ppermute | solution.py:418
  99.9 5.9 %all-to-all-start.3 = ((f32[16,2,256]{2,1,0:T(2,128)}), f32[16,2,256]{2,1,0:T(2,128)S(1)}, u32[]{:S(2)}, u32[]{:S(2)}) async-start(f32[16,2,256]{2,1,0:T(2,128)} %shard_map.81), calls=%async_computation.3 | async-start | bytes 65536 | tf_op jit(solution)/shard_map/all_to_all | solution.py:373
  107.6 1.7 %collective-permute-done.16.g3 = bf16[128,1024]{1,0:T(8,128)(2,1)} collective-permute-done((bf16[128,1024]{1,0:T(8,128)(2,1)}, bf16[128,1024]{1,0:T(8,128)(2,1)}, u32[]{:S(2)}, u32[]{:S(2)}) %collective-permute-start.16) | collective-permute-done | bytes 262176 | tf_op jit(solution)/shard_map/ppermute | solution.py:418
  109.3 2.6 %shard_map.78 = (f32[256,1024]{1,0:T(8,128)}, f32[8,128]{1,0:T(8,128)S(1)}) custom-call(bf16[256,512]{1,0:T(8,128)(2,1)S(1)} %shard_map.67.place, bf16[128,1024]{1,0:T(8,128)(2,1)} %get-tuple-element.44.g0, bf16[128,1024]{1,0:T(8,128)(2,1)} %collective-permute-done.14.g1, bf16[128,1024]{1,0:T(8,128)(2,1)} %collective-permute-done.15.g2, ...), custom_call_target="tpu_custom_call" | custom-call | flops 268435456 | bytes 2097152 | tf_op jit(solution)/shard_map/pallas_call | solution.py:335
  (57 shorter events, 20.1 us)
Async XLA Ops:
  2.4 25.8 %copy-start.7 = (bf16[256,1024]{1,0:T(8,128)(2,1)S(1)}, bf16[256,1024]{1,0:T(8,128)(2,1)}, u32[]{:S(2)}) copy-start(bf16[256,1024]{1,0:T(8,128)(2,1)} %rows.3) | copy-start | bytes 1572868
  2.4 25.8 %copy-start.8 = (s32[256]{0:T(256)S(1)}, s32[256]{0:T(256)}, u32[]{:S(2)}) copy-start(s32[256]{0:T(256)} %param.5) | copy-start | bytes 3076
  29.7 25.6 %all-to-all-start.1 = ((bf16[16,32,1024]{2,1,0:T(8,128)(2,1)}), bf16[16,32,1024]{2,1,0:T(8,128)(2,1)S(1)}, u32[]{:S(2)}, u32[]{:S(2)}) async-start(bf16[16,32,1024]{2,1,0:T(8,128)(2,1)} %bitcast.3), calls=%async_computation.1 | async-start | bytes 2097152 | tf_op jit(solution)/shard_map/all_to_all | solution.py:373
  33.4 13.5 %collective-permute-start = (bf16[256,1024]{1,0:T(8,128)(2,1)S(1)}, bf16[256,1024]{1,0:T(8,128)(2,1)S(1)}, u32[]{:S(2)}, u32[]{:S(2)}) collective-permute-start(bf16[256,1024]{1,0:T(8,128)(2,1)S(1)} %shard_map.69.refs_0_), channel_id=1, source_target_pairs={{0,2},{2,4},{4,6},{6,0},{1,3},{3,5},{5,7},{7,1},{8,10},{10,12},{12... | collective-permute-start | bytes 1572872 | tf_op jit(solution)/shard_map/ppermute | solution.py:385
  35.0 12.0 %collective-permute-start.1 = (bf16[256,1024]{1,0:T(8,128)(2,1)S(1)}, bf16[256,1024]{1,0:T(8,128)(2,1)S(1)}, u32[]{:S(2)}, u32[]{:S(2)}) collective-permute-start(bf16[256,1024]{1,0:T(8,128)(2,1)S(1)} %shard_map.69.refs_0_), channel_id=1, source_target_pairs={{0,6},{2,0},{4,2},{6,4},{1,7},{3,1},{5,3},{7,5},{8,14},{10,8},{12,... | collective-permute-start | bytes 1572872 | tf_op jit(solution)/shard_map/ppermute | solution.py:385
  36.7 20.7 %collective-permute-start.6 = (bf16[256,1024]{1,0:T(8,128)(2,1)S(1)}, bf16[256,1024]{1,0:T(8,128)(2,1)}, u32[]{:S(2)}, u32[]{:S(2)}) collective-permute-start(bf16[256,1024]{1,0:T(8,128)(2,1)S(1)} %shard_map.69.refs_0_), channel_id=1, source_target_pairs={{0,8},{8,0},{1,9},{9,1},{2,10},{10,2},{3,11},{11,3},{4,12},{12,4},... | collective-permute-start | bytes 1572872 | tf_op jit(solution)/shard_map/ppermute | solution.py:386
  47.8 7.6 %collective-permute-start.2 = (bf16[128,1024]{1,0:T(8,128)(2,1)S(1)}, bf16[128,1024]{1,0:T(8,128)(2,1)S(1)}, u32[]{:S(2)}, u32[]{:S(2)}) collective-permute-start(bf16[128,1024]{1,0:T(8,128)(2,1)S(1)} %get-tuple-element.31), channel_id=1, source_target_pairs={{0,2},{2,4},{4,6},{6,0},{1,3},{3,5},{5,7},{7,1},{8,10},{10,12},{12... | collective-permute-start | bytes 786440 | tf_op jit(solution)/shard_map/ppermute | solution.py:388
  48.5 6.8 %collective-permute-start.3 = (bf16[128,1024]{1,0:T(8,128)(2,1)S(1)}, bf16[128,1024]{1,0:T(8,128)(2,1)S(1)}, u32[]{:S(2)}, u32[]{:S(2)}) collective-permute-start(bf16[128,1024]{1,0:T(8,128)(2,1)S(1)} %get-tuple-element.32), channel_id=1, source_target_pairs={{0,6},{2,0},{4,2},{6,4},{1,7},{3,1},{5,3},{7,5},{8,14},{10,8},{12,... | collective-permute-start | bytes 786440 | tf_op jit(solution)/shard_map/ppermute | solution.py:388
  55.4 5.7 %collective-permute-start.4 = (bf16[256,1024]{1,0:T(8,128)(2,1)S(1)}, bf16[256,1024]{1,0:T(8,128)(2,1)S(1)}, u32[]{:S(2)}, u32[]{:S(2)}) collective-permute-start(bf16[256,1024]{1,0:T(8,128)(2,1)S(1)} %shard_map.72.own), channel_id=1, source_target_pairs={{0,1},{1,0},{2,3},{3,2},{4,5},{5,4},{6,7},{7,6},{8,9},{9,8},{10,11... | collective-permute-start | bytes 1572872 | tf_op jit(solution)/shard_map/ppermute | solution.py:394
  57.4 14.1 %collective-permute-start.7 = (bf16[256,1024]{1,0:T(8,128)(2,1)}, bf16[256,1024]{1,0:T(8,128)(2,1)S(1)}, u32[]{:S(2)}, u32[]{:S(2)}) collective-permute-start(bf16[256,1024]{1,0:T(8,128)(2,1)} %collective-permute-done.6.refs_3_), channel_id=1, source_target_pairs={{0,2},{2,4},{4,6},{6,0},{1,3},{3,5},{5,7},{7,1},{8,10},{10,12},{12... | collective-permute-start | bytes 1572872 | tf_op jit(solution)/shard_map/ppermute | solution.py:389
  58.6 12.9 %collective-permute-start.8 = (bf16[256,1024]{1,0:T(8,128)(2,1)}, bf16[256,1024]{1,0:T(8,128)(2,1)S(1)}, u32[]{:S(2)}, u32[]{:S(2)}) collective-permute-start(bf16[256,1024]{1,0:T(8,128)(2,1)} %collective-permute-done.6.refs_3_), channel_id=1, source_target_pairs={{0,6},{2,0},{4,2},{6,4},{1,7},{3,1},{5,3},{7,5},{8,14},{10,8},{12,... | collective-permute-start | bytes 1572872 | tf_op jit(solution)/shard_map/ppermute | solution.py:389
  60.7 12.2 %collective-permute-start.5 = (bf16[256,1024]{1,0:T(8,128)(2,1)S(1)}, bf16[256,1024]{1,0:T(8,128)(2,1)S(1)}, u32[]{:S(2)}, u32[]{:S(2)}) collective-permute-start(bf16[256,1024]{1,0:T(8,128)(2,1)S(1)} %shard_map.73.refs_4_), channel_id=1, source_target_pairs={{0,8},{8,0},{1,9},{9,1},{2,10},{10,2},{3,11},{11,3},{4,12},{12,4},... | collective-permute-start | bytes 1572872 | tf_op jit(solution)/shard_map/ppermute | solution.py:391
  74.9 2.4 %collective-permute-start.10 = (bf16[256,1024]{1,0:T(8,128)(2,1)S(1)}, bf16[256,1024]{1,0:T(8,128)(2,1)S(1)}, u32[]{:S(2)}, u32[]{:S(2)}) collective-permute-start(bf16[256,1024]{1,0:T(8,128)(2,1)S(1)} %get-tuple-element.39), channel_id=1, source_target_pairs={{0,1},{1,0},{2,3},{3,2},{4,5},{5,4},{6,7},{7,6},{8,9},{9,8},{10,11... | collective-permute-start | bytes 1572872 | tf_op jit(solution)/shard_map/ppermute | solution.py:412
  75.0 2.3 %collective-permute-start.9 = (f32[512,128]{1,0:T(8,128)S(1)}, f32[512,128]{1,0:T(8,128)S(1)}, u32[]{:S(2)}, u32[]{:S(2)}) collective-permute-start(f32[512,128]{1,0:T(8,128)S(1)} %get-tuple-element.37.mine), channel_id=1, source_target_pairs={{0,1},{1,0},{2,3},{3,2},{4,5},{5,4},{6,7},{7,6},{8,9},{9,8},{10,11... | collective-permute-start | bytes 786440 | tf_op jit(solution)/shard_map/ppermute | solution.py:411
  78.2 10.9 %collective-permute-start.11 = (bf16[64,1024]{1,0:T(8,128)(2,1)}, bf16[64,1024]{1,0:T(8,128)(2,1)}, u32[]{:S(2)}, u32[]{:S(2)}) collective-permute-start(bf16[64,1024]{1,0:T(8,128)(2,1)} %get-tuple-element.41), channel_id=1, source_target_pairs={{0,16},{16,32},{32,48},{48,0},{1,17},{17,33},{33,49},{49,1},{2,18}... | collective-permute-start | bytes 393224 | tf_op jit(solution)/shard_map/ppermute | solution.py:415
  80.7 8.4 %collective-permute-start.12 = (bf16[64,1024]{1,0:T(8,128)(2,1)}, bf16[64,1024]{1,0:T(8,128)(2,1)}, u32[]{:S(2)}, u32[]{:S(2)}) collective-permute-start(bf16[64,1024]{1,0:T(8,128)(2,1)} %get-tuple-element.42), channel_id=1, source_target_pairs={{0,32},{16,48},{32,0},{48,16},{1,33},{17,49},{33,1},{49,17},{2,34}... | collective-permute-start | bytes 393224 | tf_op jit(solution)/shard_map/ppermute | solution.py:415
  82.4 6.7 %collective-permute-start.13 = (bf16[64,1024]{1,0:T(8,128)(2,1)}, bf16[64,1024]{1,0:T(8,128)(2,1)}, u32[]{:S(2)}, u32[]{:S(2)}) collective-permute-start(bf16[64,1024]{1,0:T(8,128)(2,1)} %get-tuple-element.43), channel_id=1, source_target_pairs={{0,48},{16,0},{32,16},{48,32},{1,49},{17,1},{33,17},{49,33},{2,50}... | collective-permute-start | bytes 393224 | tf_op jit(solution)/shard_map/ppermute | solution.py:415
  85.5 10.3 %all-to-all-start.2 = ((f32[8,24,256]{2,1,0:T(8,128)}), f32[8,24,256]{2,1,0:T(8,128)S(1)}, u32[]{:S(2)}, u32[]{:S(2)}) async-start(f32[8,24,256]{2,1,0:T(8,128)} %shard_map.79), calls=%async_computation.2 | async-start | bytes 393216 | tf_op jit(solution)/shard_map/all_to_all | solution.py:422
  91.0 15.2 %collective-permute-start.14 = (bf16[128,1024]{1,0:T(8,128)(2,1)}, bf16[128,1024]{1,0:T(8,128)(2,1)}, u32[]{:S(2)}, u32[]{:S(2)}) collective-permute-start(bf16[128,1024]{1,0:T(8,128)(2,1)} %get-tuple-element.44.g0), channel_id=1, source_target_pairs={{0,8},{8,0},{64,72},{72,64},{1,9},{9,1},{65,73},{73,65},{2,10},{10... | collective-permute-start | bytes 786440 | tf_op jit(solution)/shard_map/ppermute | solution.py:418
  92.8 20.7 %copy-start.10 = (s32[256]{0:T(256)S(1)}, s32[256]{0:T(256)}, u32[]{:S(2)}) copy-start(s32[256]{0:T(256)} %param.7) | copy-start | bytes 3076
  92.8 14.9 %collective-permute-start.15 = (bf16[128,1024]{1,0:T(8,128)(2,1)}, bf16[128,1024]{1,0:T(8,128)(2,1)}, u32[]{:S(2)}, u32[]{:S(2)}) collective-permute-start(bf16[128,1024]{1,0:T(8,128)(2,1)} %get-tuple-element.45), channel_id=1, source_target_pairs={{0,64},{8,72},{64,0},{72,8},{1,65},{9,73},{65,1},{73,9},{2,66},{10... | collective-permute-start | bytes 786440 | tf_op jit(solution)/shard_map/ppermute | solution.py:418
  95.5 13.8 %collective-permute-start.16 = (bf16[128,1024]{1,0:T(8,128)(2,1)}, bf16[128,1024]{1,0:T(8,128)(2,1)}, u32[]{:S(2)}, u32[]{:S(2)}) collective-permute-start(bf16[128,1024]{1,0:T(8,128)(2,1)} %get-tuple-element.45), channel_id=1, source_target_pairs={{0,72},{8,64},{64,8},{72,0},{1,73},{9,65},{65,9},{73,1},{2,74},{10... | collective-permute-start | bytes 786440 | tf_op jit(solution)/shard_map/ppermute | solution.py:418
  97.7 1.4 %collective-permute-start.17 = (f32[256,128]{1,0:T(8,128)S(1)}, f32[256,128]{1,0:T(8,128)S(1)}, u32[]{:S(2)}, u32[]{:S(2)}) collective-permute-start(f32[256,128]{1,0:T(8,128)S(1)} %get-tuple-element.54), channel_id=1, source_target_pairs={{0,1},{1,0},{2,3},{3,2},{4,5},{5,4},{6,7},{7,6},{8,9},{9,8},{10,11... | collective-permute-start | bytes 393224 | tf_op jit(solution)/shard_map/ppermute | solution.py:424
  99.9 13.5 %all-to-all-start.3 = ((f32[16,2,256]{2,1,0:T(2,128)}), f32[16,2,256]{2,1,0:T(2,128)S(1)}, u32[]{:S(2)}, u32[]{:S(2)}) async-start(f32[16,2,256]{2,1,0:T(2,128)} %shard_map.81), calls=%async_computation.3 | async-start | bytes 65536 | tf_op jit(solution)/shard_map/all_to_all | solution.py:373
  (8 other events, 33.4 us)

commit v5 on v4

--- a/solution.py
+++ b/solution.py
@@ -266,21 +266,22 @@
     )(mine, other, partner, partner_in)
 
 
-def turn_kernel(r0, r1, r2, r3, *outs):
+def turn_kernel(r0, r1, r2, r3, after, *outs):
+    del after
     for u, out in enumerate(outs):
         for d, r in enumerate((r0, r1, r2, r3)):
             out[pl.ds(32 * d, 32)] = r[pl.ds(32 * u, 32)]
 
 
-def turn(rows):
+def turn(rows, after):
     return pl.pallas_call(
         turn_kernel,
         out_shape=(jax.ShapeDtypeStruct((128, WIDTH), BF16),) * 2,
-        in_specs=[vm()] * 4,
+        in_specs=[vm()] * 4 + [hbm()],
         out_specs=(vm(),) * 2,
         compiler_params=params(),
         cost_estimate=pl.CostEstimate(flops=0, bytes_accessed=2**20, transcendentals=0),
-    )(*rows)
+    )(*rows, after)
 
 
 def margin_kernel(mine, other, back_own, back_in, target, out):
@@ -413,14 +414,14 @@
 
     by_y = home(fwd, fwd_in, own, partner_in)
     by_y = (by_y[0],) + tuple(lax.ppermute(by_y[d], "y", shift(d)) for d in (1, 2, 3))
-    same, flip = turn(by_y)
+    heard = lax.all_to_all(fore(fwd, fwd_in, by_y[0], parts), PLANE, 0, 0, tiled=True)
+    back_own, back_sib, tgt_margin = back(heard, [part[0] for part in parts])
+    same, flip = turn(by_y, tgt_margin)
     got = [same] + [
         lax.ppermute(rows, ("zh", "zl"), [(i, i ^ z) for i in range(4)]) for z, rows in ((1, same), (2, flip), (3, flip))
     ]
     partner_out, token = unpack(place, got)
 
-    heard = lax.all_to_all(fore(fwd, fwd_in, by_y[0], parts), PLANE, 0, 0, tiled=True)
-    back_own, back_sib, tgt_margin = back(heard, [part[0] for part in parts])
     back_in = lax.ppermute(back_sib, "c", SWAP)
     both = route(margins(fwd, fwd_in, back_own, back_in, tgt_margin))
     src_margin, tgt_margin = finish(src_labels, tgt_labels, both, token)

time: 115 us -> 119 us (1.035)
  waiting for transfers between devices: 30.3 us -> 34.1 us
  Pallas kernels: 17.7 us -> 15.3 us
  local copies, waits for them, and re-layouts: 3.94 us -> 5.86 us
    unnamed x22 -> x28, local copies, waits for them, and re-layouts: 3.94 us -> 5.86 us
    ppermute x3, waiting for transfers between devices: 0.01 us -> 1.74 us  [on_device(): lax.ppermute(by_y[d], 'y', shift(d))]
    pallas_call x1, Pallas kernels: 2.61 us -> 1.41 us  [unpack(): pl.pallas_call(unpack_kernel, out_shape=(jax.ShapeDtypeStruct((ROWS, WIDT...]
  transfers between devices with their start and end apart: 21 -> 21, of which waited for: 11 -> 12; matrix products, arithmetic and copies ran while one was open for 0% -> 0% of each run, Pallas kernels for 10% -> 6%
where the time goes in v5:
time: 119 us
  starting transfers between devices  37.5 us (32%)
  waiting for transfers between devices  34.1 us (29%)
  blocking collectives  25 us (21%)
  Pallas kernels  15.3 us (13%)
  local copies, waits for them, and re-layouts  5.86 us (5%)
    all_to_all x1, blocking collectives, route(): return lax.all_to_all(packed, ROUTE, 0, 0, tiled=True)  25 us
    all_to_all x2, starting transfers between devices, route(): return lax.all_to_all(packed, ROUTE, 0, 0, tiled=True)  10.4 us
    ppermute x1, waiting for transfers between devices, on_device(): lax.ppermute(base, 'x', RIGHT)  8.47 us
    pallas_call x2, Pallas kernels, score(): pl.pallas_call(partial(score_kernel, pieces, len(arrays), bool(carry), la...  6.47 us
    ppermute x1, waiting for transfers between devices, on_device(): lax.ppermute(across, 'x', RIGHT)  6.08 us
    unnamed x28, local copies, waits for them, and re-layouts  5.86 us
    ppermute x3, starting transfers between devices, on_device(): lax.ppermute(by_y[d], 'y', shift(d))  5.74 us
    ppermute x3, starting transfers between devices, on_device(): lax.ppermute(rows, ('zh', 'zl'), [(i, i ^ z) for i in range(4)])  4.78 us
  transfers between devices with their start and end apart: 21, of which 12 were waited for; matrix products, arithmetic and copies ran while one was open for 0% of the time, Pallas kernels for 6%

profile of v5, /device:TPU:0, one launch (start us, length us, event | category | flops | bytes accessed | tf_op | source)
XLA Modules:
  0.0 118.6 jit_solution(3555130443532674211)
XLA Ops:
  3.0 25.0 %all_to_all.20.arrived = bf16[16,32,1024]{2,1,0:T(8,128)(2,1)S(1)} all-to-all(bf16[16,32,1024]{2,1,0:T(8,128)(2,1)S(1)} %bitcast.6), channel_id=1, replica_groups=mesh['zh'=2,'y'=4,'zl'=2,'x'=4,'c'=2] {'zh','y','zl'}, dimensions={0} | all-to-all | bytes 2097152 | tf_op jit(solution)/shard_map/all_to_all | solution.py:374
  28.1 1.6 %shard_map.70 = bf16[512,1024]{1,0:T(8,128)(2,1)} custom-call(s32[1,256]{1,0:T(1,128)S(1)} %bitcast.7, bf16[256,1024]{1,0:T(8,128)(2,1)S(1)} %copy-done.7, bf16[256,1024]{1,0:T(8,128)(2,1)S(1)} %shard_map.69.refs_0_), custom_call_target="tpu_custom_call" | custom-call | flops 268435456 | bytes 1572864 | tf_op jit(solution)/shard_map/pallas_call | solution.py:66
  29.7 3.7 %all-to-all-start.1 = ((bf16[16,32,1024]{2,1,0:T(8,128)(2,1)}), bf16[16,32,1024]{2,1,0:T(8,128)(2,1)S(1)}, u32[]{:S(2)}, u32[]{:S(2)}) async-start(bf16[16,32,1024]{2,1,0:T(8,128)(2,1)} %bitcast.3), calls=%async_computation.1 | async-start | bytes 2097152 | tf_op jit(solution)/shard_map/all_to_all | solution.py:374
  35.0 1.7 %collective-permute-start.1 = (bf16[256,1024]{1,0:T(8,128)(2,1)S(1)}, bf16[256,1024]{1,0:T(8,128)(2,1)S(1)}, u32[]{:S(2)}, u32[]{:S(2)}) collective-permute-start(bf16[256,1024]{1,0:T(8,128)(2,1)S(1)} %shard_map.69.refs_0_), channel_id=1, source_target_pairs={{0,6},{2,0},{4,2},{6,4},{1,7},{3,1},{5,3},{7,5},{8,14},{10,8},{12,... | collective-permute-start | bytes 1572872 | tf_op jit(solution)/shard_map/ppermute | solution.py:386
  36.7 1.7 %collective-permute-start.6 = (bf16[256,1024]{1,0:T(8,128)(2,1)S(1)}, bf16[256,1024]{1,0:T(8,128)(2,1)}, u32[]{:S(2)}, u32[]{:S(2)}) collective-permute-start(bf16[256,1024]{1,0:T(8,128)(2,1)S(1)} %shard_map.69.refs_0_), channel_id=1, source_target_pairs={{0,8},{8,0},{1,9},{9,1},{2,10},{10,2},{3,11},{11,3},{4,12},{12,4},... | collective-permute-start | bytes 1572872 | tf_op jit(solution)/shard_map/ppermute | solution.py:387
  38.4 8.5 %collective-permute-done.refs_0_.refs_1_ = bf16[256,1024]{1,0:T(8,128)(2,1)S(1)} collective-permute-done((bf16[256,1024]{1,0:T(8,128)(2,1)S(1)}, bf16[256,1024]{1,0:T(8,128)(2,1)S(1)}, u32[]{:S(2)}, u32[]{:S(2)}) %collective-permute-start) | collective-permute-done | bytes 524320 | tf_op jit(solution)/shard_map/ppermute | solution.py:386
  48.5 2.5 %collective-permute-start.3 = (bf16[128,1024]{1,0:T(8,128)(2,1)S(1)}, bf16[128,1024]{1,0:T(8,128)(2,1)S(1)}, u32[]{:S(2)}, u32[]{:S(2)}) collective-permute-start(bf16[128,1024]{1,0:T(8,128)(2,1)S(1)} %get-tuple-element.32), channel_id=1, source_target_pairs={{0,6},{2,0},{4,2},{6,4},{1,7},{3,1},{5,3},{7,5},{8,14},{10,8},{12,... | collective-permute-start | bytes 786440 | tf_op jit(solution)/shard_map/ppermute | solution.py:389
  51.0 4.3 %collective-permute-done.2.refs_0_ = bf16[128,1024]{1,0:T(8,128)(2,1)S(1)} collective-permute-done((bf16[128,1024]{1,0:T(8,128)(2,1)S(1)}, bf16[128,1024]{1,0:T(8,128)(2,1)S(1)}, u32[]{:S(2)}, u32[]{:S(2)}) %collective-permute-start.2) | collective-permute-done | bytes 262176 | tf_op jit(solution)/shard_map/ppermute | solution.py:389
  55.5 1.9 %collective-permute-done.6.refs_3_ = bf16[256,1024]{1,0:T(8,128)(2,1)} collective-permute-done((bf16[256,1024]{1,0:T(8,128)(2,1)S(1)}, bf16[256,1024]{1,0:T(8,128)(2,1)}, u32[]{:S(2)}, u32[]{:S(2)}) %collective-permute-start.6) | collective-permute-done | bytes 524320 | tf_op jit(solution)/shard_map/ppermute | solution.py:387
  58.6 2.0 %collective-permute-start.8 = (bf16[256,1024]{1,0:T(8,128)(2,1)}, bf16[256,1024]{1,0:T(8,128)(2,1)S(1)}, u32[]{:S(2)}, u32[]{:S(2)}) collective-permute-start(bf16[256,1024]{1,0:T(8,128)(2,1)} %collective-permute-done.6.refs_3_), channel_id=1, source_target_pairs={{0,6},{2,0},{4,2},{6,4},{1,7},{3,1},{5,3},{7,5},{8,14},{10,8},{12,... | collective-permute-start | bytes 1572872 | tf_op jit(solution)/shard_map/ppermute | solution.py:390
  61.1 4.3 %shard_map.74 = (f32[5,512,256]{2,1,0:T(8,128)S(1)}, f32[5,256]{1,0:T(8,128)S(1)}, f32[5,256]{1,0:T(8,128)S(1)}, f32[256,1024]{1,0:T(8,128)S(1)}, f32[256,1024]{...) custom-call(bf16[256,1024]{1,0:T(8,128)(2,1)S(1)} %shard_map.72.own, ...), custom_call_target="tpu_custom_call" | custom-call | flops 2684354560 | bytes 9437184 | tf_op jit(solution)/shard_map/pallas_call | solution.py:155
  65.4 6.1 %collective-permute-done.7.refs_1_ = bf16[256,1024]{1,0:T(8,128)(2,1)S(1)} collective-permute-done((bf16[256,1024]{1,0:T(8,128)(2,1)}, bf16[256,1024]{1,0:T(8,128)(2,1)S(1)}, u32[]{:S(2)}, u32[]{:S(2)}) %collective-permute-start.7) | collective-permute-done | bytes 524320 | tf_op jit(solution)/shard_map/ppermute | solution.py:390
  72.9 2.1 %shard_map.75 = (f32[3,512,256]{2,1,0:T(8,128)S(1)}, f32[3,256]{1,0:T(4,128)S(1)}, f32[3,256]{1,0:T(4,128)S(1)}, f32[256,1024]{1,0:T(8,128)S(1)}, bf16[256,1024]{1,0:T(8,128)(2,1)S(1)}, /*index=5*/f32[512,128]{1,0:T(8,128)S(1)}) custom-call(bf16[256,1024]{1,0:T(8,128)(2,1)S(1)} %shard_map.72.own, bf16[256,1024]{1,0:T(8,128)(2,1)S(1)} %collective-permute-done.4.sib, ...), custom_call_target="tpu_custom_call" | custom-call | flops 1610612736 | bytes 7340032 | tf_op jit(solution)/shard_map/pallas_call | solution.py:155
  75.6 1.8 %collective-permute-done.9.other = f32[512,128]{1,0:T(8,128)S(1)} collective-permute-done((f32[512,128]{1,0:T(8,128)S(1)}, f32[512,128]{1,0:T(8,128)S(1)}, u32[]{:S(2)}, u32[]{:S(2)}) %collective-permute-start.9) | collective-permute-done | bytes 262176 | tf_op jit(solution)/shard_map/ppermute | solution.py:412
  80.7 3.9 %all-to-all-start.2 = ((f32[8,24,256]{2,1,0:T(8,128)}), f32[8,24,256]{2,1,0:T(8,128)S(1)}, u32[]{:S(2)}, u32[]{:S(2)}) async-start(f32[8,24,256]{2,1,0:T(8,128)} %shard_map.77), calls=%async_computation.2 | async-start | bytes 393216 | tf_op jit(solution)/shard_map/all_to_all | solution.py:417
  84.6 2.1 %collective-permute-start.11 = (bf16[64,1024]{1,0:T(8,128)(2,1)}, bf16[64,1024]{1,0:T(8,128)(2,1)}, u32[]{:S(2)}, u32[]{:S(2)}) collective-permute-start(bf16[64,1024]{1,0:T(8,128)(2,1)} %copy-done.13), channel_id=1, source_target_pairs={{0,16},{16,32},{32,48},{48,0},{1,17},{17,33},{33,49},{49,1},{2,18}... | collective-permute-start | bytes 393224 | tf_op jit(solution)/shard_map/ppermute | solution.py:416
  86.7 2.1 %collective-permute-start.12 = (bf16[64,1024]{1,0:T(8,128)(2,1)}, bf16[64,1024]{1,0:T(8,128)(2,1)}, u32[]{:S(2)}, u32[]{:S(2)}) collective-permute-start(bf16[64,1024]{1,0:T(8,128)(2,1)} %copy-done.12), channel_id=1, source_target_pairs={{0,32},{16,48},{32,0},{48,16},{1,33},{17,49},{33,1},{49,17},{2,34}... | collective-permute-start | bytes 393224 | tf_op jit(solution)/shard_map/ppermute | solution.py:416
  88.8 1.6 %collective-permute-start.13 = (bf16[64,1024]{1,0:T(8,128)(2,1)}, bf16[64,1024]{1,0:T(8,128)(2,1)}, u32[]{:S(2)}, u32[]{:S(2)}) collective-permute-start(bf16[64,1024]{1,0:T(8,128)(2,1)} %copy-done.11), channel_id=1, source_target_pairs={{0,48},{16,0},{32,16},{48,32},{1,49},{17,1},{33,17},{49,33},{2,50}... | collective-permute-start | bytes 393224 | tf_op jit(solution)/shard_map/ppermute | solution.py:416
  93.4 1.7 %collective-permute-done.12.r2 = bf16[64,1024]{1,0:T(8,128)(2,1)} collective-permute-done((bf16[64,1024]{1,0:T(8,128)(2,1)}, bf16[64,1024]{1,0:T(8,128)(2,1)}, u32[]{:S(2)}, u32[]{:S(2)}) %collective-permute-start.12) | collective-permute-done | bytes 131104 | tf_op jit(solution)/shard_map/ppermute | solution.py:416
  96.2 1.8 %collective-permute-start.14 = (bf16[128,1024]{1,0:T(8,128)(2,1)S(1)}, bf16[128,1024]{1,0:T(8,128)(2,1)S(1)}, u32[]{:S(2)}, u32[]{:S(2)}) collective-permute-start(bf16[128,1024]{1,0:T(8,128)(2,1)S(1)} %get-tuple-element.51.g0), channel_id=1, source_target_pairs={{0,8},{8,0},{64,72},{72,64},{1,9},{9,1},{65,73},{73,65},{2,10},{10... | collective-permute-start | bytes 786440 | tf_op jit(solution)/shard_map/ppermute | solution.py:421
  98.0 2.7 %collective-permute-start.15 = (bf16[128,1024]{1,0:T(8,128)(2,1)S(1)}, bf16[128,1024]{1,0:T(8,128)(2,1)S(1)}, u32[]{:S(2)}, u32[]{:S(2)}) collective-permute-start(bf16[128,1024]{1,0:T(8,128)(2,1)S(1)} %get-tuple-element.52), channel_id=1, source_target_pairs={{0,64},{8,72},{64,0},{72,8},{1,65},{9,73},{65,1},{73,9},{2,66},{10... | collective-permute-start | bytes 786440 | tf_op jit(solution)/shard_map/ppermute | solution.py:421
  103.2 6.8 %all-to-all-start.3 = ((f32[16,2,256]{2,1,0:T(2,128)}), f32[16,2,256]{2,1,0:T(2,128)S(1)}, u32[]{:S(2)}, u32[]{:S(2)}) async-start(f32[16,2,256]{2,1,0:T(2,128)} %shard_map.81), calls=%async_computation.3 | async-start | bytes 65536 | tf_op jit(solution)/shard_map/all_to_all | solution.py:374
  111.5 2.6 %collective-permute-done.16.g3 = bf16[128,1024]{1,0:T(8,128)(2,1)S(1)} collective-permute-done((bf16[128,1024]{1,0:T(8,128)(2,1)S(1)}, bf16[128,1024]{1,0:T(8,128)(2,1)S(1)}, u32[]{:S(2)}, u32[]{:S(2)}) %collective-permute-start.16) | collective-permute-done | bytes 262176 | tf_op jit(solution)/shard_map/ppermute | solution.py:421
  115.5 2.1 %all-to-all-done.3.got = f32[16,2,256]{2,1,0:T(2,128)S(1)} async-done(((f32[16,2,256]{2,1,0:T(2,128)}), f32[16,2,256]{2,1,0:T(2,128)S(1)}, u32[]{:S(2)}, u32[]{:S(2)}) %all-to-all-start.3) | async-done | bytes 32800 | tf_op jit(solution)/shard_map/all_to_all | solution.py:374
  (63 shorter events, 23.0 us)
Async XLA Ops:
  2.4 25.8 %copy-start.7 = (bf16[256,1024]{1,0:T(8,128)(2,1)S(1)}, bf16[256,1024]{1,0:T(8,128)(2,1)}, u32[]{:S(2)}) copy-start(bf16[256,1024]{1,0:T(8,128)(2,1)} %rows.3) | copy-start | bytes 1572868
  2.4 25.8 %copy-start.8 = (s32[256]{0:T(256)S(1)}, s32[256]{0:T(256)}, u32[]{:S(2)}) copy-start(s32[256]{0:T(256)} %param.5) | copy-start | bytes 3076
  29.7 25.6 %all-to-all-start.1 = ((bf16[16,32,1024]{2,1,0:T(8,128)(2,1)}), bf16[16,32,1024]{2,1,0:T(8,128)(2,1)S(1)}, u32[]{:S(2)}, u32[]{:S(2)}) async-start(bf16[16,32,1024]{2,1,0:T(8,128)(2,1)} %bitcast.3), calls=%async_computation.1 | async-start | bytes 2097152 | tf_op jit(solution)/shard_map/all_to_all | solution.py:374
  33.4 13.5 %collective-permute-start = (bf16[256,1024]{1,0:T(8,128)(2,1)S(1)}, bf16[256,1024]{1,0:T(8,128)(2,1)S(1)}, u32[]{:S(2)}, u32[]{:S(2)}) collective-permute-start(bf16[256,1024]{1,0:T(8,128)(2,1)S(1)} %shard_map.69.refs_0_), channel_id=1, source_target_pairs={{0,2},{2,4},{4,6},{6,0},{1,3},{3,5},{5,7},{7,1},{8,10},{10,12},{12... | collective-permute-start | bytes 1572872 | tf_op jit(solution)/shard_map/ppermute | solution.py:386
  35.0 12.0 %collective-permute-start.1 = (bf16[256,1024]{1,0:T(8,128)(2,1)S(1)}, bf16[256,1024]{1,0:T(8,128)(2,1)S(1)}, u32[]{:S(2)}, u32[]{:S(2)}) collective-permute-start(bf16[256,1024]{1,0:T(8,128)(2,1)S(1)} %shard_map.69.refs_0_), channel_id=1, source_target_pairs={{0,6},{2,0},{4,2},{6,4},{1,7},{3,1},{5,3},{7,5},{8,14},{10,8},{12,... | collective-permute-start | bytes 1572872 | tf_op jit(solution)/shard_map/ppermute | solution.py:386
  36.7 20.7 %collective-permute-start.6 = (bf16[256,1024]{1,0:T(8,128)(2,1)S(1)}, bf16[256,1024]{1,0:T(8,128)(2,1)}, u32[]{:S(2)}, u32[]{:S(2)}) collective-permute-start(bf16[256,1024]{1,0:T(8,128)(2,1)S(1)} %shard_map.69.refs_0_), channel_id=1, source_target_pairs={{0,8},{8,0},{1,9},{9,1},{2,10},{10,2},{3,11},{11,3},{4,12},{12,4},... | collective-permute-start | bytes 1572872 | tf_op jit(solution)/shard_map/ppermute | solution.py:387
  47.7 7.6 %collective-permute-start.2 = (bf16[128,1024]{1,0:T(8,128)(2,1)S(1)}, bf16[128,1024]{1,0:T(8,128)(2,1)S(1)}, u32[]{:S(2)}, u32[]{:S(2)}) collective-permute-start(bf16[128,1024]{1,0:T(8,128)(2,1)S(1)} %get-tuple-element.31), channel_id=1, source_target_pairs={{0,2},{2,4},{4,6},{6,0},{1,3},{3,5},{5,7},{7,1},{8,10},{10,12},{12... | collective-permute-start | bytes 786440 | tf_op jit(solution)/shard_map/ppermute | solution.py:389
  48.5 6.8 %collective-permute-start.3 = (bf16[128,1024]{1,0:T(8,128)(2,1)S(1)}, bf16[128,1024]{1,0:T(8,128)(2,1)S(1)}, u32[]{:S(2)}, u32[]{:S(2)}) collective-permute-start(bf16[128,1024]{1,0:T(8,128)(2,1)S(1)} %get-tuple-element.32), channel_id=1, source_target_pairs={{0,6},{2,0},{4,2},{6,4},{1,7},{3,1},{5,3},{7,5},{8,14},{10,8},{12,... | collective-permute-start | bytes 786440 | tf_op jit(solution)/shard_map/ppermute | solution.py:389
  55.4 5.7 %collective-permute-start.4 = (bf16[256,1024]{1,0:T(8,128)(2,1)S(1)}, bf16[256,1024]{1,0:T(8,128)(2,1)S(1)}, u32[]{:S(2)}, u32[]{:S(2)}) collective-permute-start(bf16[256,1024]{1,0:T(8,128)(2,1)S(1)} %shard_map.72.own), channel_id=1, source_target_pairs={{0,1},{1,0},{2,3},{3,2},{4,5},{5,4},{6,7},{7,6},{8,9},{9,8},{10,11... | collective-permute-start | bytes 1572872 | tf_op jit(solution)/shard_map/ppermute | solution.py:395
  57.4 14.1 %collective-permute-start.7 = (bf16[256,1024]{1,0:T(8,128)(2,1)}, bf16[256,1024]{1,0:T(8,128)(2,1)S(1)}, u32[]{:S(2)}, u32[]{:S(2)}) collective-permute-start(bf16[256,1024]{1,0:T(8,128)(2,1)} %collective-permute-done.6.refs_3_), channel_id=1, source_target_pairs={{0,2},{2,4},{4,6},{6,0},{1,3},{3,5},{5,7},{7,1},{8,10},{10,12},{12... | collective-permute-start | bytes 1572872 | tf_op jit(solution)/shard_map/ppermute | solution.py:390
  58.6 12.9 %collective-permute-start.8 = (bf16[256,1024]{1,0:T(8,128)(2,1)}, bf16[256,1024]{1,0:T(8,128)(2,1)S(1)}, u32[]{:S(2)}, u32[]{:S(2)}) collective-permute-start(bf16[256,1024]{1,0:T(8,128)(2,1)} %collective-permute-done.6.refs_3_), channel_id=1, source_target_pairs={{0,6},{2,0},{4,2},{6,4},{1,7},{3,1},{5,3},{7,5},{8,14},{10,8},{12,... | collective-permute-start | bytes 1572872 | tf_op jit(solution)/shard_map/ppermute | solution.py:390
  60.7 12.2 %collective-permute-start.5 = (bf16[256,1024]{1,0:T(8,128)(2,1)S(1)}, bf16[256,1024]{1,0:T(8,128)(2,1)S(1)}, u32[]{:S(2)}, u32[]{:S(2)}) collective-permute-start(bf16[256,1024]{1,0:T(8,128)(2,1)S(1)} %shard_map.73.refs_4_), channel_id=1, source_target_pairs={{0,8},{8,0},{1,9},{9,1},{2,10},{10,2},{3,11},{11,3},{4,12},{12,4},... | collective-permute-start | bytes 1572872 | tf_op jit(solution)/shard_map/ppermute | solution.py:392
  75.0 2.4 %collective-permute-start.10 = (bf16[256,1024]{1,0:T(8,128)(2,1)S(1)}, bf16[256,1024]{1,0:T(8,128)(2,1)S(1)}, u32[]{:S(2)}, u32[]{:S(2)}) collective-permute-start(bf16[256,1024]{1,0:T(8,128)(2,1)S(1)} %get-tuple-element.39), channel_id=1, source_target_pairs={{0,1},{1,0},{2,3},{3,2},{4,5},{5,4},{6,7},{7,6},{8,9},{9,8},{10,11... | collective-permute-start | bytes 1572872 | tf_op jit(solution)/shard_map/ppermute | solution.py:413
  75.1 2.3 %collective-permute-start.9 = (f32[512,128]{1,0:T(8,128)S(1)}, f32[512,128]{1,0:T(8,128)S(1)}, u32[]{:S(2)}, u32[]{:S(2)}) collective-permute-start(f32[512,128]{1,0:T(8,128)S(1)} %get-tuple-element.37.mine), channel_id=1, source_target_pairs={{0,1},{1,0},{2,3},{3,2},{4,5},{5,4},{6,7},{7,6},{8,9},{9,8},{10,11... | collective-permute-start | bytes 786440 | tf_op jit(solution)/shard_map/ppermute | solution.py:412
  80.7 10.8 %all-to-all-start.2 = ((f32[8,24,256]{2,1,0:T(8,128)}), f32[8,24,256]{2,1,0:T(8,128)S(1)}, u32[]{:S(2)}, u32[]{:S(2)}) async-start(f32[8,24,256]{2,1,0:T(8,128)} %shard_map.77), calls=%async_computation.2 | async-start | bytes 393216 | tf_op jit(solution)/shard_map/all_to_all | solution.py:417
  84.6 8.8 %collective-permute-start.11 = (bf16[64,1024]{1,0:T(8,128)(2,1)}, bf16[64,1024]{1,0:T(8,128)(2,1)}, u32[]{:S(2)}, u32[]{:S(2)}) collective-permute-start(bf16[64,1024]{1,0:T(8,128)(2,1)} %copy-done.13), channel_id=1, source_target_pairs={{0,16},{16,32},{32,48},{48,0},{1,17},{17,33},{33,49},{49,1},{2,18}... | collective-permute-start | bytes 393224 | tf_op jit(solution)/shard_map/ppermute | solution.py:416
  86.7 8.5 %collective-permute-start.12 = (bf16[64,1024]{1,0:T(8,128)(2,1)}, bf16[64,1024]{1,0:T(8,128)(2,1)}, u32[]{:S(2)}, u32[]{:S(2)}) collective-permute-start(bf16[64,1024]{1,0:T(8,128)(2,1)} %copy-done.12), channel_id=1, source_target_pairs={{0,32},{16,48},{32,0},{48,16},{1,33},{17,49},{33,1},{49,17},{2,34}... | collective-permute-start | bytes 393224 | tf_op jit(solution)/shard_map/ppermute | solution.py:416
  88.8 28.8 %copy-start.10 = (s32[256]{0:T(256)S(1)}, s32[256]{0:T(256)}, u32[]{:S(2)}) copy-start(s32[256]{0:T(256)} %param.7) | copy-start | bytes 3076
  88.8 6.4 %collective-permute-start.13 = (bf16[64,1024]{1,0:T(8,128)(2,1)}, bf16[64,1024]{1,0:T(8,128)(2,1)}, u32[]{:S(2)}, u32[]{:S(2)}) collective-permute-start(bf16[64,1024]{1,0:T(8,128)(2,1)} %copy-done.11), channel_id=1, source_target_pairs={{0,48},{16,0},{32,16},{48,32},{1,49},{17,1},{33,17},{49,33},{2,50}... | collective-permute-start | bytes 393224 | tf_op jit(solution)/shard_map/ppermute | solution.py:416
  96.2 14.1 %collective-permute-start.14 = (bf16[128,1024]{1,0:T(8,128)(2,1)S(1)}, bf16[128,1024]{1,0:T(8,128)(2,1)S(1)}, u32[]{:S(2)}, u32[]{:S(2)}) collective-permute-start(bf16[128,1024]{1,0:T(8,128)(2,1)S(1)} %get-tuple-element.51.g0), channel_id=1, source_target_pairs={{0,8},{8,0},{64,72},{72,64},{1,9},{9,1},{65,73},{73,65},{2,10},{10... | collective-permute-start | bytes 786440 | tf_op jit(solution)/shard_map/ppermute | solution.py:421
  98.0 13.4 %collective-permute-start.15 = (bf16[128,1024]{1,0:T(8,128)(2,1)S(1)}, bf16[128,1024]{1,0:T(8,128)(2,1)S(1)}, u32[]{:S(2)}, u32[]{:S(2)}) collective-permute-start(bf16[128,1024]{1,0:T(8,128)(2,1)S(1)} %get-tuple-element.52), channel_id=1, source_target_pairs={{0,64},{8,72},{64,0},{72,8},{1,65},{9,73},{65,1},{73,9},{2,66},{10... | collective-permute-start | bytes 786440 | tf_op jit(solution)/shard_map/ppermute | solution.py:421
  100.8 13.3 %collective-permute-start.16 = (bf16[128,1024]{1,0:T(8,128)(2,1)S(1)}, bf16[128,1024]{1,0:T(8,128)(2,1)S(1)}, u32[]{:S(2)}, u32[]{:S(2)}) collective-permute-start(bf16[128,1024]{1,0:T(8,128)(2,1)S(1)} %get-tuple-element.52), channel_id=1, source_target_pairs={{0,72},{8,64},{64,8},{72,0},{1,73},{9,65},{65,9},{73,1},{2,74},{10... | collective-permute-start | bytes 786440 | tf_op jit(solution)/shard_map/ppermute | solution.py:421
  101.0 1.3 %collective-permute-start.17 = (f32[256,128]{1,0:T(8,128)S(1)}, f32[256,128]{1,0:T(8,128)S(1)}, u32[]{:S(2)}, u32[]{:S(2)}) collective-permute-start(f32[256,128]{1,0:T(8,128)S(1)} %get-tuple-element.55), channel_id=1, source_target_pairs={{0,1},{1,0},{2,3},{3,2},{4,5},{5,4},{6,7},{7,6},{8,9},{9,8},{10,11... | collective-permute-start | bytes 393224 | tf_op jit(solution)/shard_map/ppermute | solution.py:425
  103.2 14.4 %all-to-all-start.3 = ((f32[16,2,256]{2,1,0:T(2,128)}), f32[16,2,256]{2,1,0:T(2,128)S(1)}, u32[]{:S(2)}, u32[]{:S(2)}) async-start(f32[16,2,256]{2,1,0:T(2,128)} %shard_map.81), calls=%async_computation.3 | async-start | bytes 65536 | tf_op jit(solution)/shard_map/all_to_all | solution.py:374
  (11 other events, 30.3 us)

commit v6 on v4

--- a/solution.py
+++ b/solution.py
@@ -201,46 +201,59 @@
     )(mine, other, after, *flat)
 
 
-def back_kernel(heard, *refs):
-    weights, (back_own, back_sib, target) = refs[:-3], refs[-3:]
+def pick(values, at):
+    here = lax.broadcasted_iota(I32, (8, ROWS), 0) == at
+    return jnp.sum(jnp.where(here, values, 0.0), axis=0, keepdims=True)
+
+
+def back_rows(acc, weight, stat, first):
+    for n in range(weight.shape[0]):
+        prod = weight[n] * pick(stat, position(first + n))
+        acc = acc + (prod[:, :128] + prod[:, 128:])
+    return acc
+
+
+def back_kernel(heard, weight, acc, stat_out, target):
     sums = heard[0]
     for d in range(1, 8):
         sums = sums + heard[d]
     stat = sums[8:16] / sums[0:8]
-    row_of = lax.broadcasted_iota(I32, (8, ROWS), 0)
-
-    def pick(values, at):
-        return jnp.sum(jnp.where(row_of == at, values, 0.0), axis=0, keepdims=True)
-
+    stat_out[...] = stat
     own_stat = pick(stat, position(0))
     mean = pick(sums[16:24], position(0)) / pick(sums[0:8], position(0))
-    margin = own_stat - 0.5 * (own_stat + mean)
-    target[...] = margin
-    acc = jnp.zeros((2 * ROWS, 128), F32)
-    place = 0
-    for weight in weights:
-        for n in range(weight.shape[0]):
-            prod = weight[n] * pick(stat, position(place))
-            acc = acc + (prod[:, :128] + prod[:, 128:])
-            place += 1
-    total = jnp.broadcast_to(jnp.sum(acc, axis=1, keepdims=True), (2 * ROWS, 128))
+    target[...] = own_stat - 0.5 * (own_stat + mean)
+    acc[...] = back_rows(jnp.zeros((2 * ROWS, 128), F32), weight, stat, 0)
+
+
+def back_last_kernel(acc, stat, weight, back_own, back_sib):
+    total = back_rows(acc[...], weight, stat[...], 8 - weight.shape[0])
+    total = jnp.broadcast_to(jnp.sum(total, axis=1, keepdims=True), (2 * ROWS, 128))
     back_own[...] = total[:ROWS]
     back_sib[...] = total[ROWS:]
 
 
-def back(heard, weights):
-    return pl.pallas_call(
+def back(heard, early, late):
+    acc, stat, target = pl.pallas_call(
         back_kernel,
         out_shape=(
-            jax.ShapeDtypeStruct((ROWS, 128), F32),
-            jax.ShapeDtypeStruct((ROWS, 128), F32),
+            jax.ShapeDtypeStruct((2 * ROWS, 128), F32),
+            jax.ShapeDtypeStruct((8, ROWS), F32),
             jax.ShapeDtypeStruct((1, ROWS), F32),
         ),
-        in_specs=[vm()] * (1 + len(weights)),
+        in_specs=[vm()] * 2,
         out_specs=(vm(),) * 3,
         compiler_params=params(),
-        cost_estimate=pl.CostEstimate(flops=2**22, bytes_accessed=5 * 2**20, transcendentals=0),
-    )(heard, *weights)
+        cost_estimate=pl.CostEstimate(flops=2**21, bytes_accessed=3 * 2**20, transcendentals=0),
+    )(heard, early)
+    back_own, back_sib = pl.pallas_call(
+        back_last_kernel,
+        out_shape=(jax.ShapeDtypeStruct((ROWS, 128), F32),) * 2,
+        in_specs=[vm()] * 3,
+        out_specs=(vm(),) * 2,
+        compiler_params=params(),
+        cost_estimate=pl.CostEstimate(flops=2**21, bytes_accessed=2**21, transcendentals=0),
+    )(acc, stat, late)
+    return back_own, back_sib, target
 
 
 def home_kernel(mine, other, partner, partner_in, *refs):
@@ -420,7 +433,7 @@
     partner_out, token = unpack(place, got)
 
     heard = lax.all_to_all(fore(fwd, fwd_in, by_y[0], parts), PLANE, 0, 0, tiled=True)
-    back_own, back_sib, tgt_margin = back(heard, [part[0] for part in parts])
+    back_own, back_sib, tgt_margin = back(heard, parts[0][0], parts[1][0])
     back_in = lax.ppermute(back_sib, "c", SWAP)
     both = route(margins(fwd, fwd_in, back_own, back_in, tgt_margin))
     src_margin, tgt_margin = finish(src_labels, tgt_labels, both, token)

time: 115 us -> 115 us (level)
  no operation moved by 1% of the time
where the time goes in v6:
time: 115 us; the launch traced here: 114 us
  starting transfers between devices  36.7 us (32%)
  waiting for transfers between devices  30.3 us (26%)
  blocking collectives  25 us (22%)
  Pallas kernels  17.6 us (15%)
  local copies, waits for them, and re-layouts  3.71 us (3%)
    all_to_all x1, blocking collectives, route(): return lax.all_to_all(packed, ROUTE, 0, 0, tiled=True)  25 us
    all_to_all x2, starting transfers between devices, route(): return lax.all_to_all(packed, ROUTE, 0, 0, tiled=True)  9.57 us
    ppermute x1, waiting for transfers between devices, on_device(): lax.ppermute(base, 'x', RIGHT)  8.47 us
    ppermute x1, waiting for transfers between devices, on_device(): lax.ppermute(across, 'x', RIGHT)  6.22 us
    ppermute x3, starting transfers between devices, on_device(): lax.ppermute(by_y[d], 'y', shift(d))  6.21 us
    pallas_call x2, Pallas kernels, score(): pl.pallas_call(partial(score_kernel, pieces, len(arrays), bool(carry), la...  6.17 us
    ppermute x3, starting transfers between devices, on_device(): lax.ppermute(rows, ('zh', 'zl'), [(i, i ^ z) for i in range(4)])  4.7 us
    ppermute x1, waiting for transfers between devices, on_device(): lax.ppermute(go_right, 'x', RIGHT)  4.35 us
  transfers between devices with their start and end apart: 21, of which 11 were waited for; matrix products, arithmetic and copies ran while one was open for 0% of the time, Pallas kernels for 10%

profile of v6, /device:TPU:0, one launch (start us, length us, event | category | flops | bytes accessed | tf_op | source)
XLA Modules:
  0.0 114.3 jit_solution(16544454675729884205)
XLA Ops:
  3.0 25.0 %all_to_all.20.arrived = bf16[16,32,1024]{2,1,0:T(8,128)(2,1)S(1)} all-to-all(bf16[16,32,1024]{2,1,0:T(8,128)(2,1)S(1)} %bitcast.6), channel_id=1, replica_groups=mesh['zh'=2,'y'=4,'zl'=2,'x'=4,'c'=2] {'zh','y','zl'}, dimensions={0} | all-to-all | bytes 2097152 | tf_op jit(solution)/shard_map/all_to_all | solution.py:386
  29.7 3.7 %all-to-all-start.1 = ((bf16[16,32,1024]{2,1,0:T(8,128)(2,1)}), bf16[16,32,1024]{2,1,0:T(8,128)(2,1)S(1)}, u32[]{:S(2)}, u32[]{:S(2)}) async-start(bf16[16,32,1024]{2,1,0:T(8,128)(2,1)} %bitcast.3), calls=%async_computation.1 | async-start | bytes 2097152 | tf_op jit(solution)/shard_map/all_to_all | solution.py:386
  35.0 1.7 %collective-permute-start.1 = (bf16[256,1024]{1,0:T(8,128)(2,1)S(1)}, bf16[256,1024]{1,0:T(8,128)(2,1)S(1)}, u32[]{:S(2)}, u32[]{:S(2)}) collective-permute-start(bf16[256,1024]{1,0:T(8,128)(2,1)S(1)} %shard_map.69.refs_0_), channel_id=1, source_target_pairs={{0,6},{2,0},{4,2},{6,4},{1,7},{3,1},{5,3},{7,5},{8,14},{10,8},{12,... | collective-permute-start | bytes 1572872 | tf_op jit(solution)/shard_map/ppermute | solution.py:398
  36.7 1.7 %collective-permute-start.6 = (bf16[256,1024]{1,0:T(8,128)(2,1)S(1)}, bf16[256,1024]{1,0:T(8,128)(2,1)}, u32[]{:S(2)}, u32[]{:S(2)}) collective-permute-start(bf16[256,1024]{1,0:T(8,128)(2,1)S(1)} %shard_map.69.refs_0_), channel_id=1, source_target_pairs={{0,8},{8,0},{1,9},{9,1},{2,10},{10,2},{3,11},{11,3},{4,12},{12,4},... | collective-permute-start | bytes 1572872 | tf_op jit(solution)/shard_map/ppermute | solution.py:399
  38.4 8.5 %collective-permute-done.refs_0_.refs_1_ = bf16[256,1024]{1,0:T(8,128)(2,1)S(1)} collective-permute-done((bf16[256,1024]{1,0:T(8,128)(2,1)S(1)}, bf16[256,1024]{1,0:T(8,128)(2,1)S(1)}, u32[]{:S(2)}, u32[]{:S(2)}) %collective-permute-start) | collective-permute-done | bytes 524320 | tf_op jit(solution)/shard_map/ppermute | solution.py:398
  48.5 2.5 %collective-permute-start.3 = (bf16[128,1024]{1,0:T(8,128)(2,1)S(1)}, bf16[128,1024]{1,0:T(8,128)(2,1)S(1)}, u32[]{:S(2)}, u32[]{:S(2)}) collective-permute-start(bf16[128,1024]{1,0:T(8,128)(2,1)S(1)} %get-tuple-element.34), channel_id=1, source_target_pairs={{0,6},{2,0},{4,2},{6,4},{1,7},{3,1},{5,3},{7,5},{8,14},{10,8},{12,... | collective-permute-start | bytes 786440 | tf_op jit(solution)/shard_map/ppermute | solution.py:401
  51.0 4.3 %collective-permute-done.2.refs_0_ = bf16[128,1024]{1,0:T(8,128)(2,1)S(1)} collective-permute-done((bf16[128,1024]{1,0:T(8,128)(2,1)S(1)}, bf16[128,1024]{1,0:T(8,128)(2,1)S(1)}, u32[]{:S(2)}, u32[]{:S(2)}) %collective-permute-start.2) | collective-permute-done | bytes 262176 | tf_op jit(solution)/shard_map/ppermute | solution.py:401
  55.5 1.9 %collective-permute-done.6.refs_3_ = bf16[256,1024]{1,0:T(8,128)(2,1)} collective-permute-done((bf16[256,1024]{1,0:T(8,128)(2,1)S(1)}, bf16[256,1024]{1,0:T(8,128)(2,1)}, u32[]{:S(2)}, u32[]{:S(2)}) %collective-permute-start.6) | collective-permute-done | bytes 524320 | tf_op jit(solution)/shard_map/ppermute | solution.py:399
  58.6 2.0 %collective-permute-start.8 = (bf16[256,1024]{1,0:T(8,128)(2,1)}, bf16[256,1024]{1,0:T(8,128)(2,1)S(1)}, u32[]{:S(2)}, u32[]{:S(2)}) collective-permute-start(bf16[256,1024]{1,0:T(8,128)(2,1)} %collective-permute-done.6.refs_3_), channel_id=1, source_target_pairs={{0,6},{2,0},{4,2},{6,4},{1,7},{3,1},{5,3},{7,5},{8,14},{10,8},{12,... | collective-permute-start | bytes 1572872 | tf_op jit(solution)/shard_map/ppermute | solution.py:402
  61.1 4.2 %shard_map.74 = (f32[5,512,256]{2,1,0:T(8,128)S(1)}, f32[5,256]{1,0:T(8,128)S(1)}, f32[5,256]{1,0:T(8,128)S(1)}, f32[256,1024]{1,0:T(8,128)S(1)}, f32[256,1024]{...) custom-call(bf16[256,1024]{1,0:T(8,128)(2,1)S(1)} %shard_map.72.own, ...), custom_call_target="tpu_custom_call" | custom-call | flops 2684354560 | bytes 9437184 | tf_op jit(solution)/shard_map/pallas_call | solution.py:155
  65.3 6.2 %collective-permute-done.7.refs_1_ = bf16[256,1024]{1,0:T(8,128)(2,1)S(1)} collective-permute-done((bf16[256,1024]{1,0:T(8,128)(2,1)}, bf16[256,1024]{1,0:T(8,128)(2,1)S(1)}, u32[]{:S(2)}, u32[]{:S(2)}) %collective-permute-start.7) | collective-permute-done | bytes 524320 | tf_op jit(solution)/shard_map/ppermute | solution.py:402
  72.9 2.0 %shard_map.75 = (f32[3,512,256]{2,1,0:T(8,128)S(1)}, f32[3,256]{1,0:T(4,128)S(1)}, f32[3,256]{1,0:T(4,128)S(1)}, f32[256,1024]{1,0:T(8,128)S(1)}, bf16[256,1024]{1,0:T(8,128)(2,1)S(1)}, /*index=5*/f32[512,128]{1,0:T(8,128)S(1)}) custom-call(bf16[256,1024]{1,0:T(8,128)(2,1)S(1)} %shard_map.72.own, bf16[256,1024]{1,0:T(8,128)(2,1)S(1)} %collective-permute-done.4.sib, ...), custom_call_target="tpu_custom_call" | custom-call | flops 1610612736 | bytes 7340032 | tf_op jit(solution)/shard_map/pallas_call | solution.py:155
  75.5 1.8 %collective-permute-done.9.other = f32[512,128]{1,0:T(8,128)S(1)} collective-permute-done((f32[512,128]{1,0:T(8,128)S(1)}, f32[512,128]{1,0:T(8,128)S(1)}, u32[]{:S(2)}, u32[]{:S(2)}) %collective-permute-start.9) | collective-permute-done | bytes 262176 | tf_op jit(solution)/shard_map/ppermute | solution.py:424
  78.2 2.5 %collective-permute-start.11 = (bf16[64,1024]{1,0:T(8,128)(2,1)}, bf16[64,1024]{1,0:T(8,128)(2,1)}, u32[]{:S(2)}, u32[]{:S(2)}) collective-permute-start(bf16[64,1024]{1,0:T(8,128)(2,1)} %get-tuple-element.43), channel_id=1, source_target_pairs={{0,16},{16,32},{32,48},{48,0},{1,17},{17,33},{33,49},{49,1},{2,18}... | collective-permute-start | bytes 393224 | tf_op jit(solution)/shard_map/ppermute | solution.py:428
  80.7 1.7 %collective-permute-start.12 = (bf16[64,1024]{1,0:T(8,128)(2,1)}, bf16[64,1024]{1,0:T(8,128)(2,1)}, u32[]{:S(2)}, u32[]{:S(2)}) collective-permute-start(bf16[64,1024]{1,0:T(8,128)(2,1)} %get-tuple-element.44), channel_id=1, source_target_pairs={{0,32},{16,48},{32,0},{48,16},{1,33},{17,49},{33,1},{49,17},{2,34}... | collective-permute-start | bytes 393224 | tf_op jit(solution)/shard_map/ppermute | solution.py:428
  82.4 2.0 %collective-permute-start.13 = (bf16[64,1024]{1,0:T(8,128)(2,1)}, bf16[64,1024]{1,0:T(8,128)(2,1)}, u32[]{:S(2)}, u32[]{:S(2)}) collective-permute-start(bf16[64,1024]{1,0:T(8,128)(2,1)} %get-tuple-element.45), channel_id=1, source_target_pairs={{0,48},{16,0},{32,16},{48,32},{1,49},{17,1},{33,17},{49,33},{2,50}... | collective-permute-start | bytes 393224 | tf_op jit(solution)/shard_map/ppermute | solution.py:428
  85.5 3.6 %all-to-all-start.2 = ((f32[8,24,256]{2,1,0:T(8,128)}), f32[8,24,256]{2,1,0:T(8,128)S(1)}, u32[]{:S(2)}, u32[]{:S(2)}) async-start(f32[8,24,256]{2,1,0:T(8,128)} %shard_map.79), calls=%async_computation.2 | async-start | bytes 393216 | tf_op jit(solution)/shard_map/all_to_all | solution.py:435
  89.1 1.8 %shard_map.77 = (bf16[128,1024]{1,0:T(8,128)(2,1)}, bf16[128,1024]{1,0:T(8,128)(2,1)}) custom-call(bf16[64,1024]{1,0:T(8,128)(2,1)S(1)} %get-tuple-element.42.r0.after, bf16[64,1024]{1,0:T(8,128)(2,1)} %collective-permute-done.11.r1, bf16[64,1024]{1,0:T(8,128)(2,1)} %collective-permute-done.12.r2, bf16[64,1024]{1,0:T(8,128)(2,1)} %collective-permute-done.13.r3), custom_call_target="tpu_custom_call" | custom-call | bytes 1048576 | tf_op jit(solution)/shard_map/pallas_call | solution.py:289
  91.0 1.8 %collective-permute-start.14 = (bf16[128,1024]{1,0:T(8,128)(2,1)}, bf16[128,1024]{1,0:T(8,128)(2,1)}, u32[]{:S(2)}, u32[]{:S(2)}) collective-permute-start(bf16[128,1024]{1,0:T(8,128)(2,1)} %get-tuple-element.46.g0), channel_id=1, source_target_pairs={{0,8},{8,0},{64,72},{72,64},{1,9},{9,1},{65,73},{73,65},{2,10},{10... | collective-permute-start | bytes 786440 | tf_op jit(solution)/shard_map/ppermute | solution.py:431
  92.7 2.7 %collective-permute-start.15 = (bf16[128,1024]{1,0:T(8,128)(2,1)}, bf16[128,1024]{1,0:T(8,128)(2,1)}, u32[]{:S(2)}, u32[]{:S(2)}) collective-permute-start(bf16[128,1024]{1,0:T(8,128)(2,1)} %get-tuple-element.47), channel_id=1, source_target_pairs={{0,64},{8,72},{64,0},{72,8},{1,65},{9,73},{65,1},{73,9},{2,66},{10... | collective-permute-start | bytes 786440 | tf_op jit(solution)/shard_map/ppermute | solution.py:431
  99.8 5.9 %all-to-all-start.3 = ((f32[16,2,256]{2,1,0:T(2,128)}), f32[16,2,256]{2,1,0:T(2,128)S(1)}, u32[]{:S(2)}, u32[]{:S(2)}) async-start(f32[16,2,256]{2,1,0:T(2,128)} %shard_map.82), calls=%async_computation.3 | async-start | bytes 65536 | tf_op jit(solution)/shard_map/all_to_all | solution.py:386
  106.0 1.6 %collective-permute-done.15.g2 = bf16[128,1024]{1,0:T(8,128)(2,1)} collective-permute-done((bf16[128,1024]{1,0:T(8,128)(2,1)}, bf16[128,1024]{1,0:T(8,128)(2,1)}, u32[]{:S(2)}, u32[]{:S(2)}) %collective-permute-start.15) | collective-permute-done | bytes 262176 | tf_op jit(solution)/shard_map/ppermute | solution.py:431
  107.6 1.7 %collective-permute-done.16.g3 = bf16[128,1024]{1,0:T(8,128)(2,1)} collective-permute-done((bf16[128,1024]{1,0:T(8,128)(2,1)}, bf16[128,1024]{1,0:T(8,128)(2,1)}, u32[]{:S(2)}, u32[]{:S(2)}) %collective-permute-start.16) | collective-permute-done | bytes 262176 | tf_op jit(solution)/shard_map/ppermute | solution.py:431
  109.3 2.6 %shard_map.78 = (f32[256,1024]{1,0:T(8,128)}, f32[8,128]{1,0:T(8,128)S(1)}) custom-call(bf16[256,512]{1,0:T(8,128)(2,1)S(1)} %shard_map.67.place, bf16[128,1024]{1,0:T(8,128)(2,1)} %get-tuple-element.46.g0, bf16[128,1024]{1,0:T(8,128)(2,1)} %collective-permute-done.14.g1, bf16[128,1024]{1,0:T(8,128)(2,1)} %collective-permute-done.15.g2, ...), custom_call_target="tpu_custom_call" | custom-call | flops 268435456 | bytes 2097152 | tf_op jit(solution)/shard_map/pallas_call | solution.py:348
  (58 shorter events, 19.9 us)
Async XLA Ops:
  2.4 25.8 %copy-start.7 = (bf16[256,1024]{1,0:T(8,128)(2,1)S(1)}, bf16[256,1024]{1,0:T(8,128)(2,1)}, u32[]{:S(2)}) copy-start(bf16[256,1024]{1,0:T(8,128)(2,1)} %rows.3) | copy-start | bytes 1572868
  2.4 25.8 %copy-start.8 = (s32[256]{0:T(256)S(1)}, s32[256]{0:T(256)}, u32[]{:S(2)}) copy-start(s32[256]{0:T(256)} %param.5) | copy-start | bytes 3076
  29.7 25.6 %all-to-all-start.1 = ((bf16[16,32,1024]{2,1,0:T(8,128)(2,1)}), bf16[16,32,1024]{2,1,0:T(8,128)(2,1)S(1)}, u32[]{:S(2)}, u32[]{:S(2)}) async-start(bf16[16,32,1024]{2,1,0:T(8,128)(2,1)} %bitcast.3), calls=%async_computation.1 | async-start | bytes 2097152 | tf_op jit(solution)/shard_map/all_to_all | solution.py:386
  33.4 13.5 %collective-permute-start = (bf16[256,1024]{1,0:T(8,128)(2,1)S(1)}, bf16[256,1024]{1,0:T(8,128)(2,1)S(1)}, u32[]{:S(2)}, u32[]{:S(2)}) collective-permute-start(bf16[256,1024]{1,0:T(8,128)(2,1)S(1)} %shard_map.69.refs_0_), channel_id=1, source_target_pairs={{0,2},{2,4},{4,6},{6,0},{1,3},{3,5},{5,7},{7,1},{8,10},{10,12},{12... | collective-permute-start | bytes 1572872 | tf_op jit(solution)/shard_map/ppermute | solution.py:398
  35.0 12.0 %collective-permute-start.1 = (bf16[256,1024]{1,0:T(8,128)(2,1)S(1)}, bf16[256,1024]{1,0:T(8,128)(2,1)S(1)}, u32[]{:S(2)}, u32[]{:S(2)}) collective-permute-start(bf16[256,1024]{1,0:T(8,128)(2,1)S(1)} %shard_map.69.refs_0_), channel_id=1, source_target_pairs={{0,6},{2,0},{4,2},{6,4},{1,7},{3,1},{5,3},{7,5},{8,14},{10,8},{12,... | collective-permute-start | bytes 1572872 | tf_op jit(solution)/shard_map/ppermute | solution.py:398
  36.7 20.7 %collective-permute-start.6 = (bf16[256,1024]{1,0:T(8,128)(2,1)S(1)}, bf16[256,1024]{1,0:T(8,128)(2,1)}, u32[]{:S(2)}, u32[]{:S(2)}) collective-permute-start(bf16[256,1024]{1,0:T(8,128)(2,1)S(1)} %shard_map.69.refs_0_), channel_id=1, source_target_pairs={{0,8},{8,0},{1,9},{9,1},{2,10},{10,2},{3,11},{11,3},{4,12},{12,4},... | collective-permute-start | bytes 1572872 | tf_op jit(solution)/shard_map/ppermute | solution.py:399
  47.7 7.6 %collective-permute-start.2 = (bf16[128,1024]{1,0:T(8,128)(2,1)S(1)}, bf16[128,1024]{1,0:T(8,128)(2,1)S(1)}, u32[]{:S(2)}, u32[]{:S(2)}) collective-permute-start(bf16[128,1024]{1,0:T(8,128)(2,1)S(1)} %get-tuple-element.33), channel_id=1, source_target_pairs={{0,2},{2,4},{4,6},{6,0},{1,3},{3,5},{5,7},{7,1},{8,10},{10,12},{12... | collective-permute-start | bytes 786440 | tf_op jit(solution)/shard_map/ppermute | solution.py:401
  48.5 6.8 %collective-permute-start.3 = (bf16[128,1024]{1,0:T(8,128)(2,1)S(1)}, bf16[128,1024]{1,0:T(8,128)(2,1)S(1)}, u32[]{:S(2)}, u32[]{:S(2)}) collective-permute-start(bf16[128,1024]{1,0:T(8,128)(2,1)S(1)} %get-tuple-element.34), channel_id=1, source_target_pairs={{0,6},{2,0},{4,2},{6,4},{1,7},{3,1},{5,3},{7,5},{8,14},{10,8},{12,... | collective-permute-start | bytes 786440 | tf_op jit(solution)/shard_map/ppermute | solution.py:401
  55.4 5.7 %collective-permute-start.4 = (bf16[256,1024]{1,0:T(8,128)(2,1)S(1)}, bf16[256,1024]{1,0:T(8,128)(2,1)S(1)}, u32[]{:S(2)}, u32[]{:S(2)}) collective-permute-start(bf16[256,1024]{1,0:T(8,128)(2,1)S(1)} %shard_map.72.own), channel_id=1, source_target_pairs={{0,1},{1,0},{2,3},{3,2},{4,5},{5,4},{6,7},{7,6},{8,9},{9,8},{10,11... | collective-permute-start | bytes 1572872 | tf_op jit(solution)/shard_map/ppermute | solution.py:407
  57.4 14.1 %collective-permute-start.7 = (bf16[256,1024]{1,0:T(8,128)(2,1)}, bf16[256,1024]{1,0:T(8,128)(2,1)S(1)}, u32[]{:S(2)}, u32[]{:S(2)}) collective-permute-start(bf16[256,1024]{1,0:T(8,128)(2,1)} %collective-permute-done.6.refs_3_), channel_id=1, source_target_pairs={{0,2},{2,4},{4,6},{6,0},{1,3},{3,5},{5,7},{7,1},{8,10},{10,12},{12... | collective-permute-start | bytes 1572872 | tf_op jit(solution)/shard_map/ppermute | solution.py:402
  58.6 12.9 %collective-permute-start.8 = (bf16[256,1024]{1,0:T(8,128)(2,1)}, bf16[256,1024]{1,0:T(8,128)(2,1)S(1)}, u32[]{:S(2)}, u32[]{:S(2)}) collective-permute-start(bf16[256,1024]{1,0:T(8,128)(2,1)} %collective-permute-done.6.refs_3_), channel_id=1, source_target_pairs={{0,6},{2,0},{4,2},{6,4},{1,7},{3,1},{5,3},{7,5},{8,14},{10,8},{12,... | collective-permute-start | bytes 1572872 | tf_op jit(solution)/shard_map/ppermute | solution.py:402
  60.7 12.2 %collective-permute-start.5 = (bf16[256,1024]{1,0:T(8,128)(2,1)S(1)}, bf16[256,1024]{1,0:T(8,128)(2,1)S(1)}, u32[]{:S(2)}, u32[]{:S(2)}) collective-permute-start(bf16[256,1024]{1,0:T(8,128)(2,1)S(1)} %shard_map.73.refs_4_), channel_id=1, source_target_pairs={{0,8},{8,0},{1,9},{9,1},{2,10},{10,2},{3,11},{11,3},{4,12},{12,4},... | collective-permute-start | bytes 1572872 | tf_op jit(solution)/shard_map/ppermute | solution.py:404
  74.9 2.4 %collective-permute-start.10 = (bf16[256,1024]{1,0:T(8,128)(2,1)S(1)}, bf16[256,1024]{1,0:T(8,128)(2,1)S(1)}, u32[]{:S(2)}, u32[]{:S(2)}) collective-permute-start(bf16[256,1024]{1,0:T(8,128)(2,1)S(1)} %get-tuple-element.41), channel_id=1, source_target_pairs={{0,1},{1,0},{2,3},{3,2},{4,5},{5,4},{6,7},{7,6},{8,9},{9,8},{10,11... | collective-permute-start | bytes 1572872 | tf_op jit(solution)/shard_map/ppermute | solution.py:425
  75.0 2.3 %collective-permute-start.9 = (f32[512,128]{1,0:T(8,128)S(1)}, f32[512,128]{1,0:T(8,128)S(1)}, u32[]{:S(2)}, u32[]{:S(2)}) collective-permute-start(f32[512,128]{1,0:T(8,128)S(1)} %get-tuple-element.39.mine), channel_id=1, source_target_pairs={{0,1},{1,0},{2,3},{3,2},{4,5},{5,4},{6,7},{7,6},{8,9},{9,8},{10,11... | collective-permute-start | bytes 786440 | tf_op jit(solution)/shard_map/ppermute | solution.py:424
  78.2 10.9 %collective-permute-start.11 = (bf16[64,1024]{1,0:T(8,128)(2,1)}, bf16[64,1024]{1,0:T(8,128)(2,1)}, u32[]{:S(2)}, u32[]{:S(2)}) collective-permute-start(bf16[64,1024]{1,0:T(8,128)(2,1)} %get-tuple-element.43), channel_id=1, source_target_pairs={{0,16},{16,32},{32,48},{48,0},{1,17},{17,33},{33,49},{49,1},{2,18}... | collective-permute-start | bytes 393224 | tf_op jit(solution)/shard_map/ppermute | solution.py:428
  80.7 8.4 %collective-permute-start.12 = (bf16[64,1024]{1,0:T(8,128)(2,1)}, bf16[64,1024]{1,0:T(8,128)(2,1)}, u32[]{:S(2)}, u32[]{:S(2)}) collective-permute-start(bf16[64,1024]{1,0:T(8,128)(2,1)} %get-tuple-element.44), channel_id=1, source_target_pairs={{0,32},{16,48},{32,0},{48,16},{1,33},{17,49},{33,1},{49,17},{2,34}... | collective-permute-start | bytes 393224 | tf_op jit(solution)/shard_map/ppermute | solution.py:428
  82.4 6.7 %collective-permute-start.13 = (bf16[64,1024]{1,0:T(8,128)(2,1)}, bf16[64,1024]{1,0:T(8,128)(2,1)}, u32[]{:S(2)}, u32[]{:S(2)}) collective-permute-start(bf16[64,1024]{1,0:T(8,128)(2,1)} %get-tuple-element.45), channel_id=1, source_target_pairs={{0,48},{16,0},{32,16},{48,32},{1,49},{17,1},{33,17},{49,33},{2,50}... | collective-permute-start | bytes 393224 | tf_op jit(solution)/shard_map/ppermute | solution.py:428
  85.5 10.3 %all-to-all-start.2 = ((f32[8,24,256]{2,1,0:T(8,128)}), f32[8,24,256]{2,1,0:T(8,128)S(1)}, u32[]{:S(2)}, u32[]{:S(2)}) async-start(f32[8,24,256]{2,1,0:T(8,128)} %shard_map.79), calls=%async_computation.2 | async-start | bytes 393216 | tf_op jit(solution)/shard_map/all_to_all | solution.py:435
  91.0 15.0 %collective-permute-start.14 = (bf16[128,1024]{1,0:T(8,128)(2,1)}, bf16[128,1024]{1,0:T(8,128)(2,1)}, u32[]{:S(2)}, u32[]{:S(2)}) collective-permute-start(bf16[128,1024]{1,0:T(8,128)(2,1)} %get-tuple-element.46.g0), channel_id=1, source_target_pairs={{0,8},{8,0},{64,72},{72,64},{1,9},{9,1},{65,73},{73,65},{2,10},{10... | collective-permute-start | bytes 786440 | tf_op jit(solution)/shard_map/ppermute | solution.py:431
  92.7 14.9 %collective-permute-start.15 = (bf16[128,1024]{1,0:T(8,128)(2,1)}, bf16[128,1024]{1,0:T(8,128)(2,1)}, u32[]{:S(2)}, u32[]{:S(2)}) collective-permute-start(bf16[128,1024]{1,0:T(8,128)(2,1)} %get-tuple-element.47), channel_id=1, source_target_pairs={{0,64},{8,72},{64,0},{72,8},{1,65},{9,73},{65,1},{73,9},{2,66},{10... | collective-permute-start | bytes 786440 | tf_op jit(solution)/shard_map/ppermute | solution.py:431
  95.5 13.8 %collective-permute-start.16 = (bf16[128,1024]{1,0:T(8,128)(2,1)}, bf16[128,1024]{1,0:T(8,128)(2,1)}, u32[]{:S(2)}, u32[]{:S(2)}) collective-permute-start(bf16[128,1024]{1,0:T(8,128)(2,1)} %get-tuple-element.47), channel_id=1, source_target_pairs={{0,72},{8,64},{64,8},{72,0},{1,73},{9,65},{65,9},{73,1},{2,74},{10... | collective-permute-start | bytes 786440 | tf_op jit(solution)/shard_map/ppermute | solution.py:431
  96.1 17.2 %copy-start.10 = (s32[256]{0:T(256)S(1)}, s32[256]{0:T(256)}, u32[]{:S(2)}) copy-start(s32[256]{0:T(256)} %param.7) | copy-start | bytes 3076
  97.5 1.4 %collective-permute-start.17 = (f32[256,128]{1,0:T(8,128)S(1)}, f32[256,128]{1,0:T(8,128)S(1)}, u32[]{:S(2)}, u32[]{:S(2)}) collective-permute-start(f32[256,128]{1,0:T(8,128)S(1)} %get-tuple-element.58), channel_id=1, source_target_pairs={{0,1},{1,0},{2,3},{3,2},{4,5},{5,4},{6,7},{7,6},{8,9},{9,8},{10,11... | collective-permute-start | bytes 393224 | tf_op jit(solution)/shard_map/ppermute | solution.py:437
  99.8 13.5 %all-to-all-start.3 = ((f32[16,2,256]{2,1,0:T(2,128)}), f32[16,2,256]{2,1,0:T(2,128)S(1)}, u32[]{:S(2)}, u32[]{:S(2)}) async-start(f32[16,2,256]{2,1,0:T(2,128)} %shard_map.82), calls=%async_computation.3 | async-start | bytes 65536 | tf_op jit(solution)/shard_map/all_to_all | solution.py:386
  (8 other events, 33.4 us)
